TPU v7x, 512 devices: a whole 4x4x16 slice. The times are simulated.
512 devices in a mesh: dp: 8 (over y, core), expert: 64 (over x, z).
Axes of the slice: x: 4, y: 4, z: 16, core: 2. Of those that a mesh axis runs over, the one named last changes fastest.
Arguments:
- master: float32 [64, 1024, 1152], P('expert', 'dp'), may hold values from -1 to 1
- moment_one: float32 [64, 1024, 1152], P('expert', 'dp'), may hold values from -6 to 6
- moment_two: float32 [64, 1024, 1152], P('expert', 'dp'), may hold values from 0.25 to 4
- gradients: bfloat16 [64, 1024, 1152], P('expert', 'dp'), may hold values from -40 to 40
- old_host: int32 [64], replicated, may hold values from 0 to 63, as said below
- new_host: int32 [64], replicated, may hold values from 0 to 63, as said below
- tokens: bfloat16 [65536, 1024], P(('dp', 'expert')), may hold values from -6 to 6
- routes: int32 [65536, 8], P(('dp', 'expert')), may hold values from 0 to 63, all different within a row; in each aligned block of 128 rows (0 to 127, 128 to 255, ...) at most 24 rows name the same one
- route_weights: float32 [65536, 8], P(('dp', 'expert')), may hold values from 0.02 to 0.5
Outputs:
- new_master: float32 [64, 1024, 1152], P('expert', 'dp')
- new_moment_one: float32 [64, 1024, 1152], P('expert', 'dp')
- new_moment_two: float32 [64, 1024, 1152], P('expert', 'dp')
- mixed: bfloat16 [65536, 1024], P(('dp', 'expert'))
Inputs may be any that keep to these rules, and one draw needn't show every extreme that they name: old_host places the 64 experts on distinct hosts. new_host places the 64 experts on distinct hosts; exactly 16 experts have a new_host different from their old_host. `routes`: each token names 8 different experts; among the 128 tokens of one device no expert is named by more than 24 tokens, and in every draw some device has an expert named by exactly 24 of its tokens.
All inputs are finite; a program needn't handle non-finite values.
Results may differ from a plain program's by a relative error of at most 0.0076.
Values may be sent and summed in bfloat16 or wider, within the bound.
No kernel may reach another device: no remote copies, remote signals or barrier semaphores. Data moves between devices by JAX's collectives and lax.ppermute only.
A program may use at most 64 MiB of HBM per device.

v0:
```python
import jax
import jax.numpy as jnp
from jax import lax
from jax.sharding import PartitionSpec as P

beta_one = 0.9
beta_two = 0.95
epsilon = 1e-08
learn_rate = 0.001
decay_rate = 0.1
step_count = 10


def adamw(master, moment_one, moment_two, gradients, factor):
    scaled = gradients.astype(jnp.float32) * factor
    new_one = beta_one * moment_one + (1.0 - beta_one) * scaled
    new_two = beta_two * moment_two + (1.0 - beta_two) * scaled * scaled
    corrected_one = new_one / (1.0 - beta_one**step_count)
    corrected_two = new_two / (1.0 - beta_two**step_count)
    step_size = corrected_one / (jnp.sqrt(corrected_two) + epsilon) + decay_rate * master
    return (master - learn_rate * step_size, new_one, new_two)


def clip_factor(gradients, element_count):
    local_sum = jnp.sum(jnp.square(gradients.astype(jnp.float32)))
    square_sum = lax.psum(local_sum, ("dp", "expert"))
    clip_limit = jnp.sqrt(jnp.float32(element_count))
    return jnp.minimum(1.0, clip_limit / (jnp.sqrt(square_sum) + 1e-06))


def relocate_state(master, moment_one, moment_two, source):
    host_count = lax.axis_size("expert")
    shape = master.shape
    spread = (
        lax.all_to_all(
            master.reshape(host_count, -1), "expert", split_axis=0, concat_axis=0, tiled=True
        ),
        lax.all_to_all(
            moment_one.reshape(host_count, -1), "expert", split_axis=0, concat_axis=0, tiled=True
        ),
        lax.all_to_all(
            moment_two.reshape(host_count, -1), "expert", split_axis=0, concat_axis=0, tiled=True
        ),
    )
    ordered = tuple((jnp.take(item, source, axis=0) for item in spread))
    arrived = (
        lax.all_to_all(ordered[0], "expert", split_axis=0, concat_axis=0, tiled=True),
        lax.all_to_all(ordered[1], "expert", split_axis=0, concat_axis=0, tiled=True),
        lax.all_to_all(ordered[2], "expert", split_axis=0, concat_axis=0, tiled=True),
    )
    return tuple((item.reshape(shape) for item in arrived))


def per_device(
    master, moment_one, moment_two, gradients, old_host, new_host, tokens, routes, route_weights
):
    host_count = lax.axis_size("expert")
    expert_ids = jnp.arange(host_count, dtype=jnp.int32)
    owner = jnp.zeros((host_count,), jnp.int32).at[new_host].set(expert_ids)
    source = old_host[owner]
    element_count = host_count * lax.axis_size("dp") * gradients.shape[1] * gradients.shape[2]
    factor = clip_factor(gradients, element_count)
    updated = adamw(master, moment_one, moment_two, gradients, factor)
    new_master, new_one, new_two = relocate_state(updated[0], updated[1], updated[2], source)
    moved_rounded = new_master.astype(jnp.bfloat16)
    full_weights = lax.all_gather(moved_rounded, "dp", axis=1, tiled=True)[0]
    hidden_units = full_weights.shape[1] // 3
    width = tokens.shape[1]
    tok_count = tokens.shape[0]
    top = routes.shape[1]
    assignments = tok_count * top
    capacity = 3 * tok_count * top // (2 * host_count)
    flat_routes = routes.reshape(-1)
    target = jnp.sum(
        jnp.where(flat_routes[:, None] == expert_ids[None, :], new_host[None, :], 0), axis=1
    )
    onehot = (target[:, None] == expert_ids[None, :]).astype(jnp.int32)
    earlier = jnp.sum((jnp.cumsum(onehot, axis=0) - onehot) * onehot, axis=1)
    slot_index = target * capacity + earlier
    assign = (
        jnp.full((host_count * capacity,), assignments, jnp.int32)
        .at[slot_index]
        .set(jnp.arange(assignments, dtype=jnp.int32))
    )
    filled = assign < assignments
    row_data = tokens[jnp.minimum(assign, assignments - 1) // top]
    row_data = jnp.where(filled[:, None], row_data, jnp.zeros_like(row_data))
    outgoing = row_data.reshape(host_count, capacity, width)
    received = lax.all_to_all(outgoing, "expert", split_axis=0, concat_axis=0, tiled=True)
    inputs = received.reshape(-1, width)
    projected = jnp.dot(
        inputs, full_weights[:, : 2 * hidden_units], preferred_element_type=jnp.float32
    )
    hidden = (jax.nn.silu(projected[:, :hidden_units]) * projected[:, hidden_units:]).astype(
        jnp.bfloat16
    )
    produced = lax.dot_general(
        hidden,
        full_weights[:, 2 * hidden_units :],
        (((1,), (1,)), ((), ())),
        preferred_element_type=jnp.float32,
    )
    results = produced.astype(jnp.bfloat16).reshape(received.shape)
    returned = lax.all_to_all(results, "expert", split_axis=0, concat_axis=0, tiled=True)
    picked = returned.reshape(host_count * capacity, width)[slot_index]
    weighted = picked.reshape(tok_count, top, width).astype(jnp.float32) * route_weights[:, :, None]
    mixed = jnp.sum(weighted, axis=1).astype(jnp.bfloat16)
    return (new_master, new_one, new_two, mixed)


def solution(mesh):
    return jax.shard_map(
        per_device,
        mesh=mesh,
        in_specs=(
            P("expert", "dp", None),
            P("expert", "dp", None),
            P("expert", "dp", None),
            P("expert", "dp", None),
            P(),
            P(),
            P(("dp", "expert"), None),
            P(("dp", "expert"), None),
            P(("dp", "expert"), None),
        ),
        out_specs=(
            P("expert", "dp", None),
            P("expert", "dp", None),
            P("expert", "dp", None),
            P(("dp", "expert"), None),
        ),
        check_vma=False,
    )
```

profile of v0, /device:TPU:1, one launch (start us, length us, event | category | flops | bytes accessed | tf_op | source)
XLA Modules:
  0.0 689.8 jit_solution(16970705681204284824)
XLA Ops:
  7.2 0.0 copy-start
  7.2 1.8 fusion.9
  8.9 111.0 %psum.7 = f32[]{:T(128)} all-reduce(f32[]{:T(128)} %fusion.9), channel_id=1, replica_groups=mesh['dp'=8,'expert'=64] {'dp','expert'}, use_global_device_ids=true, to_apply=%region_1.0 | all-reduce | flops 1 | bytes 8 | tf_op jit(solution)/shard_map/psum | solution.py:26
  120.7 2.0 multiply_subtract_fusion
  122.7 1.4 all_to_all.58
  124.1 9.1 %all-to-all-start.4 = ((f32[64,1,2304]{2,1,0:T(1,128)}), f32[64,1,2304]{2,1,0:T(1,128)S(1)}, u32[]{:S(2)}, u32[]{:S(2)}) async-start(f32[64,1,2304]{2,1,0:T(1,128)} %all_to_all.58), calls=%async_computation.4 | async-start | bytes 1179648 | tf_op jit(solution)/shard_map/all_to_all | solution.py:41
  133.2 1.4 all_to_all.53
  134.6 30.3 %all-to-all-done.4 = f32[64,1,2304]{2,1,0:T(1,128)S(1)} async-done(((f32[64,1,2304]{2,1,0:T(1,128)}), f32[64,1,2304]{2,1,0:T(1,128)S(1)}, u32[]{:S(2)}, u32[]{:S(2)}) %all-to-all-start.4) | async-done | bytes 589856 | tf_op jit(solution)/shard_map/all_to_all | solution.py:41
  164.9 9.1 %all-to-all-start.2 = ((f32[64,1,2304]{2,1,0:T(1,128)}), f32[64,1,2304]{2,1,0:T(1,128)S(1)}, u32[]{:S(2)}, u32[]{:S(2)}) async-start(f32[64,1,2304]{2,1,0:T(1,128)} %all_to_all.53), calls=%async_computation.2 | async-start | bytes 1179648 | tf_op jit(solution)/shard_map/all_to_all | solution.py:38
  174.1 1.4 all_to_all.48
  175.5 30.1 %all-to-all-done.2 = f32[64,1,2304]{2,1,0:T(1,128)S(1)} async-done(((f32[64,1,2304]{2,1,0:T(1,128)}), f32[64,1,2304]{2,1,0:T(1,128)S(1)}, u32[]{:S(2)}, u32[]{:S(2)}) %all-to-all-start.2) | async-done | bytes 589856 | tf_op jit(solution)/shard_map/all_to_all | solution.py:38
  205.6 9.2 %all-to-all-start = ((f32[64,1,2304]{2,1,0:T(1,128)}), f32[64,1,2304]{2,1,0:T(1,128)S(1)}, u32[]{:S(2)}, u32[]{:S(2)}) async-start(f32[64,1,2304]{2,1,0:T(1,128)} %all_to_all.48), calls=%async_computation | async-start | bytes 1179648 | tf_op jit(solution)/shard_map/all_to_all | solution.py:35
  214.8 0.0 copy-done.5
  214.9 0.8 scatter_custom_fusion
  215.7 0.0 copy-done.1
  215.7 0.8 gather_fusion
  216.5 0.8 gather_fusion.5
  217.4 0.8 gather_fusion.4
  218.2 28.2 %all-to-all-done = f32[64,1,2304]{2,1,0:T(1,128)S(1)} async-done(((f32[64,1,2304]{2,1,0:T(1,128)}), f32[64,1,2304]{2,1,0:T(1,128)S(1)}, u32[]{:S(2)}, u32[]{:S(2)}) %all-to-all-start) | async-done | bytes 589856 | tf_op jit(solution)/shard_map/all_to_all | solution.py:35
  246.4 0.8 gather_fusion.3
  247.2 1.0 select_bitcast_fusion
  248.2 1.4 copy.18
  249.6 9.2 %all-to-all-start.1 = ((f32[64,1,2304]{2,1,0:T(1,128)}), f32[64,1,2304]{2,1,0:T(1,128)S(1)}, u32[]{:S(2)}, u32[]{:S(2)}) async-start(f32[64,1,2304]{2,1,0:T(1,128)} %copy.18), calls=%async_computation.1 | async-start | bytes 1179648 | tf_op jit(solution)/shard_map/all_to_all | solution.py:47
  258.9 1.4 copy.19
  260.3 30.1 %all-to-all-done.1 = f32[64,1,2304]{2,1,0:T(1,128)S(1)} async-done(((f32[64,1,2304]{2,1,0:T(1,128)}), f32[64,1,2304]{2,1,0:T(1,128)S(1)}, u32[]{:S(2)}, u32[]{:S(2)}) %all-to-all-start.1) | async-done | bytes 589856 | tf_op jit(solution)/shard_map/all_to_all | solution.py:47
  290.4 9.6 %all-to-all-start.3 = ((f32[64,1,2304]{2,1,0:T(1,128)}), f32[64,1,2304]{2,1,0:T(1,128)}, u32[]{:S(2)}, u32[]{:S(2)}) async-start(f32[64,1,2304]{2,1,0:T(1,128)} %copy.19), calls=%async_computation.3 | async-start | bytes 1179648 | tf_op jit(solution)/shard_map/all_to_all | solution.py:48
  300.0 0.0 copy-done.3
  300.1 0.1 copy.21
  300.2 0.1 eq.38
  300.3 0.1 select_reduce_fusion
  300.4 0.0 copy-done.2
  300.4 18.0 %reduce-window.6 = s32[64,8,128]{2,1,0:T(8,128)S(1)} reduce-window(s32[64,8,128]{2,1,0:T(8,128)S(1)} %fusion.14, s32[]{:T(128)} %constant.26.clone.1), window={size=1x1x128 pad=0_0x0_0x127_0}, to_apply=%region_4.6 | reduce-window | flops 8323072 | bytes 524292 | tf_op jit(solution)/shard_map/reduce-window
  318.4 0.1 slice.36
  318.5 0.1 copy.22
  318.7 0.1 copy.23
  318.8 0.1 broadcast_add_fusion
  319.0 0.1 fusion.13
  319.1 4.3 scatter_custom_fusion.1
  323.4 0.1 broadcast_in_dim.55
  323.6 5.1 gather_fusion.1
  328.6 1.9 broadcast_select_fusion
  330.5 0.4 all-to-all-done.3
  330.9 13.9 %all-to-all-start.6 = ((bf16[64,24,1024]{2,1,0:T(8,128)(2,1)}), bf16[64,24,1024]{2,1,0:T(8,128)(2,1)S(1)}, u32[]{:S(2)}, u32[]{:S(2)}) async-start(bf16[64,24,1024]{2,1,0:T(8,128)(2,1)} %broadcast_select_fusion), calls=%async_computation.6 | async-start | bytes 6291456 | tf_op jit(solution)/shard_map/all_to_all | solution.py:89
  344.9 0.0 all-gather.2.cloned.1.call-start
  344.9 3.3 reduce
  348.2 2.0 reshape.121
  350.1 1.8 convert_element_type.40
  352.0 0.0 all-gather.2.cloned.1.call-update
  352.0 2.5 copy.20
  354.5 128.0 %all-to-all-done.6 = bf16[64,24,1024]{2,1,0:T(8,128)(2,1)S(1)} async-done(((bf16[64,24,1024]{2,1,0:T(8,128)(2,1)}), bf16[64,24,1024]{2,1,0:T(8,128)(2,1)S(1)}, u32[]{:S(2)}, u32[]{:S(2)}) %all-to-all-start.6) | async-done | bytes 3145760 | tf_op jit(solution)/shard_map/all_to_all | solution.py:89
  482.5 13.2 %all-to-all-start.5 = ((f32[64,1,2304]{2,1,0:T(1,128)}), f32[64,1,2304]{2,1,0:T(1,128)}, u32[]{:S(2)}, u32[]{:S(2)}) async-start(f32[64,1,2304]{2,1,0:T(1,128)} %copy.20), calls=%async_computation.5 | async-start | bytes 1179648 | tf_op jit(solution)/shard_map/all_to_all | solution.py:49
  495.7 0.0 all-gather.2.cloned.1.call-done
  495.7 4.0 fusion.2
  499.8 4.6 convolution_convert_fusion
  504.4 22.9 %all-to-all-done.5 = f32[64,1,2304]{2,1,0:T(1,128)} async-done(((f32[64,1,2304]{2,1,0:T(1,128)}), f32[64,1,2304]{2,1,0:T(1,128)}, u32[]{:S(2)}, u32[]{:S(2)}) %all-to-all-start.5) | async-done | bytes 589856 | tf_op jit(solution)/shard_map/all_to_all | solution.py:49
  527.3 9.2 %all-to-all-start.7 = ((bf16[64,24,1024]{2,1,0:T(8,128)(2,1)}), bf16[64,24,1024]{2,1,0:T(8,128)(2,1)S(1)}, u32[]{:S(2)}, u32[]{:S(2)}) async-start(bf16[64,24,1024]{2,1,0:T(8,128)(2,1)} %bitcast.51), calls=%async_computation.7 | async-start | bytes 6291456 | tf_op jit(solution)/shard_map/all_to_all | solution.py:104
  536.6 0.1 copy.24
  536.7 3.3 reduce.1
  540.0 2.0 reshape.122
  541.9 3.3 reduce.2
  545.2 2.0 reshape.123
  547.2 126.8 %all-to-all-done.7 = bf16[64,24,1024]{2,1,0:T(8,128)(2,1)S(1)} async-done(((bf16[64,24,1024]{2,1,0:T(8,128)(2,1)}), bf16[64,24,1024]{2,1,0:T(8,128)(2,1)S(1)}, u32[]{:S(2)}, u32[]{:S(2)}) %all-to-all-start.7) | async-done | bytes 3145760 | tf_op jit(solution)/shard_map/all_to_all | solution.py:104
  674.0 5.4 gather_fusion.2
  679.3 3.7 fusion
  (27 shorter events, 0.3 us)
Async XLA Ops:
  7.2 316.4 %copy-start = (bf16[128,1024]{1,0:T(8,128)(2,1)S(1)}, bf16[128,1024]{1,0:T(8,128)(2,1)}, u32[]{:S(2)}) copy-start(bf16[128,1024]{1,0:T(8,128)(2,1)} %param.17) | copy-start | bytes 786436
  124.1 90.8 %copy-start.5 = (s32[64]{0:T(128)S(1)}, s32[64]{0:T(128)}, u32[]{:S(2)}) copy-start(s32[64]{0:T(128)} %param.16) | copy-start | bytes 772
  124.1 91.6 %copy-start.1 = (s32[64]{0:T(128)S(1)}, s32[64]{0:T(128)}, u32[]{:S(2)}) copy-start(s32[64]{0:T(128)} %param.15) | copy-start | bytes 772
  124.1 40.8 %all-to-all-start.4 = ((f32[64,1,2304]{2,1,0:T(1,128)}), f32[64,1,2304]{2,1,0:T(1,128)S(1)}, u32[]{:S(2)}, u32[]{:S(2)}) async-start(f32[64,1,2304]{2,1,0:T(1,128)} %all_to_all.58), calls=%async_computation.4 | async-start | bytes 1179648 | tf_op jit(solution)/shard_map/all_to_all | solution.py:41
  164.9 40.7 %all-to-all-start.2 = ((f32[64,1,2304]{2,1,0:T(1,128)}), f32[64,1,2304]{2,1,0:T(1,128)S(1)}, u32[]{:S(2)}, u32[]{:S(2)}) async-start(f32[64,1,2304]{2,1,0:T(1,128)} %all_to_all.53), calls=%async_computation.2 | async-start | bytes 1179648 | tf_op jit(solution)/shard_map/all_to_all | solution.py:38
  205.6 40.8 %all-to-all-start = ((f32[64,1,2304]{2,1,0:T(1,128)}), f32[64,1,2304]{2,1,0:T(1,128)S(1)}, u32[]{:S(2)}, u32[]{:S(2)}) async-start(f32[64,1,2304]{2,1,0:T(1,128)} %all_to_all.48), calls=%async_computation | async-start | bytes 1179648 | tf_op jit(solution)/shard_map/all_to_all | solution.py:35
  248.2 51.8 %copy-start.3 = (s32[128,8]{0,1:T(8,128)S(1)}, s32[128,8]{0,1:T(8,128)}, u32[]{:S(2)}) copy-start(s32[128,8]{0,1:T(8,128)} %param.18) | copy-start | bytes 12292
  249.6 40.8 %all-to-all-start.1 = ((f32[64,1,2304]{2,1,0:T(1,128)}), f32[64,1,2304]{2,1,0:T(1,128)S(1)}, u32[]{:S(2)}, u32[]{:S(2)}) async-start(f32[64,1,2304]{2,1,0:T(1,128)} %copy.18), calls=%async_computation.1 | async-start | bytes 1179648 | tf_op jit(solution)/shard_map/all_to_all | solution.py:47
  290.4 9.9 %copy-start.2 = (f32[64,1,2304]{2,1,0:T(1,128)}, f32[64,1,2304]{2,1,0:T(1,128)S(1)}, u32[]{:S(2)}) copy-start(f32[64,1,2304]{2,1,0:T(1,128)S(1)} %all-to-all-done.1) | copy-start | bytes 1769476
  290.4 40.5 %all-to-all-start.3 = ((f32[64,1,2304]{2,1,0:T(1,128)}), f32[64,1,2304]{2,1,0:T(1,128)}, u32[]{:S(2)}, u32[]{:S(2)}) async-start(f32[64,1,2304]{2,1,0:T(1,128)} %copy.19), calls=%async_computation.3 | async-start | bytes 1179648 | tf_op jit(solution)/shard_map/all_to_all | solution.py:48
  330.9 151.6 %all-to-all-start.6 = ((bf16[64,24,1024]{2,1,0:T(8,128)(2,1)}), bf16[64,24,1024]{2,1,0:T(8,128)(2,1)S(1)}, u32[]{:S(2)}, u32[]{:S(2)}) async-start(bf16[64,24,1024]{2,1,0:T(8,128)(2,1)} %broadcast_select_fusion), calls=%async_computation.6 | async-start | bytes 6291456 | tf_op jit(solution)/shard_map/all_to_all | solution.py:89
  344.9 150.9 %all-gather.2.cloned.1.call-start = ((), (), s32[]{:S(2)}) async-start(), calls=%async_computation.8 | async-start | bytes 2654208 | tf_op jit(solution)/shard_map/all_gather | solution.py:66
  482.5 44.8 %all-to-all-start.5 = ((f32[64,1,2304]{2,1,0:T(1,128)}), f32[64,1,2304]{2,1,0:T(1,128)}, u32[]{:S(2)}, u32[]{:S(2)}) async-start(f32[64,1,2304]{2,1,0:T(1,128)} %copy.20), calls=%async_computation.5 | async-start | bytes 1179648 | tf_op jit(solution)/shard_map/all_to_all | solution.py:49
  527.3 9.3 %copy-start.4 = (f32[128,8]{0,1:T(8,128)S(1)}, f32[128,8]{0,1:T(8,128)}, u32[]{:S(2)}) copy-start(f32[128,8]{0,1:T(8,128)} %param.19) | copy-start | bytes 12292
  527.3 146.7 %all-to-all-start.7 = ((bf16[64,24,1024]{2,1,0:T(8,128)(2,1)}), bf16[64,24,1024]{2,1,0:T(8,128)(2,1)S(1)}, u32[]{:S(2)}, u32[]{:S(2)}) async-start(bf16[64,24,1024]{2,1,0:T(8,128)(2,1)} %bitcast.51), calls=%async_computation.7 | async-start | bytes 6291456 | tf_op jit(solution)/shard_map/all_to_all | solution.py:104
Sparse Core Ops, SparseCore 0:
  352.1 33.8 all-gather.1
where the time goes:
time: 696 us; the launch traced here: 690 us
  waiting for transfers between devices  397 us (57%)
  blocking collectives  111 us (16%)
  starting transfers between devices  82.7 us (12%)
  other arithmetic  40.4 us (6%)
  local copies, waits for them, and re-layouts  35 us (5%)
  between operations  15.1 us (2%)
  matrix products  8.67 us (1%)
    all_to_all x1, waiting for transfers between devices, per_device(): lax.all_to_all(outgoing, 'expert', split_axis=0, concat_axis=0, tiled=True)  128 us
    all_to_all x1, waiting for transfers between devices, per_device(): lax.all_to_all(results, 'expert', split_axis=0, concat_axis=0, tiled=True)  127 us
    psum x1, blocking collectives, clip_factor(): square_sum = lax.psum(local_sum, ('dp', 'expert'))  111 us
    all_to_all x1, waiting for transfers between devices, relocate_state(): lax.all_to_all(moment_two.reshape(host_count, -1), 'expert', split_axis=0...  30.3 us
    all_to_all x1, waiting for transfers between devices, relocate_state(): lax.all_to_all(ordered[0], 'expert', split_axis=0, concat_axis=0, tiled=T...  30.1 us
    all_to_all x1, waiting for transfers between devices, relocate_state(): lax.all_to_all(moment_one.reshape(host_count, -1), 'expert', split_axis=0...  30.1 us
    all_to_all x1, waiting for transfers between devices, relocate_state(): lax.all_to_all(master.reshape(host_count, -1), 'expert', split_axis=0, co...  28.2 us
    all_to_all x1, waiting for transfers between devices, relocate_state(): lax.all_to_all(ordered[2], 'expert', split_axis=0, concat_axis=0, tiled=T...  22.9 us
  transfers between devices with their start and end apart: 9, of which 8 were waited for; matrix products, arithmetic and copies ran while one was open for 9% of the time, Pallas kernels for 0%

commit v1 on v0

v1 whole, which is shorter than its diff:
```python
import jax
import jax.numpy as jnp
from jax import lax
from jax.sharding import Mesh, PartitionSpec as P

beta_one = 0.9
beta_two = 0.95
epsilon = 1e-08
learn_rate = 0.001
decay_rate = 0.1
step_count = 10

Y, CORE, X, Z = 4, 2, 4, 16
DP = ("y", "c")
PLANE = ("y", "c", "x")
SHARE = Z // (Y * CORE)
bf16, f32 = jnp.bfloat16, jnp.float32


def adamw(master, moment_one, moment_two, gradients, factor):
    scaled = gradients.astype(f32) * factor
    new_one = beta_one * moment_one + (1.0 - beta_one) * scaled
    new_two = beta_two * moment_two + (1.0 - beta_two) * scaled * scaled
    corrected_one = new_one / (1.0 - beta_one**step_count)
    corrected_two = new_two / (1.0 - beta_two**step_count)
    step_size = corrected_one / (jnp.sqrt(corrected_two) + epsilon) + decay_rate * master
    return (master - learn_rate * step_size, new_one, new_two)


def swap(array, axes):
    return lax.all_to_all(array, axes, split_axis=0, concat_axis=0, tiled=True)


def total(value, axes):
    count = lax.axis_size(axes)
    sent = jnp.broadcast_to(value, (count, 1, 128))
    return jnp.sum(swap(sent, axes)[:, 0, 0])


def per_device(
    master, moment_one, moment_two, gradients, old_host, new_host, tokens, routes, route_weights
):
    master, moment_one, moment_two, gradients = (
        item[0] for item in (master, moment_one, moment_two, gradients)
    )
    rows, cols = master.shape
    host_count = X * Z
    my_x, my_z = lax.axis_index("x"), lax.axis_index("z")
    my_host = my_x * Z + my_z
    hosts = jnp.arange(host_count, dtype=jnp.int32)

    local_sum = jnp.sum(jnp.square(gradients.astype(f32)))
    square_sum = total(total(local_sum, PLANE), "z")
    element_count = host_count * Y * CORE * rows * cols
    factor = jnp.minimum(1.0, jnp.sqrt(f32(element_count)) / (jnp.sqrt(square_sum) + 1e-06))

    owner_hot = (new_host[None, :] == hosts[:, None]).astype(jnp.int32)
    source = jnp.sum(owner_hot * old_host[None, :], axis=1)

    tok_count, width = tokens.shape
    top = routes.shape[1]
    capacity = 3 * tok_count * top // (2 * host_count)
    place = ((old_host % Z) // SHARE * X + old_host // Z) * SHARE + old_host % SHARE
    route_place = jnp.sum(
        jnp.where(routes[:, :, None] == hosts[None, None, :], place[None, None, :], 0), axis=2
    ).T
    hits = route_place[None, :, :] == hosts[:, None, None]
    chosen = jnp.any(hits, axis=1)
    gate = jnp.sum(jnp.where(hits, route_weights.T[None, :, :], 0.0), axis=1)
    token_ids = jnp.arange(tok_count, dtype=jnp.int32)
    before = (token_ids[:, None] < token_ids[None, :]).astype(bf16)
    rank = jnp.dot(chosen.astype(bf16), before, preferred_element_type=f32)
    slot = jnp.where(chosen, rank, -1.0)
    slot_ids = jnp.arange(capacity, dtype=jnp.int32).astype(f32)
    taken = slot[:, None, :] == slot_ids[None, :, None]
    pick = taken.astype(bf16).reshape(-1, tok_count)
    outgoing = jnp.dot(pick, tokens, preferred_element_type=f32).astype(bf16)
    outgoing = outgoing.reshape(Y * CORE * X, SHARE * capacity, width)
    mix = jnp.where(taken, gate[:, None, :], 0.0).reshape(-1, tok_count)
    mix_high = mix.astype(bf16)
    mix_low = (mix - mix_high.astype(f32)).astype(bf16)
    outgoing, factor = lax.optimization_barrier((outgoing, factor))

    new_master, new_one, new_two = adamw(master, moment_one, moment_two, gradients, factor)
    gathered = lax.all_gather(new_master.astype(bf16), "z", axis=0, tiled=True)
    moments = jnp.stack([new_one.astype(bf16), new_two.astype(bf16)])
    quarter = rows // X
    moments = moments.reshape(2, X, quarter, cols).transpose(1, 0, 2, 3)
    received = swap(outgoing, PLANE)
    moments, received = lax.optimization_barrier((moments, received))
    moments = swap(moments, "x")
    moments, gathered, received = lax.optimization_barrier((moments, gathered, received))
    moments = lax.all_gather(moments.reshape(-1, cols), "z", axis=0, tiled=True)

    planes = gathered.reshape(Z, rows, cols)
    weights = swap(gathered.reshape(Y * CORE, SHARE * rows, cols), DP)
    weights = weights.reshape(Y * CORE, SHARE, rows, cols)
    hidden_units = cols // 3
    inputs = received.reshape(-1, SHARE, capacity, width)
    outs = []
    for j in range(SHARE):
        weight = weights[:, j].reshape(-1, cols)
        rows_in = inputs[:, j].reshape(-1, width)
        projected = jnp.dot(rows_in, weight[:, : 2 * hidden_units], preferred_element_type=f32)
        hidden = (jax.nn.silu(projected[:, :hidden_units]) * projected[:, hidden_units:]).astype(bf16)
        produced = lax.dot_general(
            hidden,
            weight[:, 2 * hidden_units :],
            (((1,), (1,)), ((), ())),
            preferred_element_type=f32,
        )
        outs.append(produced.astype(bf16).reshape(-1, capacity, width))
    results = jnp.stack(outs, axis=1).reshape(received.shape)
    returned = swap(results, PLANE).reshape(-1, width)
    contract = (((0,), (0,)), ((), ()))
    mixed = lax.dot_general(mix_high, returned, contract, preferred_element_type=f32)
    mixed += lax.dot_general(mix_low, returned, contract, preferred_element_type=f32)
    mixed = mixed.astype(bf16)

    plane_source = source.reshape(X, Z)[:, my_z]
    src_x, src_z = plane_source // Z, plane_source % Z
    sent = jnp.stack([lax.dynamic_index_in_dim(planes, src_z[i], 0, False) for i in range(X)])
    sent, returned = lax.optimization_barrier((sent, returned))
    arrived = swap(sent, "x")
    moved_master = lax.dynamic_index_in_dim(arrived, src_x[my_x], 0, False)
    pieces = moments.reshape(Z, X, 2, quarter, cols)
    sent = jnp.stack(
        [
            lax.dynamic_slice(pieces, (src_z[i], src_x[i], 0, 0, 0), (1, 1, 2, quarter, cols))[0, 0]
            for i in range(X)
        ]
    )
    arrived = swap(sent, "x")
    moved_moments = arrived.transpose(1, 0, 2, 3).reshape(2, rows, cols)
    moved = source[my_host] != my_host
    return (
        jnp.where(moved, moved_master.astype(f32), new_master)[None],
        jnp.where(moved, moved_moments[0].astype(f32), new_one)[None],
        jnp.where(moved, moved_moments[1].astype(f32), new_two)[None],
        mixed,
    )


def solution(mesh):
    fine = Mesh(mesh.devices.reshape(Y, CORE, X, Z), ("y", "c", "x", "z"))
    state = P(("x", "z"), DP, None)
    rows = P(("y", "c", "x", "z"), None)
    return jax.shard_map(
        per_device,
        mesh=fine,
        in_specs=(state, state, state, state, P(), P(), rows, rows, rows),
        out_specs=(state, state, state, rows),
        check_vma=False,
    )
```

time: 696 us -> 287 us (0.41)
  waiting for transfers between devices: 397 us -> 139 us
  blocking collectives: 111 us -> 14.8 us
  starting transfers between devices: 82.7 us -> 56.6 us
  other arithmetic: 40.4 us -> 17.7 us
  local copies, waits for them, and re-layouts: 35 us -> 13.3 us
  between operations: 15.1 us -> 32.9 us
    all_to_all x8 -> x7, waiting for transfers between devices: 397 us -> 119 us  [swap(): return lax.all_to_all(array, axes, split_axis=0, concat_axis=0, tiled=True)]
    psum x1 -> x0, blocking collectives: 111 us -> none  [clip_factor(): square_sum = lax.psum(local_sum, ('dp', 'expert'))]
    all_to_all x8 -> x7, starting transfers between devices: 82.7 us -> 56.5 us  [swap(): return lax.all_to_all(array, axes, split_axis=0, concat_axis=0, tiled=True)]
    all_gather x1 -> x2, waiting for transfers between devices: 0.02 us -> 20.2 us  [the longest x1 17.1 us: per_device(): moments = lax.all_gather(moments.reshape(-1, cols), 'z', axis=0, tiled=True)]
    all_to_all x0 -> x1, blocking collectives: none -> 14.8 us  [swap(): return lax.all_to_all(array, axes, split_axis=0, concat_axis=0, tiled=True)]
    another operation x3, other arithmetic: 18.2 us -> 4.01 us  [the longest x1 1.9 us: per_device(): results = jnp.stack(outs, axis=1).reshape(received.shape)]
    gather x6 -> x0, local copies, waits for them, and re-layouts: 13.6 us -> none  [the longest x1 5.35 us: per_device(): picked = returned.reshape(host_count * capacity, width)[slot_index]]
    all_to_all x4 -> x0, other arithmetic: 10.8 us -> none  [the longest x2 4.27 us: relocate_state(): lax.all_to_all(ordered[2], 'expert', split_axis=0, concat_axis=0, tiled=T...]
  transfers between devices with their start and end apart: 9 -> 9, of which waited for: 8 -> 8; matrix products, arithmetic and copies ran while one was open for 9% -> 11% of each run, Pallas kernels for 0% -> 0%
where the time goes in v1:
time: 287 us; the launch traced here: 285 us
  waiting for transfers between devices  139 us (48%)
  starting transfers between devices  56.6 us (20%)
  between operations  32.9 us (11%)
  other arithmetic  17.7 us (6%)
  blocking collectives  14.8 us (5%)
  local copies, waits for them, and re-layouts  13.3 us (5%)
  matrix products  10.5 us (4%)
    all_to_all x7, waiting for transfers between devices, swap(): return lax.all_to_all(array, axes, split_axis=0, concat_axis=0, tiled=True)  119 us
    all_to_all x7, starting transfers between devices, swap(): return lax.all_to_all(array, axes, split_axis=0, concat_axis=0, tiled=True)  56.5 us
    all_gather x1, waiting for transfers between devices, per_device(): moments = lax.all_gather(moments.reshape(-1, cols), 'z', axis=0, tiled=True)  17.1 us
    all_to_all x1, blocking collectives, swap(): return lax.all_to_all(array, axes, split_axis=0, concat_axis=0, tiled=True)  14.8 us
  transfers between devices with their start and end apart: 9, of which 8 were waited for; matrix products, arithmetic and copies ran while one was open for 11% of the time, Pallas kernels for 0%

profile of v1, /device:TPU:1, one launch (start us, length us, event | category | flops | bytes accessed | tf_op | source)
XLA Modules:
  0.0 285.1 jit_solution(17409572028023099250)
XLA Ops:
  7.2 0.0 copy-start
  7.2 1.8 fusion.20
  8.9 1.3 broadcast_in_dim.66
  10.2 10.4 %all-to-all-start = ((f32[32,1,128]{2,1,0:T(1,128)}), f32[32,1,128]{2,1,0:T(1,128)S(1)}, u32[]{:S(2)}, u32[]{:S(2)}) async-start(f32[32,1,128]{2,1,0:T(1,128)} %broadcast_in_dim.66), calls=%async_computation | async-start | bytes 32768 | tf_op jit(solution)/shard_map/all_to_all | solution.py:31
  20.6 0.7 fusion.34
  21.3 0.8 select_reduce_fusion.1
  22.1 0.1 fusion.31
  22.2 0.1 convolution_select_fusion
  22.3 0.1 eq.95
  22.4 0.3 bitcast_compare_fusion
  22.7 4.9 %all-to-all-done = f32[32,1,128]{2,1,0:T(1,128)S(1)} async-done(((f32[32,1,128]{2,1,0:T(1,128)}), f32[32,1,128]{2,1,0:T(1,128)S(1)}, u32[]{:S(2)}, u32[]{:S(2)}) %all-to-all-start) | async-done | bytes 16416 | tf_op jit(solution)/shard_map/all_to_all | solution.py:31
  27.5 0.6 slice_reduce_fusion
  28.2 1.2 broadcast_in_dim.67
  29.4 13.0 %all-to-all-start.1 = ((f32[16,1,128]{2,1,0:T(1,128)}), f32[16,1,128]{2,1,0:T(1,128)S(1)}, u32[]{:S(2)}, u32[]{:S(2)}) async-start(f32[16,1,128]{2,1,0:T(1,128)} %broadcast_in_dim.67), calls=%async_computation.1 | async-start | bytes 16384 | tf_op jit(solution)/shard_map/all_to_all | solution.py:31
  42.5 0.0 copy-start.1
  42.5 0.0 copy-start.3
  42.5 0.0 copy-start.5
  42.5 0.0 copy-start.6
  42.5 0.0 all-gather.3.cloned.1.call-start
  42.6 2.6 convolution_convert_fusion
  45.2 8.5 %all-to-all-done.1 = f32[16,1,128]{2,1,0:T(1,128)S(1)} async-done(((f32[16,1,128]{2,1,0:T(1,128)}), f32[16,1,128]{2,1,0:T(1,128)S(1)}, u32[]{:S(2)}, u32[]{:S(2)}) %all-to-all-start.1) | async-done | bytes 8224 | tf_op jit(solution)/shard_map/all_to_all | solution.py:31
  53.7 0.6 slice_reduce_fusion.1
  55.1 1.2 fusion.30
  56.3 0.0 all-gather.3.cloned.1.call-update
  56.3 5.8 %all-to-all-start.2 = ((bf16[32,48,1024]{2,1,0:T(8,128)(2,1)}), bf16[32,48,1024]{2,1,0:T(8,128)(2,1)S(1)}, u32[]{:S(2)}, u32[]{:S(2)}) async-start(bf16[32,48,1024]{2,1,0:T(8,128)(2,1)} %bitcast.3), calls=%async_computation.2 | async-start | bytes 6291456 | tf_op jit(solution)/shard_map/all_to_all | solution.py:31
  62.1 0.0 all-gather.5.cloned.1.call-start
  62.2 1.5 fusion.32
  63.7 0.9 maximum_bitcast_fusion
  64.6 35.5 %all-to-all-done.2 = bf16[32,48,1024]{2,1,0:T(8,128)(2,1)S(1)} async-done(((bf16[32,48,1024]{2,1,0:T(8,128)(2,1)}), bf16[32,48,1024]{2,1,0:T(8,128)(2,1)S(1)}, u32[]{:S(2)}, u32[]{:S(2)}) %all-to-all-start.2) | async-done | bytes 3145760 | tf_op jit(solution)/shard_map/all_to_all | solution.py:31
  100.1 14.8 %all_to_all.40 = bf16[4,2,32,1152]{3,2,1,0:T(8,128)(2,1)} all-to-all(bf16[4,2,32,1152]{3,2,1,0:T(8,128)(2,1)} %maximum_bitcast_fusion), channel_id=1, replica_groups=mesh['y'=4,'c'=2,'x'=4,'z'=16] {'x'}, dimensions={0} | all-to-all | bytes 1179648 | tf_op jit(solution)/shard_map/all_to_all | solution.py:31
  114.9 3.2 %all-gather.3.cloned.1.call-done = bf16[2048,1152]{1,0:T(8,128)(2,1)} async-done(((bf16[128,1152]{1,0:T(8,128)(2,1)}), bf16[2048,1152]{1,0:T(8,128)(2,1)}) %all-gather.3.cloned.1.call-update) | async-done | bytes 4718608 | tf_op jit(solution)/shard_map/all_gather | solution.py:85
  118.0 0.0 all-gather.5.cloned.1.call-update
  118.1 12.8 %all-to-all-start.4 = ((bf16[8,256,1152]{2,1,0:T(8,128)(2,1)}), bf16[8,256,1152]{2,1,0:T(8,128)(2,1)}, u32[]{:S(2)}, u32[]{:S(2)}) async-start(bf16[8,256,1152]{2,1,0:T(8,128)(2,1)} %bitcast.110), calls=%async_computation.4 | async-start | bytes 9437184 | tf_op jit(solution)/shard_map/all_to_all | solution.py:31
  130.9 2.1 fusion.39
  132.9 52.5 %all-to-all-done.4 = bf16[8,256,1152]{2,1,0:T(8,128)(2,1)} async-done(((bf16[8,256,1152]{2,1,0:T(8,128)(2,1)}), bf16[8,256,1152]{2,1,0:T(8,128)(2,1)}, u32[]{:S(2)}, u32[]{:S(2)}) %all-to-all-start.4) | async-done | bytes 4718624 | tf_op jit(solution)/shard_map/all_to_all | solution.py:31
  185.4 2.9 %fusion.38 = (bf16[8,1,128,1152]{3,2,1,0:T(8,128)(2,1)S(1)}, bf16[8,1,128,1152]{3,2,1,0:T(8,128)(2,1)S(1)}) fusion(bf16[8,2,128,1152]{3,2,1,0:T(8,128)(2,1)} %bitcast.19), kind=kLoop, calls=%fused_computation.93 | loop fusion | bytes 9437184 | tf_op jit(solution)/shard_map/slice | solution.py:102
  188.4 1.4 fusion.2
  189.8 1.0 convolution_convert_fusion.2
  190.8 0.4 copy-done.8
  191.2 1.4 fusion
  192.6 1.0 convolution_convert_fusion.1
  193.6 1.9 pad_maximum_fusion
  195.5 6.0 %all-to-all-start.5 = ((bf16[32,48,1024]{2,1,0:T(8,128)(2,1)}), bf16[32,48,1024]{2,1,0:T(8,128)(2,1)S(1)}, u32[]{:S(2)}, u32[]{:S(2)}) async-start(bf16[32,48,1024]{2,1,0:T(8,128)(2,1)} %bitcast.108), calls=%async_computation.5 | async-start | bytes 6291456 | tf_op jit(solution)/shard_map/all_to_all | solution.py:31
  201.5 0.1 select_reduce_fusion.2
  201.7 0.1 reshape.165
  201.7 0.2 fusion.33
  202.0 0.7 fusion.41
  214.1 0.7 dynamic_slice.38
  221.2 0.1 select_reduce_fusion
  221.2 0.9 select_convert_fusion
  222.2 0.9 fusion.7
  223.1 17.1 %all-gather.5.cloned.1.call-done = bf16[4096,1152]{1,0:T(8,128)(2,1)} async-done(((bf16[256,1152]{1,0:T(8,128)(2,1)}), bf16[4096,1152]{1,0:T(8,128)(2,1)}) %all-gather.5.cloned.1.call-update) | async-done | bytes 9437200 | tf_op jit(solution)/shard_map/all_gather | solution.py:93
  240.2 1.2 dynamic-slice_bitcast_fusion.3
  241.3 0.9 pad_maximum_fusion.2
  242.3 4.2 %all-to-all-start.7 = ((bf16[4,2,32,1152]{3,2,1,0:T(8,128)(2,1)}), bf16[4,2,32,1152]{3,2,1,0:T(8,128)(2,1)}, u32[]{:S(2)}, u32[]{:S(2)}) async-start(bf16[4,2,32,1152]{3,2,1,0:T(8,128)(2,1)} %pad_maximum_fusion.2), calls=%async_computation.7 | async-start | bytes 1179648 | tf_op jit(solution)/shard_map/all_to_all | solution.py:31
  246.4 1.3 constant_dynamic-slice_fusion.3
  247.8 1.2 pad_maximum_fusion.1
  248.9 7.0 %all-to-all-done.7 = bf16[4,2,32,1152]{3,2,1,0:T(8,128)(2,1)} async-done(((bf16[4,2,32,1152]{3,2,1,0:T(8,128)(2,1)}), bf16[4,2,32,1152]{3,2,1,0:T(8,128)(2,1)}, u32[]{:S(2)}, u32[]{:S(2)}) %all-to-all-start.7) | async-done | bytes 589856 | tf_op jit(solution)/shard_map/all_to_all | solution.py:31
  255.9 4.3 %all-to-all-start.6 = ((bf16[4,128,1152]{2,1,0:T(8,128)(2,1)}), bf16[4,128,1152]{2,1,0:T(8,128)(2,1)}, u32[]{:S(2)}, u32[]{:S(2)}) async-start(bf16[4,128,1152]{2,1,0:T(8,128)(2,1)} %pad_maximum_fusion.1), calls=%async_computation.6 | async-start | bytes 2359296 | tf_op jit(solution)/shard_map/all_to_all | solution.py:31
  260.2 1.6 fusion.43
  261.9 1.3 fusion.4
  263.2 1.2 fusion.40
  264.4 10.7 %all-to-all-done.6 = bf16[4,128,1152]{2,1,0:T(8,128)(2,1)} async-done(((bf16[4,128,1152]{2,1,0:T(8,128)(2,1)}), bf16[4,128,1152]{2,1,0:T(8,128)(2,1)}, u32[]{:S(2)}, u32[]{:S(2)}) %all-to-all-start.6) | async-done | bytes 1179680 | tf_op jit(solution)/shard_map/all_to_all | solution.py:31
  275.1 3.1 %convert_select_fusion = (f32[1,128,1152]{2,1,0:T(8,128)}, f32[1,128,1152]{2,1,0:T(8,128)}, f32[1,128,1152]{2,1,0:T(8,128)}) fusion(bf16[1,128,1152]{2,1,0:T(8,128)(2,1)S(1)} %bitcast.125, pred[]{:T(512)S(6)} %ne.54, f32[]{:T(128)S(6)} %min_shard_map.3, bf16[1,128,1152]{2,1,0:T(8,128)(2,1)} %param.12, f32[1,128,1152]{2,1,0:T(8,128)S(1)} %copy-done.2, ...), kind=kLoop, calls=%fused_computation.44 | loop fusion | flops 3391488 | bytes 4718601 | tf_op jit(solution)/shard_map/jit(_where)/select_n | solution.py:139
  (24 shorter events, 0.1 us)
Async XLA Ops:
  7.2 35.4 %copy-start = (bf16[128,1024]{1,0:T(8,128)(2,1)S(1)}, bf16[128,1024]{1,0:T(8,128)(2,1)}, u32[]{:S(2)}) copy-start(bf16[128,1024]{1,0:T(8,128)(2,1)} %param.15) | copy-start | bytes 786436
  10.2 17.3 %all-to-all-start = ((f32[32,1,128]{2,1,0:T(1,128)}), f32[32,1,128]{2,1,0:T(1,128)S(1)}, u32[]{:S(2)}, u32[]{:S(2)}) async-start(f32[32,1,128]{2,1,0:T(1,128)} %broadcast_in_dim.66), calls=%async_computation | async-start | bytes 32768 | tf_op jit(solution)/shard_map/all_to_all | solution.py:31
  29.4 24.3 %all-to-all-start.1 = ((f32[16,1,128]{2,1,0:T(1,128)}), f32[16,1,128]{2,1,0:T(1,128)S(1)}, u32[]{:S(2)}, u32[]{:S(2)}) async-start(f32[16,1,128]{2,1,0:T(1,128)} %broadcast_in_dim.67), calls=%async_computation.1 | async-start | bytes 16384 | tf_op jit(solution)/shard_map/all_to_all | solution.py:31
  42.5 12.6 %copy-start.1 = (f32[1,128,1152]{2,1,0:T(8,128)S(1)}, f32[1,128,1152]{2,1,0:T(8,128)}, u32[]{:S(2)}) copy-start(f32[1,128,1152]{2,1,0:T(8,128)} %param.11) | copy-start | bytes 1769476
  42.5 12.6 %copy-start.3 = (f32[1,128,1152]{2,1,0:T(8,128)S(1)}, f32[1,128,1152]{2,1,0:T(8,128)}, u32[]{:S(2)}) copy-start(f32[1,128,1152]{2,1,0:T(8,128)} %param.10) | copy-start | bytes 1769476
  42.5 12.6 %copy-start.5 = (bf16[1,128,1152]{2,1,0:T(8,128)(2,1)S(1)}, bf16[1,128,1152]{2,1,0:T(8,128)(2,1)}, u32[]{:S(2)}) copy-start(bf16[1,128,1152]{2,1,0:T(8,128)(2,1)} %param.12) | copy-start | bytes 884740
  42.5 12.6 %copy-start.6 = (f32[1,128,1152]{2,1,0:T(8,128)S(1)}, f32[1,128,1152]{2,1,0:T(8,128)}, u32[]{:S(2)}) copy-start(f32[1,128,1152]{2,1,0:T(8,128)} %param.9) | copy-start | bytes 1769476
  42.5 75.5 %all-gather.3.cloned.1.call-start = ((), (), s32[]{:S(2)}) async-start(), calls=%async_computation.8 | async-start | bytes 5013504 | tf_op jit(solution)/shard_map/all_gather | solution.py:85
  56.3 43.8 %all-to-all-start.2 = ((bf16[32,48,1024]{2,1,0:T(8,128)(2,1)}), bf16[32,48,1024]{2,1,0:T(8,128)(2,1)S(1)}, u32[]{:S(2)}, u32[]{:S(2)}) async-start(bf16[32,48,1024]{2,1,0:T(8,128)(2,1)} %bitcast.3), calls=%async_computation.2 | async-start | bytes 6291456 | tf_op jit(solution)/shard_map/all_to_all | solution.py:31
  62.1 178.1 %all-gather.5.cloned.1.call-start = ((), (), s32[]{:S(2)}) async-start(), calls=%async_computation.9 | async-start | bytes 10027008 | tf_op jit(solution)/shard_map/all_gather | solution.py:93
  118.1 67.4 %all-to-all-start.4 = ((bf16[8,256,1152]{2,1,0:T(8,128)(2,1)}), bf16[8,256,1152]{2,1,0:T(8,128)(2,1)}, u32[]{:S(2)}, u32[]{:S(2)}) async-start(bf16[8,256,1152]{2,1,0:T(8,128)(2,1)} %bitcast.110), calls=%async_computation.4 | async-start | bytes 9437184 | tf_op jit(solution)/shard_map/all_to_all | solution.py:31
  185.4 2.9 %copy-start.9 = (bf16[32,1,24,1024]{3,2,1,0:T(8,128)(2,1)S(1)}, bf16[32,1,24,1024]{3,2,1,0:T(8,128)(2,1)}, u32[]{:S(2)}) copy-start(bf16[32,1,24,1024]{3,2,1,0:T(8,128)(2,1)} %get-tuple-element.30) | copy-start | bytes 4718596
  189.8 1.4 copy-start.8
  195.5 6.0 %copy-start.11 = (s32[64]{0:T(128)S(1)}, s32[64]{0:T(128)}, u32[]{:S(2)}) copy-start(s32[64]{0:T(128)} %param.13) | copy-start | bytes 772
  195.5 6.0 %copy-start.12 = (s32[64]{0:T(128)S(1)}, s32[64]{0:T(128)}, u32[]{:S(2)}) copy-start(s32[64]{0:T(128)} %param.14) | copy-start | bytes 772
  195.5 25.6 %copy-start.10 = (f32[128,8]{0,1:T(8,128)S(1)}, f32[128,8]{0,1:T(8,128)}, u32[]{:S(2)}) copy-start(f32[128,8]{0,1:T(8,128)} %param.17) | copy-start | bytes 12292
  195.5 46.7 %all-to-all-start.5 = ((bf16[32,48,1024]{2,1,0:T(8,128)(2,1)}), bf16[32,48,1024]{2,1,0:T(8,128)(2,1)S(1)}, u32[]{:S(2)}, u32[]{:S(2)}) async-start(bf16[32,48,1024]{2,1,0:T(8,128)(2,1)} %bitcast.108), calls=%async_computation.5 | async-start | bytes 6291456 | tf_op jit(solution)/shard_map/all_to_all | solution.py:31
  242.3 13.7 %all-to-all-start.7 = ((bf16[4,2,32,1152]{3,2,1,0:T(8,128)(2,1)}), bf16[4,2,32,1152]{3,2,1,0:T(8,128)(2,1)}, u32[]{:S(2)}, u32[]{:S(2)}) async-start(bf16[4,2,32,1152]{3,2,1,0:T(8,128)(2,1)} %pad_maximum_fusion.2), calls=%async_computation.7 | async-start | bytes 1179648 | tf_op jit(solution)/shard_map/all_to_all | solution.py:31
  255.9 19.2 %all-to-all-start.6 = ((bf16[4,128,1152]{2,1,0:T(8,128)(2,1)}), bf16[4,128,1152]{2,1,0:T(8,128)(2,1)}, u32[]{:S(2)}, u32[]{:S(2)}) async-start(bf16[4,128,1152]{2,1,0:T(8,128)(2,1)} %pad_maximum_fusion.1), calls=%async_computation.6 | async-start | bytes 2359296 | tf_op jit(solution)/shard_map/all_to_all | solution.py:31
  260.2 1.7 copy-start.7
  263.2 11.9 %copy-start.2 = (f32[1,128,1152]{2,1,0:T(8,128)S(1)}, f32[1,128,1152]{2,1,0:T(8,128)}, u32[]{:S(2)}) copy-start(f32[1,128,1152]{2,1,0:T(8,128)} %param.11) | copy-start | bytes 1769476
  263.2 11.9 %copy-start.4 = (f32[1,128,1152]{2,1,0:T(8,128)S(1)}, f32[1,128,1152]{2,1,0:T(8,128)}, u32[]{:S(2)}) copy-start(f32[1,128,1152]{2,1,0:T(8,128)} %param.10) | copy-start | bytes 1769476
Sparse Core Ops, SparseCore 0:
  56.4 61.5 all-gather.2
  120.1 120.0 all-gather.4

commit v2 on v1

--- a/solution.py
+++ b/solution.py
@@ -1,6 +1,7 @@
 import jax
 import jax.numpy as jnp
 from jax import lax
+from jax.experimental import pallas as pl
 from jax.sharding import Mesh, PartitionSpec as P
 
 beta_one = 0.9
@@ -31,10 +32,26 @@
     return lax.all_to_all(array, axes, split_axis=0, concat_axis=0, tiled=True)
 
 
-def total(value, axes):
-    count = lax.axis_size(axes)
-    sent = jnp.broadcast_to(value, (count, 1, 128))
-    return jnp.sum(swap(sent, axes)[:, 0, 0])
+def spread_squares(values, sent):
+    value = values[...].astype(f32)
+    sent[...] = jnp.full(sent.shape, jnp.sum(value * value), f32)
+
+
+def spread_sum(values, sent):
+    sent[...] = jnp.broadcast_to(jnp.sum(values[...], axis=0, keepdims=True), sent.shape)
+
+
+def spread(kernel, operand, axes):
+    return pl.pallas_call(
+        kernel, out_shape=jax.ShapeDtypeStruct((lax.axis_size(axes), 1, 128), f32)
+    )(operand)
+
+
+def shifted(blocks, size):
+    return [
+        lax.ppermute(block, "x", [(i, (i + shift) % size) for i in range(size)])
+        for shift, block in enumerate(blocks, 1)
+    ]
 
 
 def per_device(
@@ -49,8 +66,9 @@
     my_host = my_x * Z + my_z
     hosts = jnp.arange(host_count, dtype=jnp.int32)
 
-    local_sum = jnp.sum(jnp.square(gradients.astype(f32)))
-    square_sum = total(total(local_sum, PLANE), "z")
+    squares = swap(spread(spread_squares, gradients, PLANE), PLANE)
+    squares = swap(spread(spread_sum, squares, "z"), "z")
+    square_sum = jnp.sum(squares[:, 0, 0])
     element_count = host_count * Y * CORE * rows * cols
     factor = jnp.minimum(1.0, jnp.sqrt(f32(element_count)) / (jnp.sqrt(square_sum) + 1e-06))
 
@@ -89,10 +107,17 @@
     received = swap(outgoing, PLANE)
     moments, received = lax.optimization_barrier((moments, received))
     moments = swap(moments, "x")
-    moments, gathered, received = lax.optimization_barrier((moments, gathered, received))
     moments = lax.all_gather(moments.reshape(-1, cols), "z", axis=0, tiled=True)
 
     planes = gathered.reshape(Z, rows, cols)
+    plane_source = source.reshape(X, Z)[:, my_z]
+    src_x, src_z = plane_source // Z, plane_source % Z
+    to = [(my_x + shift) % X for shift in range(X)]
+    held = [lax.dynamic_index_in_dim(planes, src_z[i], 0, False) for i in to]
+    arrived = held[:1] + shifted(held[1:], X)
+    back = (my_x - src_x[my_x]) % X
+    moved_master = lax.select_n(back, *arrived)
+
     weights = swap(gathered.reshape(Y * CORE, SHARE * rows, cols), DP)
     weights = weights.reshape(Y * CORE, SHARE, rows, cols)
     hidden_units = cols // 3
@@ -117,20 +142,14 @@
     mixed += lax.dot_general(mix_low, returned, contract, preferred_element_type=f32)
     mixed = mixed.astype(bf16)
 
-    plane_source = source.reshape(X, Z)[:, my_z]
-    src_x, src_z = plane_source // Z, plane_source % Z
-    sent = jnp.stack([lax.dynamic_index_in_dim(planes, src_z[i], 0, False) for i in range(X)])
-    sent, returned = lax.optimization_barrier((sent, returned))
-    arrived = swap(sent, "x")
-    moved_master = lax.dynamic_index_in_dim(arrived, src_x[my_x], 0, False)
     pieces = moments.reshape(Z, X, 2, quarter, cols)
-    sent = jnp.stack(
-        [
-            lax.dynamic_slice(pieces, (src_z[i], src_x[i], 0, 0, 0), (1, 1, 2, quarter, cols))[0, 0]
-            for i in range(X)
-        ]
-    )
-    arrived = swap(sent, "x")
+    held = [
+        lax.dynamic_slice(pieces, (src_z[i], src_x[i], 0, 0, 0), (1, 1, 2, quarter, cols))[0, 0]
+        for i in to
+    ]
+    arrived = jnp.stack(held[:1] + shifted(held[1:], X))
+    order = (my_x - jnp.arange(X, dtype=jnp.int32)) % X
+    arrived = jnp.take(arrived, order, axis=0)
     moved_moments = arrived.transpose(1, 0, 2, 3).reshape(2, rows, cols)
     moved = source[my_host] != my_host
     return (

time: 287 us -> 282 us (0.983)
  waiting for transfers between devices: 139 us -> 126 us
  starting transfers between devices: 56.6 us -> 67.4 us
  other arithmetic: 17.7 us -> 13.6 us
  Pallas kernels: 0 us -> 3.35 us
    ppermute x0 -> x6, waiting for transfers between devices: none -> 21.7 us  [shifted(): lax.ppermute(block, 'x', [(i, (i + shift) % size) for i in range(size)])]
    ppermute x0 -> x6, starting transfers between devices: none -> 19.2 us  [shifted(): lax.ppermute(block, 'x', [(i, (i + shift) % size) for i in range(size)])]
    all_to_all x7 -> x5, waiting for transfers between devices: 119 us -> 101 us  [swap(): return lax.all_to_all(array, axes, split_axis=0, concat_axis=0, tiled=True)]
    all_gather x1, waiting for transfers between devices: 17.1 us -> 0.01 us  [per_device(): moments = lax.all_gather(moments.reshape(-1, cols), 'z', axis=0, tiled=True)]
    all_to_all x7 -> x5, starting transfers between devices: 56.5 us -> 48.2 us  [swap(): return lax.all_to_all(array, axes, split_axis=0, concat_axis=0, tiled=True)]
    pallas_call x0 -> x2, Pallas kernels: none -> 3.35 us  [spread(): pl.pallas_call(kernel, out_shape=jax.ShapeDtypeStruct((lax.axis_size(axes...]
  transfers between devices with their start and end apart: 9 -> 13, of which waited for: 8 -> 8; matrix products, arithmetic and copies ran while one was open for 11% -> 11% of each run, Pallas kernels for 0% -> 0%
where the time goes in v2:
time: 282 us; the launch traced here: 281 us
  waiting for transfers between devices  126 us (45%)
  starting transfers between devices  67.4 us (24%)
  between operations  31.7 us (11%)
  blocking collectives  14.8 us (5%)
  other arithmetic  13.6 us (5%)
  matrix products  12.4 us (4%)
  local copies, waits for them, and re-layouts  11.2 us (4%)
  Pallas kernels  3.35 us (1%)
    all_to_all x5, waiting for transfers between devices, swap(): return lax.all_to_all(array, axes, split_axis=0, concat_axis=0, tiled=True)  101 us
    all_to_all x5, starting transfers between devices, swap(): return lax.all_to_all(array, axes, split_axis=0, concat_axis=0, tiled=True)  48.2 us
    ppermute x6, waiting for transfers between devices, shifted(): lax.ppermute(block, 'x', [(i, (i + shift) % size) for i in range(size)])  21.7 us
    ppermute x6, starting transfers between devices, shifted(): lax.ppermute(block, 'x', [(i, (i + shift) % size) for i in range(size)])  19.2 us
    all_to_all x1, blocking collectives, swap(): return lax.all_to_all(array, axes, split_axis=0, concat_axis=0, tiled=True)  14.8 us
  transfers between devices with their start and end apart: 13, of which 8 were waited for; matrix products, arithmetic and copies ran while one was open for 11% of the time, Pallas kernels for 0%

profile of v2, /device:TPU:1, one launch (start us, length us, event | category | flops | bytes accessed | tf_op | source)
XLA Modules:
  0.0 280.5 jit_solution(12406931579454140235)
XLA Ops:
  7.2 2.0 shard_map.120
  9.2 10.4 %all-to-all-start = ((f32[32,1,128]{2,1,0:T(1,128)}), f32[32,1,128]{2,1,0:T(1,128)S(1)}, u32[]{:S(2)}, u32[]{:S(2)}) async-start(f32[32,1,128]{2,1,0:T(1,128)} %shard_map.120), calls=%async_computation | async-start | bytes 32768 | tf_op jit(solution)/shard_map/all_to_all | solution.py:32
  19.6 0.7 fusion.27
  20.3 0.8 select_reduce_fusion.1
  21.1 0.1 fusion.25
  21.2 0.1 convolution_select_fusion
  21.3 0.1 eq.102
  21.4 0.3 bitcast_compare_fusion
  21.7 4.9 %all-to-all-done.values = f32[32,1,128]{2,1,0:T(1,128)S(1)} async-done(((f32[32,1,128]{2,1,0:T(1,128)}), f32[32,1,128]{2,1,0:T(1,128)S(1)}, u32[]{:S(2)}, u32[]{:S(2)}) %all-to-all-start) | async-done | bytes 16416 | tf_op jit(solution)/shard_map/all_to_all | solution.py:32
  26.5 0.6 copy-done.11
  27.2 1.4 shard_map.121
  28.5 13.0 %all-to-all-start.1 = ((f32[16,1,128]{2,1,0:T(1,128)}), f32[16,1,128]{2,1,0:T(1,128)S(1)}, u32[]{:S(2)}, u32[]{:S(2)}) async-start(f32[16,1,128]{2,1,0:T(1,128)} %shard_map.121), calls=%async_computation.1 | async-start | bytes 16384 | tf_op jit(solution)/shard_map/all_to_all | solution.py:32
  41.6 0.0 all-gather.3.cloned.1.call-start
  41.6 2.6 convolution_convert_fusion
  44.2 8.6 %all-to-all-done.1 = f32[16,1,128]{2,1,0:T(1,128)S(1)} async-done(((f32[16,1,128]{2,1,0:T(1,128)}), f32[16,1,128]{2,1,0:T(1,128)S(1)}, u32[]{:S(2)}, u32[]{:S(2)}) %all-to-all-start.1) | async-done | bytes 8224 | tf_op jit(solution)/shard_map/all_to_all | solution.py:32
  52.8 0.6 slice_reduce_fusion
  54.2 1.4 fusion.33
  55.6 5.8 %all-to-all-start.2 = ((bf16[32,48,1024]{2,1,0:T(8,128)(2,1)}), bf16[32,48,1024]{2,1,0:T(8,128)(2,1)S(1)}, u32[]{:S(2)}, u32[]{:S(2)}) async-start(bf16[32,48,1024]{2,1,0:T(8,128)(2,1)} %bitcast.7), calls=%async_computation.2 | async-start | bytes 6291456 | tf_op jit(solution)/shard_map/all_to_all | solution.py:32
  61.4 0.0 all-gather.5.cloned.1.call-start
  61.5 1.5 fusion.22
  63.0 0.9 maximum_bitcast_fusion
  63.9 35.5 %all-to-all-done.2 = bf16[32,48,1024]{2,1,0:T(8,128)(2,1)S(1)} async-done(((bf16[32,48,1024]{2,1,0:T(8,128)(2,1)}), bf16[32,48,1024]{2,1,0:T(8,128)(2,1)S(1)}, u32[]{:S(2)}, u32[]{:S(2)}) %all-to-all-start.2) | async-done | bytes 3145760 | tf_op jit(solution)/shard_map/all_to_all | solution.py:32
  99.4 14.8 %all_to_all.30 = bf16[4,2,32,1152]{3,2,1,0:T(8,128)(2,1)} all-to-all(bf16[4,2,32,1152]{3,2,1,0:T(8,128)(2,1)} %maximum_bitcast_fusion), channel_id=1, replica_groups=mesh['y'=4,'c'=2,'x'=4,'z'=16] {'x'}, dimensions={0} | all-to-all | bytes 1179648 | tf_op jit(solution)/shard_map/all_to_all | solution.py:32
  114.2 3.0 %all-gather.3.cloned.1.call-done = bf16[2048,1152]{1,0:T(8,128)(2,1)} async-done(((bf16[128,1152]{1,0:T(8,128)(2,1)}), bf16[2048,1152]{1,0:T(8,128)(2,1)}) %all-gather.3.cloned.1.call-update) | async-done | bytes 4718608 | tf_op jit(solution)/shard_map/all_gather | solution.py:103
  117.2 12.8 %all-to-all-start.4 = ((bf16[8,256,1152]{2,1,0:T(8,128)(2,1)}), bf16[8,256,1152]{2,1,0:T(8,128)(2,1)}, u32[]{:S(2)}, u32[]{:S(2)}) async-start(bf16[8,256,1152]{2,1,0:T(8,128)(2,1)} %bitcast.114), calls=%async_computation.4 | async-start | bytes 9437184 | tf_op jit(solution)/shard_map/all_to_all | solution.py:32
  129.9 2.1 fusion.35
  132.0 52.5 %all-to-all-done.4 = bf16[8,256,1152]{2,1,0:T(8,128)(2,1)} async-done(((bf16[8,256,1152]{2,1,0:T(8,128)(2,1)}), bf16[8,256,1152]{2,1,0:T(8,128)(2,1)}, u32[]{:S(2)}, u32[]{:S(2)}) %all-to-all-start.4) | async-done | bytes 4718624 | tf_op jit(solution)/shard_map/all_to_all | solution.py:32
  184.5 2.9 %fusion.34 = (bf16[8,1,128,1152]{3,2,1,0:T(8,128)(2,1)S(1)}, bf16[8,1,128,1152]{3,2,1,0:T(8,128)(2,1)S(1)}) fusion(bf16[8,2,128,1152]{3,2,1,0:T(8,128)(2,1)} %bitcast.46), kind=kLoop, calls=%fused_computation.101 | loop fusion | bytes 9437184 | tf_op jit(solution)/shard_map/slice | solution.py:127
  187.4 1.4 fusion.2
  188.8 1.0 convolution_convert_fusion.2
  189.8 0.4 copy-done.8
  190.2 1.4 fusion
  191.6 1.0 convolution_convert_fusion.1
  192.6 1.9 pad_maximum_fusion
  194.6 6.2 %all-to-all-start.5 = ((bf16[32,48,1024]{2,1,0:T(8,128)(2,1)}), bf16[32,48,1024]{2,1,0:T(8,128)(2,1)S(1)}, u32[]{:S(2)}, u32[]{:S(2)}) async-start(bf16[32,48,1024]{2,1,0:T(8,128)(2,1)} %bitcast.112), calls=%async_computation.5 | async-start | bytes 6291456 | tf_op jit(solution)/shard_map/all_to_all | solution.py:32
  200.9 0.1 select_reduce_fusion.2
  201.0 0.1 reshape.213
  201.1 0.2 fusion.26
  201.3 0.7 fusion.37
  212.8 0.6 dynamic_slice.62
  219.1 0.1 select_reduce_fusion
  219.2 0.9 select_convert_fusion
  220.2 1.2 dynamic-slice_bitcast_fusion
  221.4 3.3 %collective-permute-start = (bf16[128,1152]{1,0:T(8,128)(2,1)S(1)}, bf16[128,1152]{1,0:T(8,128)(2,1)S(1)}, u32[]{:S(2)}, u32[]{:S(2)}) collective-permute-start(bf16[128,1152]{1,0:T(8,128)(2,1)S(1)} %get-tuple-element.22), channel_id=1, source_target_pairs={{0,16},{16,32},{32,48},{48,0},{1,17},{17,33},{33,49},{49,1},{2,18}... | collective-permute-start | bytes 884744 | tf_op jit(solution)/shard_map/ppermute | solution.py:52
  224.7 4.3 %collective-permute-start.1 = (bf16[128,1152]{1,0:T(8,128)(2,1)S(1)}, bf16[128,1152]{1,0:T(8,128)(2,1)S(1)}, u32[]{:S(2)}, u32[]{:S(2)}) collective-permute-start(bf16[128,1152]{1,0:T(8,128)(2,1)S(1)} %get-tuple-element.21), channel_id=1, source_target_pairs={{0,32},{16,48},{32,0},{48,16},{1,33},{17,49},{33,1},{49,17},{2,34}... | collective-permute-start | bytes 884744 | tf_op jit(solution)/shard_map/ppermute | solution.py:52
  229.0 3.1 %collective-permute-start.2 = (bf16[128,1152]{1,0:T(8,128)(2,1)S(1)}, bf16[128,1152]{1,0:T(8,128)(2,1)S(1)}, u32[]{:S(2)}, u32[]{:S(2)}) collective-permute-start(bf16[128,1152]{1,0:T(8,128)(2,1)S(1)} %get-tuple-element.20), channel_id=1, source_target_pairs={{0,48},{16,0},{32,16},{48,32},{1,49},{17,1},{33,17},{49,33},{2,50}... | collective-permute-start | bytes 884744 | tf_op jit(solution)/shard_map/ppermute | solution.py:52
  232.2 0.9 fusion.7
  233.1 11.7 %collective-permute-done = bf16[128,1152]{1,0:T(8,128)(2,1)S(1)} collective-permute-done((bf16[128,1152]{1,0:T(8,128)(2,1)S(1)}, bf16[128,1152]{1,0:T(8,128)(2,1)S(1)}, u32[]{:S(2)}, u32[]{:S(2)}) %collective-permute-start) | collective-permute-done | bytes 294944 | tf_op jit(solution)/shard_map/ppermute | solution.py:52
  244.8 7.5 %collective-permute-done.1 = bf16[128,1152]{1,0:T(8,128)(2,1)S(1)} collective-permute-done((bf16[128,1152]{1,0:T(8,128)(2,1)S(1)}, bf16[128,1152]{1,0:T(8,128)(2,1)S(1)}, u32[]{:S(2)}, u32[]{:S(2)}) %collective-permute-start.1) | collective-permute-done | bytes 294944 | tf_op jit(solution)/shard_map/ppermute | solution.py:52
  252.3 1.9 select_bitcast_fusion.1
  254.2 2.4 fusion.39
  256.6 1.2 dynamic-slice_bitcast_fusion.6
  257.7 1.9 collective-permute-start.3
  259.7 2.4 collective-permute-start.4
  262.0 4.1 %collective-permute-start.5 = (bf16[2,32,1152]{2,1,0:T(8,128)(2,1)S(1)}, bf16[2,32,1152]{2,1,0:T(8,128)(2,1)S(1)}, u32[]{:S(2)}, u32[]{:S(2)}) collective-permute-start(bf16[2,32,1152]{2,1,0:T(8,128)(2,1)S(1)} %get-tuple-element.15), channel_id=1, source_target_pairs={{0,48},{16,0},{32,16},{48,32},{1,49},{17,1},{33,17},{49,33},{2,50}... | collective-permute-start | bytes 442376 | tf_op jit(solution)/shard_map/ppermute | solution.py:52
  266.2 2.5 fusion.4
  268.6 2.5 collective-permute-done.5
  271.1 0.1 pad_maximum_fusion.1
  271.2 0.6 gather_fusion
  271.9 0.1 select_bitcast_fusion
  272.1 0.1 copy-done.2
  272.2 0.2 copy-done.4
  272.4 0.1 copy-done.6
  272.4 1.3 convert_select_fusion
  (39 shorter events, 0.2 us)
Async XLA Ops:
  7.2 34.4 %copy-start = (bf16[128,1024]{1,0:T(8,128)(2,1)S(1)}, bf16[128,1024]{1,0:T(8,128)(2,1)}, u32[]{:S(2)}) copy-start(bf16[128,1024]{1,0:T(8,128)(2,1)} %param.15) | copy-start | bytes 786436
  7.2 47.0 %copy-start.5 = (bf16[1,128,1152]{2,1,0:T(8,128)(2,1)S(1)}, bf16[1,128,1152]{2,1,0:T(8,128)(2,1)}, u32[]{:S(2)}) copy-start(bf16[1,128,1152]{2,1,0:T(8,128)(2,1)} %param.12) | copy-start | bytes 884740
  7.2 46.9 %copy-start.3 = (f32[1,128,1152]{2,1,0:T(8,128)S(1)}, f32[1,128,1152]{2,1,0:T(8,128)}, u32[]{:S(2)}) copy-start(f32[1,128,1152]{2,1,0:T(8,128)} %param.10) | copy-start | bytes 1769476
  7.2 46.9 %copy-start.1 = (f32[1,128,1152]{2,1,0:T(8,128)S(1)}, f32[1,128,1152]{2,1,0:T(8,128)}, u32[]{:S(2)}) copy-start(f32[1,128,1152]{2,1,0:T(8,128)} %param.11) | copy-start | bytes 1769476
  7.2 46.9 %copy-start.10 = (f32[1,128,1152]{2,1,0:T(8,128)S(1)}, f32[1,128,1152]{2,1,0:T(8,128)}, u32[]{:S(2)}) copy-start(f32[1,128,1152]{2,1,0:T(8,128)} %param.9) | copy-start | bytes 1769476
  9.2 17.3 %all-to-all-start = ((f32[32,1,128]{2,1,0:T(1,128)}), f32[32,1,128]{2,1,0:T(1,128)S(1)}, u32[]{:S(2)}, u32[]{:S(2)}) async-start(f32[32,1,128]{2,1,0:T(1,128)} %shard_map.120), calls=%async_computation | async-start | bytes 32768 | tf_op jit(solution)/shard_map/all_to_all | solution.py:32
  26.5 0.6 copy-start.11
  28.5 24.3 %all-to-all-start.1 = ((f32[16,1,128]{2,1,0:T(1,128)}), f32[16,1,128]{2,1,0:T(1,128)S(1)}, u32[]{:S(2)}, u32[]{:S(2)}) async-start(f32[16,1,128]{2,1,0:T(1,128)} %shard_map.121), calls=%async_computation.1 | async-start | bytes 16384 | tf_op jit(solution)/shard_map/all_to_all | solution.py:32
  41.6 75.6 %all-gather.3.cloned.1.call-start = ((), (), s32[]{:S(2)}) async-start(), calls=%async_computation.6 | async-start | bytes 5013504 | tf_op jit(solution)/shard_map/all_gather | solution.py:103
  55.6 43.8 %all-to-all-start.2 = ((bf16[32,48,1024]{2,1,0:T(8,128)(2,1)}), bf16[32,48,1024]{2,1,0:T(8,128)(2,1)S(1)}, u32[]{:S(2)}, u32[]{:S(2)}) async-start(bf16[32,48,1024]{2,1,0:T(8,128)(2,1)} %bitcast.7), calls=%async_computation.2 | async-start | bytes 6291456 | tf_op jit(solution)/shard_map/all_to_all | solution.py:32
  61.4 195.1 %all-gather.5.cloned.1.call-start = ((), (), s32[]{:S(2)}) async-start(), calls=%async_computation.7 | async-start | bytes 10027008 | tf_op jit(solution)/shard_map/all_gather | solution.py:110
  117.2 67.3 %all-to-all-start.4 = ((bf16[8,256,1152]{2,1,0:T(8,128)(2,1)}), bf16[8,256,1152]{2,1,0:T(8,128)(2,1)}, u32[]{:S(2)}, u32[]{:S(2)}) async-start(bf16[8,256,1152]{2,1,0:T(8,128)(2,1)} %bitcast.114), calls=%async_computation.4 | async-start | bytes 9437184 | tf_op jit(solution)/shard_map/all_to_all | solution.py:32
  184.5 2.9 %copy-start.9 = (bf16[32,1,24,1024]{3,2,1,0:T(8,128)(2,1)S(1)}, bf16[32,1,24,1024]{3,2,1,0:T(8,128)(2,1)}, u32[]{:S(2)}) copy-start(bf16[32,1,24,1024]{3,2,1,0:T(8,128)(2,1)} %get-tuple-element.23) | copy-start | bytes 4718596
  188.8 1.4 copy-start.8
  194.6 6.3 %copy-start.13 = (s32[64]{0:T(128)S(1)}, s32[64]{0:T(128)}, u32[]{:S(2)}) copy-start(s32[64]{0:T(128)} %param.13) | copy-start | bytes 772
  194.6 6.3 %copy-start.14 = (s32[64]{0:T(128)S(1)}, s32[64]{0:T(128)}, u32[]{:S(2)}) copy-start(s32[64]{0:T(128)} %param.14) | copy-start | bytes 772
  194.6 24.6 %copy-start.12 = (f32[128,8]{0,1:T(8,128)S(1)}, f32[128,8]{0,1:T(8,128)}, u32[]{:S(2)}) copy-start(f32[128,8]{0,1:T(8,128)} %param.17) | copy-start | bytes 12292
  194.6 59.6 %all-to-all-start.5 = ((bf16[32,48,1024]{2,1,0:T(8,128)(2,1)}), bf16[32,48,1024]{2,1,0:T(8,128)(2,1)S(1)}, u32[]{:S(2)}, u32[]{:S(2)}) async-start(bf16[32,48,1024]{2,1,0:T(8,128)(2,1)} %bitcast.112), calls=%async_computation.5 | async-start | bytes 6291456 | tf_op jit(solution)/shard_map/all_to_all | solution.py:32
  219.1 33.2 %copy-start.7 = (f32[128,1152]{1,0:T(8,128)S(1)}, f32[128,1152]{1,0:T(8,128)}, u32[]{:S(2)}) copy-start(f32[128,1152]{1,0:T(8,128)} %get-tuple-element.13) | copy-start | bytes 1769476
  221.4 23.4 %collective-permute-start = (bf16[128,1152]{1,0:T(8,128)(2,1)S(1)}, bf16[128,1152]{1,0:T(8,128)(2,1)S(1)}, u32[]{:S(2)}, u32[]{:S(2)}) collective-permute-start(bf16[128,1152]{1,0:T(8,128)(2,1)S(1)} %get-tuple-element.22), channel_id=1, source_target_pairs={{0,16},{16,32},{32,48},{48,0},{1,17},{17,33},{33,49},{49,1},{2,18}... | collective-permute-start | bytes 884744 | tf_op jit(solution)/shard_map/ppermute | solution.py:52
  224.7 27.6 %collective-permute-start.1 = (bf16[128,1152]{1,0:T(8,128)(2,1)S(1)}, bf16[128,1152]{1,0:T(8,128)(2,1)S(1)}, u32[]{:S(2)}, u32[]{:S(2)}) collective-permute-start(bf16[128,1152]{1,0:T(8,128)(2,1)S(1)} %get-tuple-element.21), channel_id=1, source_target_pairs={{0,32},{16,48},{32,0},{48,16},{1,33},{17,49},{33,1},{49,17},{2,34}... | collective-permute-start | bytes 884744 | tf_op jit(solution)/shard_map/ppermute | solution.py:52
  229.0 23.3 %collective-permute-start.2 = (bf16[128,1152]{1,0:T(8,128)(2,1)S(1)}, bf16[128,1152]{1,0:T(8,128)(2,1)S(1)}, u32[]{:S(2)}, u32[]{:S(2)}) collective-permute-start(bf16[128,1152]{1,0:T(8,128)(2,1)S(1)} %get-tuple-element.20), channel_id=1, source_target_pairs={{0,48},{16,0},{32,16},{48,32},{1,49},{17,1},{33,17},{49,33},{2,50}... | collective-permute-start | bytes 884744 | tf_op jit(solution)/shard_map/ppermute | solution.py:52
  257.7 10.9 %collective-permute-start.3 = (bf16[2,32,1152]{2,1,0:T(8,128)(2,1)S(1)}, bf16[2,32,1152]{2,1,0:T(8,128)(2,1)S(1)}, u32[]{:S(2)}, u32[]{:S(2)}) collective-permute-start(bf16[2,32,1152]{2,1,0:T(8,128)(2,1)S(1)} %get-tuple-element.17), channel_id=1, source_target_pairs={{0,16},{16,32},{32,48},{48,0},{1,17},{17,33},{33,49},{49,1},{2,18}... | collective-permute-start | bytes 442376 | tf_op jit(solution)/shard_map/ppermute | solution.py:52
  259.7 9.0 %collective-permute-start.4 = (bf16[2,32,1152]{2,1,0:T(8,128)(2,1)S(1)}, bf16[2,32,1152]{2,1,0:T(8,128)(2,1)S(1)}, u32[]{:S(2)}, u32[]{:S(2)}) collective-permute-start(bf16[2,32,1152]{2,1,0:T(8,128)(2,1)S(1)} %get-tuple-element.16), channel_id=1, source_target_pairs={{0,32},{16,48},{32,0},{48,16},{1,33},{17,49},{33,1},{49,17},{2,34}... | collective-permute-start | bytes 442376 | tf_op jit(solution)/shard_map/ppermute | solution.py:52
  262.0 9.1 %collective-permute-start.5 = (bf16[2,32,1152]{2,1,0:T(8,128)(2,1)S(1)}, bf16[2,32,1152]{2,1,0:T(8,128)(2,1)S(1)}, u32[]{:S(2)}, u32[]{:S(2)}) collective-permute-start(bf16[2,32,1152]{2,1,0:T(8,128)(2,1)S(1)} %get-tuple-element.15), channel_id=1, source_target_pairs={{0,48},{16,0},{32,16},{48,32},{1,49},{17,1},{33,17},{49,33},{2,50}... | collective-permute-start | bytes 442376 | tf_op jit(solution)/shard_map/ppermute | solution.py:52
  271.1 1.1 copy-start.2
  271.1 1.2 copy-start.4
  271.1 1.3 copy-start.6
Sparse Core Ops, SparseCore 0:
  55.7 61.3 all-gather.2
  119.2 120.0 all-gather.4

commit v3 on v2

--- a/solution.py
+++ b/solution.py
@@ -2,6 +2,7 @@
 import jax.numpy as jnp
 from jax import lax
 from jax.experimental import pallas as pl
+from jax.experimental.pallas import tpu as pltpu
 from jax.sharding import Mesh, PartitionSpec as P
 
 beta_one = 0.9
@@ -12,8 +13,11 @@
 step_count = 10
 
 Y, CORE, X, Z = 4, 2, 4, 16
+NEAR = 4
+SLOTS = 10
 DP = ("y", "c")
 PLANE = ("y", "c", "x")
+RING = ("far", "near")
 SHARE = Z // (Y * CORE)
 bf16, f32 = jnp.bfloat16, jnp.float32
 
@@ -47,6 +51,172 @@
     )(operand)
 
 
+PLANE_AT, GROUP_AT, SLOT_AT, BACK, MOVED, MY_X, OVER, PICK_AT, PLAN = 0, 4, 8, 12, 13, 14, 15, 16, 32
+
+
+def make_plan(old_host, new_host, plan, source, target, rank):
+    my_x = lax.axis_index("x")
+    my_group = lax.axis_index("far")
+    my_z = my_group * NEAR + lax.axis_index("near")
+
+    @pl.loop(0, X * Z)
+    def _(expert):
+        source[new_host[expert]] = old_host[expert]
+        target[old_host[expert]] = new_host[expert]
+
+    for k in range(SLOTS):
+        plan[PICK_AT + k] = 0
+    over = jnp.int32(0)
+    for group in range(Z // NEAR):
+
+        def visit(place, count, group=group):
+            host = (place // NEAR) * Z + group * NEAR + lax.rem(place, NEAR)
+            leaves = target[host] != host
+            rank[host] = count
+
+            @pl.when(leaves & (my_group == group) & (count < SLOTS))
+            def _():
+                plan[PICK_AT + count] = place
+
+            return count + leaves.astype(jnp.int32)
+
+        count = lax.fori_loop(0, X * NEAR, visit, jnp.int32(0))
+        over = jnp.maximum(over, (count > SLOTS).astype(jnp.int32))
+    for shift in range(X):
+        host = source[lax.rem(my_x + shift, X) * Z + my_z]
+        plan[PLANE_AT + shift] = lax.rem(host, Z)
+        plan[GROUP_AT + shift] = lax.rem(host, Z) // NEAR
+        plan[SLOT_AT + shift] = jnp.minimum(rank[host], SLOTS - 1)
+    mine = source[my_x * Z + my_z]
+    plan[BACK] = lax.rem(my_x + X - mine // Z, X)
+    plan[MOVED] = (mine != my_x * Z + my_z).astype(jnp.int32)
+    plan[MY_X] = my_x
+    plan[OVER] = over
+
+
+def plan_of(old_host, new_host):
+    scalars = pl.BlockSpec(memory_space=pltpu.SMEM)
+    return pl.pallas_call(
+        make_plan,
+        out_shape=jax.ShapeDtypeStruct((PLAN,), jnp.int32),
+        in_specs=[scalars, scalars],
+        out_specs=scalars,
+        scratch_shapes=[pltpu.SMEM((X * Z,), jnp.int32)] * 3,
+    )(old_host, new_host)
+
+
+def copy_picked(plan, *refs):
+    half = len(refs) // 2
+    for taken, kept in zip(refs[:half], refs[half:]):
+        kept[...] = taken[...].reshape(kept.shape)
+
+
+def pick_planes(plan, planes):
+    rows, cols = planes.shape[1:]
+
+    def take(shift):
+        return pl.BlockSpec((1, rows, cols), lambda i, plan: (plan[PLANE_AT + shift], 0, 0))
+
+    return pl.pallas_call(
+        copy_picked,
+        out_shape=[jax.ShapeDtypeStruct((rows, cols), bf16)] * X,
+        grid_spec=pltpu.PrefetchScalarGridSpec(
+            num_scalar_prefetch=1,
+            grid=(1,),
+            in_specs=[take(shift) for shift in range(X)],
+            out_specs=[pl.BlockSpec((rows, cols), lambda i, plan: (0, 0))] * X,
+        ),
+    )(plan, *[planes] * X)
+
+
+def pick_pieces(plan, pieces):
+    rows, cols = pieces.shape[3:]
+    block = (1, NEAR, 1, rows, cols)
+
+    def take(shift):
+        return pl.BlockSpec(
+            block, lambda i, plan: (plan[GROUP_AT + shift], 0, plan[SLOT_AT + shift], 0, 0)
+        )
+
+    return pl.pallas_call(
+        copy_picked,
+        out_shape=[jax.ShapeDtypeStruct((NEAR, rows, cols), bf16)] * X,
+        grid_spec=pltpu.PrefetchScalarGridSpec(
+            num_scalar_prefetch=1,
+            grid=(1,),
+            in_specs=[take(shift) for shift in range(X)],
+            out_specs=[pl.BlockSpec((NEAR, rows, cols), lambda i, plan: (0, 0, 0))] * X,
+        ),
+    )(plan, *[pieces] * X)
+
+
+def compact(plan, pieces, slots):
+    for k in range(SLOTS):
+        slots[k] = pieces[plan[PICK_AT + k]]
+
+
+def compacted(plan, pieces):
+    return pl.pallas_call(
+        compact,
+        out_shape=jax.ShapeDtypeStruct((SLOTS,) + pieces.shape[1:], bf16),
+        grid_spec=pltpu.PrefetchScalarGridSpec(
+            num_scalar_prefetch=1,
+            grid=(1,),
+            in_specs=[pl.BlockSpec(pieces.shape, lambda i, plan: (0, 0, 0))],
+            out_specs=pl.BlockSpec((SLOTS,) + pieces.shape[1:], lambda i, plan: (0, 0, 0)),
+        ),
+    )(plan, pieces)
+
+
+def finish(plan, here, one, two, three, own_one, own_two, new_one, new_two):
+    new_one[...] = own_one[...]
+    new_two[...] = own_two[...]
+
+    @pl.when(plan[MOVED] == 1)
+    def _():
+        for shift, quarter in enumerate((here, one, two, three)):
+            at = lax.rem(plan[MY_X] + X - shift, X) * NEAR
+            for near in range(NEAR):
+                piece = quarter[near].astype(f32)
+                half = piece.shape[0] // 2
+                rows = pl.ds(pl.multiple_of((at + near) * half, half), half)
+                new_one[rows] = piece[:half]
+                new_two[rows] = piece[half:]
+
+
+def finished(plan, arrived, own_one, own_two):
+    whole = pl.BlockSpec(memory_space=pltpu.VMEM)
+    return pl.pallas_call(
+        finish,
+        out_shape=[jax.ShapeDtypeStruct(own_one.shape, f32)] * 2,
+        in_specs=[pl.BlockSpec(memory_space=pltpu.SMEM)] + [whole] * 6,
+        out_specs=[whole] * 2,
+    )(plan, *arrived, own_one, own_two)
+
+
+def relocated_whole(old_host, new_host, own_one, own_two):
+    rows, cols = own_one.shape
+    quarter = rows // X
+    hosts = jnp.arange(X * Z, dtype=jnp.int32)
+    owner_hot = (new_host[None, :] == hosts[:, None]).astype(jnp.int32)
+    source = jnp.sum(owner_hot * old_host[None, :], axis=1)
+    my_x, my_z = lax.axis_index("x"), lax.axis_index(RING)
+    plane_source = source.reshape(X, Z)[:, my_z]
+    src_x, src_z = plane_source // Z, plane_source % Z
+    moments = jnp.stack([own_one.astype(bf16), own_two.astype(bf16)])
+    moments = swap(moments.reshape(2, X, quarter, cols).transpose(1, 0, 2, 3), "x")
+    moments = lax.all_gather(moments.reshape(-1, cols), RING, axis=0, tiled=True)
+    pieces = moments.reshape(Z, X, 2, quarter, cols)
+    size = (1, 1, 2, quarter, cols)
+    sent = [lax.dynamic_slice(pieces, (src_z[i], src_x[i], 0, 0, 0), size)[0, 0] for i in range(X)]
+    arrived = swap(jnp.stack(sent), "x").transpose(1, 0, 2, 3).reshape(2, rows, cols)
+    moved = plane_source[my_x] != my_x * Z + my_z
+    return [
+        jnp.where(moved, arrived[0].astype(f32), own_one),
+        jnp.where(moved, arrived[1].astype(f32), own_two),
+    ]
+
+
 def shifted(blocks, size):
     return [
         lax.ppermute(block, "x", [(i, (i + shift) % size) for i in range(size)])
@@ -62,18 +232,15 @@
     )
     rows, cols = master.shape
     host_count = X * Z
-    my_x, my_z = lax.axis_index("x"), lax.axis_index("z")
-    my_host = my_x * Z + my_z
     hosts = jnp.arange(host_count, dtype=jnp.int32)
 
     squares = swap(spread(spread_squares, gradients, PLANE), PLANE)
-    squares = swap(spread(spread_sum, squares, "z"), "z")
+    squares = swap(spread(spread_sum, squares, RING), RING)
     square_sum = jnp.sum(squares[:, 0, 0])
     element_count = host_count * Y * CORE * rows * cols
     factor = jnp.minimum(1.0, jnp.sqrt(f32(element_count)) / (jnp.sqrt(square_sum) + 1e-06))
 
-    owner_hot = (new_host[None, :] == hosts[:, None]).astype(jnp.int32)
-    source = jnp.sum(owner_hot * old_host[None, :], axis=1)
+    plan = plan_of(old_host, new_host)
 
     tok_count, width = tokens.shape
     top = routes.shape[1]
@@ -97,28 +264,28 @@
     mix = jnp.where(taken, gate[:, None, :], 0.0).reshape(-1, tok_count)
     mix_high = mix.astype(bf16)
     mix_low = (mix - mix_high.astype(f32)).astype(bf16)
+    mix_both = jnp.concatenate([mix_high, mix_low], axis=1)
     outgoing, factor = lax.optimization_barrier((outgoing, factor))
 
     new_master, new_one, new_two = adamw(master, moment_one, moment_two, gradients, factor)
-    gathered = lax.all_gather(new_master.astype(bf16), "z", axis=0, tiled=True)
-    moments = jnp.stack([new_one.astype(bf16), new_two.astype(bf16)])
-    quarter = rows // X
-    moments = moments.reshape(2, X, quarter, cols).transpose(1, 0, 2, 3)
+    gathered = lax.all_gather(new_master.astype(bf16), RING, axis=0, tiled=True)
     received = swap(outgoing, PLANE)
-    moments, received = lax.optimization_barrier((moments, received))
-    moments = swap(moments, "x")
-    moments = lax.all_gather(moments.reshape(-1, cols), "z", axis=0, tiled=True)
-
-    planes = gathered.reshape(Z, rows, cols)
-    plane_source = source.reshape(X, Z)[:, my_z]
-    src_x, src_z = plane_source // Z, plane_source % Z
-    to = [(my_x + shift) % X for shift in range(X)]
-    held = [lax.dynamic_index_in_dim(planes, src_z[i], 0, False) for i in to]
-    arrived = held[:1] + shifted(held[1:], X)
-    back = (my_x - src_x[my_x]) % X
-    moved_master = lax.select_n(back, *arrived)
+    piece = rows // (X * NEAR)
+    pieces = jnp.concatenate(
+        [item.astype(bf16).reshape(-1, piece, cols) for item in (new_one, new_two)], axis=1
+    )
+    pieces, received = lax.optimization_barrier((pieces, received))
+    pieces = compacted(plan, swap(pieces, ("x", "near")))
+    pieces = lax.all_gather(pieces.reshape(-1, cols), RING, axis=0, tiled=True)
+
+    held = pick_planes(plan, gathered.reshape(Z, rows, cols))
+    gathered, held = lax.optimization_barrier((gathered, held))
+    masters = [held[0]] + shifted(held[1:], X)
 
     weights = swap(gathered.reshape(Y * CORE, SHARE * rows, cols), DP)
+    weights, masters = lax.optimization_barrier((weights, masters))
+    moved = plan[MOVED] == 1
+    moved_master = lax.select_n(plan[BACK], *masters).astype(f32)
     weights = weights.reshape(Y * CORE, SHARE, rows, cols)
     hidden_units = cols // 3
     inputs = received.reshape(-1, SHARE, capacity, width)
@@ -138,32 +305,28 @@
     results = jnp.stack(outs, axis=1).reshape(received.shape)
     returned = swap(results, PLANE).reshape(-1, width)
     contract = (((0,), (0,)), ((), ()))
-    mixed = lax.dot_general(mix_high, returned, contract, preferred_element_type=f32)
-    mixed += lax.dot_general(mix_low, returned, contract, preferred_element_type=f32)
-    mixed = mixed.astype(bf16)
-
-    pieces = moments.reshape(Z, X, 2, quarter, cols)
-    held = [
-        lax.dynamic_slice(pieces, (src_z[i], src_x[i], 0, 0, 0), (1, 1, 2, quarter, cols))[0, 0]
-        for i in to
-    ]
-    arrived = jnp.stack(held[:1] + shifted(held[1:], X))
-    order = (my_x - jnp.arange(X, dtype=jnp.int32)) % X
-    arrived = jnp.take(arrived, order, axis=0)
-    moved_moments = arrived.transpose(1, 0, 2, 3).reshape(2, rows, cols)
-    moved = source[my_host] != my_host
+    mixed = lax.dot_general(mix_both, returned, contract, preferred_element_type=f32)
+    mixed = (mixed[:tok_count] + mixed[tok_count:]).astype(bf16)
+
+    held = pick_pieces(plan, pieces.reshape(Z // NEAR, NEAR, SLOTS, 2 * piece, cols))
+    moments = finished(plan, [held[0]] + shifted(held[1:], X), new_one, new_two)
+    moments = lax.cond(
+        plan[OVER] == 1,
+        lambda: relocated_whole(old_host, new_host, new_one, new_two),
+        lambda: list(moments),
+    )
     return (
-        jnp.where(moved, moved_master.astype(f32), new_master)[None],
-        jnp.where(moved, moved_moments[0].astype(f32), new_one)[None],
-        jnp.where(moved, moved_moments[1].astype(f32), new_two)[None],
+        jnp.where(moved, moved_master, new_master)[None],
+        moments[0][None],
+        moments[1][None],
         mixed,
     )
 
 
 def solution(mesh):
-    fine = Mesh(mesh.devices.reshape(Y, CORE, X, Z), ("y", "c", "x", "z"))
-    state = P(("x", "z"), DP, None)
-    rows = P(("y", "c", "x", "z"), None)
+    fine = Mesh(mesh.devices.reshape(Y, CORE, X, Z // NEAR, NEAR), PLANE + RING)
+    state = P(("x",) + RING, DP, None)
+    rows = P(PLANE + RING, None)
     return jax.shard_map(
         per_device,
         mesh=fine,

time: 282 us -> 286 us (1.014)
  waiting for transfers between devices: 126 us -> 145 us
  blocking collectives: 14.8 us -> 0 us
  between operations: 31.7 us -> 18.4 us
  Pallas kernels: 3.35 us -> 15.7 us
  starting transfers between devices: 67.4 us -> 72.7 us
    all_to_all x5 -> x6, waiting for transfers between devices: 101 us -> 133 us  [swap(): return lax.all_to_all(array, axes, split_axis=0, concat_axis=0, tiled=True)]
    all_to_all x1 -> x0, blocking collectives: 14.8 us -> none  [swap(): return lax.all_to_all(array, axes, split_axis=0, concat_axis=0, tiled=True)]
    pallas_call x0 -> x5, Pallas kernels: none -> 12.5 us  [the longest x1 3.13 us: pick_planes(): pl.pallas_call(copy_picked, out_shape=[jax.ShapeDtypeStruct((rows, cols),...]
    ppermute x6, waiting for transfers between devices: 21.7 us -> 12.1 us  [shifted(): lax.ppermute(block, 'x', [(i, (i + shift) % size) for i in range(size)])]
    all_gather x2, waiting for transfers between devices: 2.98 us -> 0.02 us  [the longest x1 0.02 us: per_device(): gathered = lax.all_gather(new_master.astype(bf16), RING, axis=0, tiled=True)]
    all_to_all x5 -> x6, starting transfers between devices: 48.2 us -> 51 us  [swap(): return lax.all_to_all(array, axes, split_axis=0, concat_axis=0, tiled=True)]
  transfers between devices with their start and end apart: 13 -> 14, of which waited for: 8 -> 10; matrix products, arithmetic and copies ran while one was open for 11% -> 10% of each run, Pallas kernels for 0% -> 3%
where the time goes in v3:
time: 286 us; the launch traced here: 285 us
  waiting for transfers between devices  145 us (51%)
  starting transfers between devices  72.7 us (25%)
  between operations  18.4 us (6%)
  Pallas kernels  15.7 us (5%)
  other arithmetic  13.5 us (5%)
  matrix products  10.7 us (4%)
  local copies, waits for them, and re-layouts  8.54 us (3%)
    all_to_all x6, waiting for transfers between devices, swap(): return lax.all_to_all(array, axes, split_axis=0, concat_axis=0, tiled=True)  133 us
    all_to_all x6, starting transfers between devices, swap(): return lax.all_to_all(array, axes, split_axis=0, concat_axis=0, tiled=True)  51 us
    ppermute x6, starting transfers between devices, shifted(): lax.ppermute(block, 'x', [(i, (i + shift) % size) for i in range(size)])  21.6 us
    ppermute x6, waiting for transfers between devices, shifted(): lax.ppermute(block, 'x', [(i, (i + shift) % size) for i in range(size)])  12.1 us
  transfers between devices with their start and end apart: 14, of which 10 were waited for; matrix products, arithmetic and copies ran while one was open for 10% of the time, Pallas kernels for 3%

profile of v3, /device:TPU:1, one launch (start us, length us, event | category | flops | bytes accessed | tf_op | source)
XLA Modules:
  0.0 285.0 jit_solution(9497709463405152214)
XLA Ops:
  7.2 1.9 shard_map.121
  9.1 10.4 %all-to-all-start.2 = ((f32[32,1,128]{2,1,0:T(1,128)}), f32[32,1,128]{2,1,0:T(1,128)S(1)}, u32[]{:S(2)}, u32[]{:S(2)}) async-start(f32[32,1,128]{2,1,0:T(1,128)} %shard_map.121), calls=%async_computation.2 | async-start | bytes 32768 | tf_op jit(solution)/shard_map/all_to_all | solution.py:36
  19.5 0.7 fusion.30
  20.1 0.8 select_reduce_fusion.2
  20.9 0.1 fusion.29
  21.0 0.1 convolution_select_fusion
  21.2 0.1 eq.86
  21.3 0.3 bitcast_compare_fusion
  21.5 4.9 %all-to-all-done.2.values = f32[32,1,128]{2,1,0:T(1,128)S(1)} async-done(((f32[32,1,128]{2,1,0:T(1,128)}), f32[32,1,128]{2,1,0:T(1,128)S(1)}, u32[]{:S(2)}, u32[]{:S(2)}) %all-to-all-start.2) | async-done | bytes 16416 | tf_op jit(solution)/shard_map/all_to_all | solution.py:36
  26.4 0.6 copy-done.14
  27.0 1.4 shard_map.122
  28.4 13.0 %all-to-all-start.3 = ((f32[16,1,128]{2,1,0:T(1,128)}), f32[16,1,128]{2,1,0:T(1,128)S(1)}, u32[]{:S(2)}, u32[]{:S(2)}) async-start(f32[16,1,128]{2,1,0:T(1,128)} %shard_map.122), calls=%async_computation.3 | async-start | bytes 16384 | tf_op jit(solution)/shard_map/all_to_all | solution.py:36
  41.4 0.0 all-gather.6.cloned.1.call-start
  41.5 2.6 convolution_convert_fusion
  44.1 8.5 %all-to-all-done.3 = f32[16,1,128]{2,1,0:T(1,128)S(1)} async-done(((f32[16,1,128]{2,1,0:T(1,128)}), f32[16,1,128]{2,1,0:T(1,128)S(1)}, u32[]{:S(2)}, u32[]{:S(2)}) %all-to-all-start.3) | async-done | bytes 8224 | tf_op jit(solution)/shard_map/all_to_all | solution.py:36
  52.6 0.6 slice_reduce_fusion
  54.0 1.6 fusion.34
  55.6 0.0 all-gather.6.cloned.1.call-update
  55.6 5.8 %all-to-all-start.5 = ((bf16[32,48,1024]{2,1,0:T(8,128)(2,1)}), bf16[32,48,1024]{2,1,0:T(8,128)(2,1)S(1)}, u32[]{:S(2)}, u32[]{:S(2)}) async-start(bf16[32,48,1024]{2,1,0:T(8,128)(2,1)} %bitcast.130), calls=%async_computation.5 | async-start | bytes 6291456 | tf_op jit(solution)/shard_map/all_to_all | solution.py:36
  61.4 1.5 fusion.23
  63.0 0.9 pad_maximum_fusion.2
  63.9 35.6 %all-to-all-done.5 = bf16[32,48,1024]{2,1,0:T(8,128)(2,1)S(1)} async-done(((bf16[32,48,1024]{2,1,0:T(8,128)(2,1)}), bf16[32,48,1024]{2,1,0:T(8,128)(2,1)S(1)}, u32[]{:S(2)}, u32[]{:S(2)}) %all-to-all-start.5) | async-done | bytes 3145760 | tf_op jit(solution)/shard_map/all_to_all | solution.py:36
  99.4 5.2 %all-to-all-start.6 = ((bf16[16,16,1152]{2,1,0:T(8,128)(2,1)}), bf16[16,16,1152]{2,1,0:T(8,128)(2,1)}, u32[]{:S(2)}, u32[]{:S(2)}) async-start(bf16[16,16,1152]{2,1,0:T(8,128)(2,1)} %pad_maximum_fusion.2), calls=%async_computation.6 | async-start | bytes 1179648 | tf_op jit(solution)/shard_map/all_to_all | solution.py:36
  104.7 0.0 all-gather.8.cloned.1.call-start
  104.7 2.9 %shard_map.120.plan = s32[32]{0:T(128)} custom-call(s32[64]{0:T(128)S(1)} %copy-done.19, s32[64]{0:T(128)S(1)} %copy-done.20), custom_call_target="tpu_custom_call" | custom-call | tf_op jit(solution)/shard_map/pallas_call | solution.py:99
  107.6 20.5 %all-to-all-done.6.pieces = bf16[16,16,1152]{2,1,0:T(8,128)(2,1)} async-done(((bf16[16,16,1152]{2,1,0:T(8,128)(2,1)}), bf16[16,16,1152]{2,1,0:T(8,128)(2,1)}, u32[]{:S(2)}, u32[]{:S(2)}) %all-to-all-start.6) | async-done | bytes 589856 | tf_op jit(solution)/shard_map/all_to_all | solution.py:36
  128.1 2.5 shard_map.124
  130.6 0.0 all-gather.6.cloned.1.call-done
  130.7 3.1 %shard_map.123 = (bf16[128,1152]{1,0:T(8,128)(2,1)}, bf16[128,1152]{1,0:T(8,128)(2,1)}, bf16[128,1152]{1,0:T(8,128)(2,1)}, bf16[128,1152]{1,0:T(8,128)(2,1)}) custom-call(s32[32]{0:T(128)} %shard_map.120.plan, bf16[16,128,1152]{2,1,0:T(8,128)(2,1)} %bitcast.120, bf16[16,128,1152]{2,1,0:T(8,128)(2,1)} %bitcast.121, bf16[16,128,1152]{2,1,0:T(8,128)(2,1)} %bitcast.122, ...), custom_call_target="tpu_custom_call" | custom-call | tf_op jit(solution)/shard_map/pallas_call | solution.py:120
  133.8 10.4 %all-to-all-start.4 = ((bf16[8,256,1152]{2,1,0:T(8,128)(2,1)}), bf16[8,256,1152]{2,1,0:T(8,128)(2,1)}, u32[]{:S(2)}, u32[]{:S(2)}) async-start(bf16[8,256,1152]{2,1,0:T(8,128)(2,1)} %bitcast.124), calls=%async_computation.4 | async-start | bytes 9437184 | tf_op jit(solution)/shard_map/all_to_all | solution.py:36
  144.2 3.3 %collective-permute-start = (bf16[128,1152]{1,0:T(8,128)(2,1)}, bf16[128,1152]{1,0:T(8,128)(2,1)}, u32[]{:S(2)}, u32[]{:S(2)}) collective-permute-start(bf16[128,1152]{1,0:T(8,128)(2,1)} %get-tuple-element.63), channel_id=1, source_target_pairs={{0,16},{16,32},{32,48},{48,0},{1,17},{17,33},{33,49},{49,1},{2,18}... | collective-permute-start | bytes 884744 | tf_op jit(solution)/shard_map/ppermute | solution.py:222
  147.5 4.2 %collective-permute-start.1 = (bf16[128,1152]{1,0:T(8,128)(2,1)}, bf16[128,1152]{1,0:T(8,128)(2,1)}, u32[]{:S(2)}, u32[]{:S(2)}) collective-permute-start(bf16[128,1152]{1,0:T(8,128)(2,1)} %get-tuple-element.64), channel_id=1, source_target_pairs={{0,32},{16,48},{32,0},{48,16},{1,33},{17,49},{33,1},{49,17},{2,34}... | collective-permute-start | bytes 884744 | tf_op jit(solution)/shard_map/ppermute | solution.py:222
  151.7 3.2 %collective-permute-start.2 = (bf16[128,1152]{1,0:T(8,128)(2,1)}, bf16[128,1152]{1,0:T(8,128)(2,1)}, u32[]{:S(2)}, u32[]{:S(2)}) collective-permute-start(bf16[128,1152]{1,0:T(8,128)(2,1)} %get-tuple-element.65), channel_id=1, source_target_pairs={{0,48},{16,0},{32,16},{48,32},{1,49},{17,1},{33,17},{49,33},{2,50}... | collective-permute-start | bytes 884744 | tf_op jit(solution)/shard_map/ppermute | solution.py:222
  154.9 2.0 fusion.40
  156.9 6.5 %collective-permute-done.1 = bf16[128,1152]{1,0:T(8,128)(2,1)} collective-permute-done((bf16[128,1152]{1,0:T(8,128)(2,1)}, bf16[128,1152]{1,0:T(8,128)(2,1)}, u32[]{:S(2)}, u32[]{:S(2)}) %collective-permute-start.1) | collective-permute-done | bytes 294944 | tf_op jit(solution)/shard_map/ppermute | solution.py:222
  163.4 1.2 collective-permute-done.2
  164.6 34.2 %all-to-all-done.4 = bf16[8,256,1152]{2,1,0:T(8,128)(2,1)} async-done(((bf16[8,256,1152]{2,1,0:T(8,128)(2,1)}), bf16[8,256,1152]{2,1,0:T(8,128)(2,1)}, u32[]{:S(2)}, u32[]{:S(2)}) %all-to-all-start.4) | async-done | bytes 4718624 | tf_op jit(solution)/shard_map/all_to_all | solution.py:36
  198.8 2.9 %fusion.39 = (bf16[8,1,128,1152]{3,2,1,0:T(8,128)(2,1)S(1)}, bf16[8,1,128,1152]{3,2,1,0:T(8,128)(2,1)S(1)}) fusion(bf16[8,2,128,1152]{3,2,1,0:T(8,128)(2,1)} %bitcast.49), kind=kLoop, calls=%fused_computation.90 | loop fusion | bytes 9437184 | tf_op jit(solution)/shard_map/slice | solution.py:294
  201.7 1.4 fusion.4
  203.1 1.0 convolution_convert_fusion.2
  204.2 0.4 copy-done.7
  204.5 1.4 fusion.2
  205.9 1.0 convolution_convert_fusion.1
  207.0 2.0 pad_maximum_fusion.1
  209.0 6.1 %all-to-all-start.7 = ((bf16[32,48,1024]{2,1,0:T(8,128)(2,1)}), bf16[32,48,1024]{2,1,0:T(8,128)(2,1)S(1)}, u32[]{:S(2)}, u32[]{:S(2)}) async-start(bf16[32,48,1024]{2,1,0:T(8,128)(2,1)} %bitcast.57), calls=%async_computation.7 | async-start | bytes 6291456 | tf_op jit(solution)/shard_map/all_to_all | solution.py:36
  215.1 0.1 select_reduce_fusion.1
  215.2 1.0 fusion.15
  216.2 1.0 fusion.16
  217.3 0.6 fusion.41
  221.1 2.1 select_bitcast_fusion
  223.3 29.7 %all-to-all-done.7 = bf16[32,48,1024]{2,1,0:T(8,128)(2,1)S(1)} async-done(((bf16[32,48,1024]{2,1,0:T(8,128)(2,1)}), bf16[32,48,1024]{2,1,0:T(8,128)(2,1)S(1)}, u32[]{:S(2)}, u32[]{:S(2)}) %all-to-all-start.7) | async-done | bytes 3145760 | tf_op jit(solution)/shard_map/all_to_all | solution.py:36
  253.0 3.1 %fusion.10 = f32[256,1024]{1,0:T(8,128)} fusion(bf16[1536,1024]{1,0:T(8,128)(2,1)S(1)} %bitcast.131, bf16[1536,128]{1,0:T(8,128)(2,1)} %fusion.16, bf16[1536,128]{1,0:T(8,128)(2,1)} %fusion.15), kind=kOutput, calls=%fused_computation.35 | convolution fusion | flops 806879232 | bytes 4980736 | tf_op jit(solution)/shard_map/dot_general | solution.py:308
  256.1 2.7 shard_map.125
  258.9 3.9 %collective-permute-start.3 = (bf16[4,16,1152]{2,1,0:T(8,128)(2,1)}, bf16[4,16,1152]{2,1,0:T(8,128)(2,1)S(1)}, u32[]{:S(2)}, u32[]{:S(2)}) collective-permute-start(bf16[4,16,1152]{2,1,0:T(8,128)(2,1)} %get-tuple-element.73), channel_id=1, source_target_pairs={{0,16},{16,32},{32,48},{48,0},{1,17},{17,33},{33,49},{49,1},{2,18}... | collective-permute-start | bytes 442376 | tf_op jit(solution)/shard_map/ppermute | solution.py:222
  262.7 4.9 %collective-permute-start.4 = (bf16[4,16,1152]{2,1,0:T(8,128)(2,1)}, bf16[4,16,1152]{2,1,0:T(8,128)(2,1)S(1)}, u32[]{:S(2)}, u32[]{:S(2)}) collective-permute-start(bf16[4,16,1152]{2,1,0:T(8,128)(2,1)} %get-tuple-element.74), channel_id=1, source_target_pairs={{0,32},{16,48},{32,0},{48,16},{1,33},{17,49},{33,1},{49,17},{2,34}... | collective-permute-start | bytes 442376 | tf_op jit(solution)/shard_map/ppermute | solution.py:222
  267.7 2.2 collective-permute-start.5
  269.9 0.8 fusion.28
  270.6 1.7 collective-permute-done.4.two
  272.3 2.7 collective-permute-done.5.three
  275.0 0.6 copy-done.13
  275.7 1.2 shard_map.126
  277.0 0.8 copy-done.17
  277.7 0.2 copy-done.18
  277.9 0.2 copy-done.1
  (43 shorter events, 0.1 us)
Async XLA Ops:
  7.2 34.3 %copy-start = (bf16[128,1024]{1,0:T(8,128)(2,1)S(1)}, bf16[128,1024]{1,0:T(8,128)(2,1)}, u32[]{:S(2)}) copy-start(bf16[128,1024]{1,0:T(8,128)(2,1)} %param.17) | copy-start | bytes 786436
  9.1 17.3 %all-to-all-start.2 = ((f32[32,1,128]{2,1,0:T(1,128)}), f32[32,1,128]{2,1,0:T(1,128)S(1)}, u32[]{:S(2)}, u32[]{:S(2)}) async-start(f32[32,1,128]{2,1,0:T(1,128)} %shard_map.121), calls=%async_computation.2 | async-start | bytes 32768 | tf_op jit(solution)/shard_map/all_to_all | solution.py:36
  26.4 0.6 copy-start.14
  28.4 24.3 %all-to-all-start.3 = ((f32[16,1,128]{2,1,0:T(1,128)}), f32[16,1,128]{2,1,0:T(1,128)S(1)}, u32[]{:S(2)}, u32[]{:S(2)}) async-start(f32[16,1,128]{2,1,0:T(1,128)} %shard_map.122), calls=%async_computation.3 | async-start | bytes 16384 | tf_op jit(solution)/shard_map/all_to_all | solution.py:36
  41.4 12.6 %copy-start.4 = (bf16[1,128,1152]{2,1,0:T(8,128)(2,1)S(1)}, bf16[1,128,1152]{2,1,0:T(8,128)(2,1)}, u32[]{:S(2)}) copy-start(bf16[1,128,1152]{2,1,0:T(8,128)(2,1)} %param.14) | copy-start | bytes 884740
  41.4 12.6 %copy-start.5 = (f32[1,128,1152]{2,1,0:T(8,128)S(1)}, f32[1,128,1152]{2,1,0:T(8,128)}, u32[]{:S(2)}) copy-start(f32[1,128,1152]{2,1,0:T(8,128)} %param.12) | copy-start | bytes 1769476
  41.4 12.6 %copy-start.6 = (f32[1,128,1152]{2,1,0:T(8,128)S(1)}, f32[1,128,1152]{2,1,0:T(8,128)}, u32[]{:S(2)}) copy-start(f32[1,128,1152]{2,1,0:T(8,128)} %param.13) | copy-start | bytes 1769476
  41.4 12.6 %copy-start.10 = (f32[1,128,1152]{2,1,0:T(8,128)S(1)}, f32[1,128,1152]{2,1,0:T(8,128)}, u32[]{:S(2)}) copy-start(f32[1,128,1152]{2,1,0:T(8,128)} %param.11) | copy-start | bytes 1769476
  41.4 89.2 %all-gather.6.cloned.1.call-start = ((), (), s32[]{:S(2)}) async-start(), calls=%async_computation.9 | async-start | bytes 5013504 | tf_op jit(solution)/shard_map/all_gather | solution.py:271
  55.6 43.8 %all-to-all-start.5 = ((bf16[32,48,1024]{2,1,0:T(8,128)(2,1)}), bf16[32,48,1024]{2,1,0:T(8,128)(2,1)S(1)}, u32[]{:S(2)}, u32[]{:S(2)}) async-start(bf16[32,48,1024]{2,1,0:T(8,128)(2,1)} %bitcast.130), calls=%async_computation.5 | async-start | bytes 6291456 | tf_op jit(solution)/shard_map/all_to_all | solution.py:36
  63.0 41.7 %copy-start.19 = (s32[64]{0:T(128)S(1)}, s32[64]{0:T(128)}, u32[]{:S(2)}) copy-start(s32[64]{0:T(128)} %old_host.1) | copy-start | bytes 772
  63.0 41.7 %copy-start.20 = (s32[64]{0:T(128)S(1)}, s32[64]{0:T(128)}, u32[]{:S(2)}) copy-start(s32[64]{0:T(128)} %new_host.1) | copy-start | bytes 772
  99.4 28.7 %all-to-all-start.6 = ((bf16[16,16,1152]{2,1,0:T(8,128)(2,1)}), bf16[16,16,1152]{2,1,0:T(8,128)(2,1)}, u32[]{:S(2)}, u32[]{:S(2)}) async-start(bf16[16,16,1152]{2,1,0:T(8,128)(2,1)} %pad_maximum_fusion.2), calls=%async_computation.6 | async-start | bytes 1179648 | tf_op jit(solution)/shard_map/all_to_all | solution.py:36
  104.7 151.5 %all-gather.8.cloned.1.call-start = ((), (), s32[]{:S(2)}) async-start(), calls=%async_computation.10 | async-start | bytes 6266880 | tf_op jit(solution)/shard_map/all_gather | solution.py:279
  133.8 65.0 %all-to-all-start.4 = ((bf16[8,256,1152]{2,1,0:T(8,128)(2,1)}), bf16[8,256,1152]{2,1,0:T(8,128)(2,1)}, u32[]{:S(2)}, u32[]{:S(2)}) async-start(bf16[8,256,1152]{2,1,0:T(8,128)(2,1)} %bitcast.124), calls=%async_computation.4 | async-start | bytes 9437184 | tf_op jit(solution)/shard_map/all_to_all | solution.py:36
  144.2 12.7 %collective-permute-start = (bf16[128,1152]{1,0:T(8,128)(2,1)}, bf16[128,1152]{1,0:T(8,128)(2,1)}, u32[]{:S(2)}, u32[]{:S(2)}) collective-permute-start(bf16[128,1152]{1,0:T(8,128)(2,1)} %get-tuple-element.63), channel_id=1, source_target_pairs={{0,16},{16,32},{32,48},{48,0},{1,17},{17,33},{33,49},{49,1},{2,18}... | collective-permute-start | bytes 884744 | tf_op jit(solution)/shard_map/ppermute | solution.py:222
  147.5 15.9 %collective-permute-start.1 = (bf16[128,1152]{1,0:T(8,128)(2,1)}, bf16[128,1152]{1,0:T(8,128)(2,1)}, u32[]{:S(2)}, u32[]{:S(2)}) collective-permute-start(bf16[128,1152]{1,0:T(8,128)(2,1)} %get-tuple-element.64), channel_id=1, source_target_pairs={{0,32},{16,48},{32,0},{48,16},{1,33},{17,49},{33,1},{49,17},{2,34}... | collective-permute-start | bytes 884744 | tf_op jit(solution)/shard_map/ppermute | solution.py:222
  151.7 12.9 %collective-permute-start.2 = (bf16[128,1152]{1,0:T(8,128)(2,1)}, bf16[128,1152]{1,0:T(8,128)(2,1)}, u32[]{:S(2)}, u32[]{:S(2)}) collective-permute-start(bf16[128,1152]{1,0:T(8,128)(2,1)} %get-tuple-element.65), channel_id=1, source_target_pairs={{0,48},{16,0},{32,16},{48,32},{1,49},{17,1},{33,17},{49,33},{2,50}... | collective-permute-start | bytes 884744 | tf_op jit(solution)/shard_map/ppermute | solution.py:222
  198.8 2.9 %copy-start.8 = (bf16[32,1,24,1024]{3,2,1,0:T(8,128)(2,1)S(1)}, bf16[32,1,24,1024]{3,2,1,0:T(8,128)(2,1)}, u32[]{:S(2)}) copy-start(bf16[32,1,24,1024]{3,2,1,0:T(8,128)(2,1)} %get-tuple-element.108) | copy-start | bytes 4718596
  203.1 1.4 copy-start.7
  209.0 6.2 %copy-start.16 = (f32[128,8]{0,1:T(8,128)S(1)}, f32[128,8]{0,1:T(8,128)}, u32[]{:S(2)}) copy-start(f32[128,8]{0,1:T(8,128)} %param.19) | copy-start | bytes 12292
  209.0 8.3 %copy-start.15 = (s32[32]{0:T(128)S(1)}, s32[32]{0:T(128)}, u32[]{:S(2)}) copy-start(s32[32]{0:T(128)} %shard_map.120.plan) | copy-start | bytes 388
  209.0 44.1 %all-to-all-start.7 = ((bf16[32,48,1024]{2,1,0:T(8,128)(2,1)}), bf16[32,48,1024]{2,1,0:T(8,128)(2,1)S(1)}, u32[]{:S(2)}, u32[]{:S(2)}) async-start(bf16[32,48,1024]{2,1,0:T(8,128)(2,1)} %bitcast.57), calls=%async_computation.7 | async-start | bytes 6291456 | tf_op jit(solution)/shard_map/all_to_all | solution.py:36
  256.1 13.7 %copy-start.9 = (f32[256,1024]{1,0:T(8,128)S(1)}, f32[256,1024]{1,0:T(8,128)}, u32[]{:S(2)}) copy-start(f32[256,1024]{1,0:T(8,128)} %fusion.10) | copy-start | bytes 3145732
  258.9 16.8 %copy-start.2 = (f32[128,1152]{1,0:T(8,128)S(1)}, f32[128,1152]{1,0:T(8,128)}, u32[]{:S(2)}) copy-start(f32[128,1152]{1,0:T(8,128)} %get-tuple-element.86.own_one) | copy-start | bytes 1769476
  258.9 16.8 %copy-start.3 = (f32[128,1152]{1,0:T(8,128)S(1)}, f32[128,1152]{1,0:T(8,128)}, u32[]{:S(2)}) copy-start(f32[128,1152]{1,0:T(8,128)} %get-tuple-element.87.own_two) | copy-start | bytes 1769476
  258.9 11.8 %collective-permute-start.3 = (bf16[4,16,1152]{2,1,0:T(8,128)(2,1)}, bf16[4,16,1152]{2,1,0:T(8,128)(2,1)S(1)}, u32[]{:S(2)}, u32[]{:S(2)}) collective-permute-start(bf16[4,16,1152]{2,1,0:T(8,128)(2,1)} %get-tuple-element.73), channel_id=1, source_target_pairs={{0,16},{16,32},{32,48},{48,0},{1,17},{17,33},{33,49},{49,1},{2,18}... | collective-permute-start | bytes 442376 | tf_op jit(solution)/shard_map/ppermute | solution.py:222
  262.7 9.6 %collective-permute-start.4 = (bf16[4,16,1152]{2,1,0:T(8,128)(2,1)}, bf16[4,16,1152]{2,1,0:T(8,128)(2,1)S(1)}, u32[]{:S(2)}, u32[]{:S(2)}) collective-permute-start(bf16[4,16,1152]{2,1,0:T(8,128)(2,1)} %get-tuple-element.74), channel_id=1, source_target_pairs={{0,32},{16,48},{32,0},{48,16},{1,33},{17,49},{33,1},{49,17},{2,34}... | collective-permute-start | bytes 442376 | tf_op jit(solution)/shard_map/ppermute | solution.py:222
  267.7 7.4 %collective-permute-start.5 = (bf16[4,16,1152]{2,1,0:T(8,128)(2,1)}, bf16[4,16,1152]{2,1,0:T(8,128)(2,1)S(1)}, u32[]{:S(2)}, u32[]{:S(2)}) collective-permute-start(bf16[4,16,1152]{2,1,0:T(8,128)(2,1)} %get-tuple-element.75), channel_id=1, source_target_pairs={{0,48},{16,0},{32,16},{48,32},{1,49},{17,1},{33,17},{49,33},{2,50}... | collective-permute-start | bytes 442376 | tf_op jit(solution)/shard_map/ppermute | solution.py:222
  270.6 4.4 %copy-start.11 = (bf16[4,16,1152]{2,1,0:T(8,128)(2,1)}, bf16[4,16,1152]{2,1,0:T(8,128)(2,1)S(1)}, u32[]{:S(2)}) copy-start(bf16[4,16,1152]{2,1,0:T(8,128)(2,1)S(1)} %collective-permute-done.3.one) | copy-start | bytes 442372
  272.3 2.7 copy-start.12
  275.0 0.7 copy-start.13
  276.9 0.8 copy-start.17
  276.9 1.0 copy-start.18
  277.0 1.2 copy-start.1
Sparse Core Ops, SparseCore 0:
  55.8 72.1 all-gather.5
  130.8 83.4 all-gather.7

commit v4 on v3

--- a/solution.py
+++ b/solution.py
@@ -13,8 +13,8 @@
 step_count = 10
 
 Y, CORE, X, Z = 4, 2, 4, 16
-NEAR = 4
-SLOTS = 10
+NEAR = 2
+SLOTS = 6
 DP = ("y", "c")
 PLANE = ("y", "c", "x")
 RING = ("far", "near")
@@ -215,6 +215,40 @@
         jnp.where(moved, arrived[0].astype(f32), own_one),
         jnp.where(moved, arrived[1].astype(f32), own_two),
     ]
+
+
+def expert_layer(rows, weights, outs):
+    weight = weights[...].reshape(-1, weights.shape[-1])
+    units = weight.shape[1] // 3
+    projected = jnp.dot(rows[0], weight[:, : 2 * units], preferred_element_type=f32)
+    hidden = (jax.nn.silu(projected[:, :units]) * projected[:, units:]).astype(bf16)
+    produced = lax.dot_general(
+        hidden, weight[:, 2 * units :], (((1,), (1,)), ((), ())), preferred_element_type=f32
+    )
+    outs[...] = produced.reshape(outs.shape).astype(bf16)
+
+
+def experts(rows, weights, capacity):
+    shares, row_count, width = rows.shape
+    shards, _, shard_rows, cols = weights.shape
+    parts = 2
+    part = row_count // parts
+    return pl.pallas_call(
+        expert_layer,
+        out_shape=jax.ShapeDtypeStruct((row_count // capacity, shares, capacity, width), bf16),
+        grid=(shares, parts),
+        in_specs=[
+            pl.BlockSpec((1, part, width), lambda j, i: (j, i, 0)),
+            pl.BlockSpec((shards, 1, shard_rows, cols), lambda j, i: (0, j, 0, 0)),
+        ],
+        out_specs=pl.BlockSpec((part // capacity, 1, capacity, width), lambda j, i: (i, j, 0, 0)),
+        compiler_params=pltpu.CompilerParams(vmem_limit_bytes=48 * 2**20),
+        cost_estimate=pl.CostEstimate(
+            flops=2 * shares * row_count * width * cols,
+            bytes_accessed=2 * (weights.size + 2 * rows.size),
+            transcendentals=shares * row_count * cols // 3,
+        ),
+    )(rows, weights)
 
 
 def shifted(blocks, size):
@@ -279,7 +313,6 @@
     pieces = lax.all_gather(pieces.reshape(-1, cols), RING, axis=0, tiled=True)
 
     held = pick_planes(plan, gathered.reshape(Z, rows, cols))
-    gathered, held = lax.optimization_barrier((gathered, held))
     masters = [held[0]] + shifted(held[1:], X)
 
     weights = swap(gathered.reshape(Y * CORE, SHARE * rows, cols), DP)
@@ -287,34 +320,23 @@
     moved = plan[MOVED] == 1
     moved_master = lax.select_n(plan[BACK], *masters).astype(f32)
     weights = weights.reshape(Y * CORE, SHARE, rows, cols)
-    hidden_units = cols // 3
-    inputs = received.reshape(-1, SHARE, capacity, width)
-    outs = []
-    for j in range(SHARE):
-        weight = weights[:, j].reshape(-1, cols)
-        rows_in = inputs[:, j].reshape(-1, width)
-        projected = jnp.dot(rows_in, weight[:, : 2 * hidden_units], preferred_element_type=f32)
-        hidden = (jax.nn.silu(projected[:, :hidden_units]) * projected[:, hidden_units:]).astype(bf16)
-        produced = lax.dot_general(
-            hidden,
-            weight[:, 2 * hidden_units :],
-            (((1,), (1,)), ((), ())),
-            preferred_element_type=f32,
-        )
-        outs.append(produced.astype(bf16).reshape(-1, capacity, width))
-    results = jnp.stack(outs, axis=1).reshape(received.shape)
+    inputs = received.reshape(-1, SHARE, capacity, width).transpose(1, 0, 2, 3)
+    results = experts(inputs.reshape(SHARE, -1, width), weights, capacity).reshape(received.shape)
+    results, late_plan = lax.optimization_barrier((results, plan))
     returned = swap(results, PLANE).reshape(-1, width)
+
+    held = pick_pieces(late_plan, pieces.reshape(Z // NEAR, NEAR, SLOTS, 2 * piece, cols))
+    moments = finished(plan, [held[0]] + shifted(held[1:], X), new_one, new_two)
+    returned, moments = lax.optimization_barrier((returned, list(moments)))
+    moments = lax.cond(
+        plan[OVER] == 1,
+        lambda: relocated_whole(old_host, new_host, new_one, new_two),
+        lambda: moments,
+    )
+
     contract = (((0,), (0,)), ((), ()))
     mixed = lax.dot_general(mix_both, returned, contract, preferred_element_type=f32)
     mixed = (mixed[:tok_count] + mixed[tok_count:]).astype(bf16)
-
-    held = pick_pieces(plan, pieces.reshape(Z // NEAR, NEAR, SLOTS, 2 * piece, cols))
-    moments = finished(plan, [held[0]] + shifted(held[1:], X), new_one, new_two)
-    moments = lax.cond(
-        plan[OVER] == 1,
-        lambda: relocated_whole(old_host, new_host, new_one, new_two),
-        lambda: list(moments),
-    )
     return (
         jnp.where(moved, moved_master, new_master)[None],
         moments[0][None],

time: 286 us -> 267 us (0.934)
  waiting for transfers between devices: 145 us -> 126 us
  Pallas kernels: 15.7 us -> 26.8 us
  matrix products: 10.7 us -> 5.68 us
  local copies, waits for them, and re-layouts: 8.54 us -> 4.94 us
    all_to_all x6, waiting for transfers between devices: 133 us -> 92.5 us  [swap(): return lax.all_to_all(array, axes, split_axis=0, concat_axis=0, tiled=True)]
    all_gather x1, waiting for transfers between devices: 0.01 us -> 10.5 us  [per_device(): pieces = lax.all_gather(pieces.reshape(-1, cols), RING, axis=0, tiled=True)]
    ppermute x6, waiting for transfers between devices: 12.1 us -> 22.6 us  [shifted(): lax.ppermute(block, 'x', [(i, (i + shift) % size) for i in range(size)])]
    pallas_call x0 -> x1, Pallas kernels: none -> 10.1 us  [experts(): pl.pallas_call(expert_layer, out_shape=jax.ShapeDtypeStruct((row_count //...]
    slice x2 -> x0, local copies, waits for them, and re-layouts: 4.95 us -> none  [the longest x1 2.92 us: per_device(): weight = weights[:, j].reshape(-1, cols)]
    dot_general x4 -> x0, matrix products: 4.83 us -> none  [the longest x2 2.77 us: per_device(): jnp.dot(rows_in, weight[:, :2 * hidden_units], preferred_element_type=f32)]
    mul x0 -> x3, other arithmetic: none -> 3.25 us  [the longest x1 1.13 us: adamw(): new_two = beta_two * moment_two + (1.0 - beta_two) * scaled * scaled]
  transfers between devices with their start and end apart: 14 -> 14, of which waited for: 10 -> 10; matrix products, arithmetic and copies ran while one was open for 10% -> 5% of each run, Pallas kernels for 3% -> 9%
where the time goes in v4:
time: 267 us; the launch traced here: 265 us
  waiting for transfers between devices  126 us (47%)
  starting transfers between devices  72.3 us (27%)
  Pallas kernels  26.8 us (10%)
  between operations  18.4 us (7%)
  other arithmetic  11.6 us (4%)
  matrix products  5.68 us (2%)
  local copies, waits for them, and re-layouts  4.94 us (2%)
    all_to_all x6, waiting for transfers between devices, swap(): return lax.all_to_all(array, axes, split_axis=0, concat_axis=0, tiled=True)  92.5 us
    all_to_all x6, starting transfers between devices, swap(): return lax.all_to_all(array, axes, split_axis=0, concat_axis=0, tiled=True)  51.2 us
    ppermute x6, waiting for transfers between devices, shifted(): lax.ppermute(block, 'x', [(i, (i + shift) % size) for i in range(size)])  22.6 us
    ppermute x6, starting transfers between devices, shifted(): lax.ppermute(block, 'x', [(i, (i + shift) % size) for i in range(size)])  21.1 us
    all_gather x1, waiting for transfers between devices, per_device(): pieces = lax.all_gather(pieces.reshape(-1, cols), RING, axis=0, tiled=True)  10.5 us
    pallas_call x1, Pallas kernels, experts(): pl.pallas_call(expert_layer, out_shape=jax.ShapeDtypeStruct((row_count //...  10.1 us
  transfers between devices with their start and end apart: 14, of which 10 were waited for; matrix products, arithmetic and copies ran while one was open for 5% of the time, Pallas kernels for 9%

profile of v4, /device:TPU:1, one launch (start us, length us, event | category | flops | bytes accessed | tf_op | source)
XLA Modules:
  0.0 265.3 jit_solution(9163613848959994563)
XLA Ops:
  7.2 0.0 copy-start
  7.2 0.0 copy-start.3
  7.2 2.0 shard_map.121
  9.2 10.4 %all-to-all-start.2 = ((f32[32,1,128]{2,1,0:T(1,128)}), f32[32,1,128]{2,1,0:T(1,128)S(1)}, u32[]{:S(2)}, u32[]{:S(2)}) async-start(f32[32,1,128]{2,1,0:T(1,128)} %shard_map.121), calls=%async_computation.2 | async-start | bytes 32768 | tf_op jit(solution)/shard_map/all_to_all | solution.py:36
  19.6 0.7 fusion.16
  20.3 0.8 select_reduce_fusion.2
  21.1 0.1 fusion.15
  21.2 0.1 convolution_select_fusion
  21.3 0.1 eq.86
  21.4 0.3 bitcast_compare_fusion
  21.7 4.9 %all-to-all-done.2.values = f32[32,1,128]{2,1,0:T(1,128)S(1)} async-done(((f32[32,1,128]{2,1,0:T(1,128)}), f32[32,1,128]{2,1,0:T(1,128)S(1)}, u32[]{:S(2)}, u32[]{:S(2)}) %all-to-all-start.2) | async-done | bytes 16416 | tf_op jit(solution)/shard_map/all_to_all | solution.py:36
  26.5 0.6 copy-done.12
  27.2 1.4 shard_map.122
  28.5 13.0 %all-to-all-start.3 = ((f32[16,1,128]{2,1,0:T(1,128)}), f32[16,1,128]{2,1,0:T(1,128)S(1)}, u32[]{:S(2)}, u32[]{:S(2)}) async-start(f32[16,1,128]{2,1,0:T(1,128)} %shard_map.122), calls=%async_computation.3 | async-start | bytes 16384 | tf_op jit(solution)/shard_map/all_to_all | solution.py:36
  41.5 0.0 all-gather.6.cloned.1.call-start
  41.6 2.6 convolution_convert_fusion
  44.2 8.5 %all-to-all-done.3 = f32[16,1,128]{2,1,0:T(1,128)S(1)} async-done(((f32[16,1,128]{2,1,0:T(1,128)}), f32[16,1,128]{2,1,0:T(1,128)S(1)}, u32[]{:S(2)}, u32[]{:S(2)}) %all-to-all-start.3) | async-done | bytes 8224 | tf_op jit(solution)/shard_map/all_to_all | solution.py:36
  52.8 0.6 slice_reduce_fusion
  54.2 1.6 fusion.18
  55.8 0.0 all-gather.6.cloned.1.call-update
  55.8 5.8 %all-to-all-start.5 = ((bf16[32,48,1024]{2,1,0:T(8,128)(2,1)}), bf16[32,48,1024]{2,1,0:T(8,128)(2,1)S(1)}, u32[]{:S(2)}, u32[]{:S(2)}) async-start(bf16[32,48,1024]{2,1,0:T(8,128)(2,1)} %bitcast.113), calls=%async_computation.5 | async-start | bytes 6291456 | tf_op jit(solution)/shard_map/all_to_all | solution.py:36
  61.6 1.1 broadcast_multiply_fusion.1
  62.7 0.0 copy-start.16
  62.8 1.1 broadcast_multiply_fusion
  63.9 1.0 convert_multiply_fusion
  64.9 0.1 add_convert_fusion
  65.0 0.9 pad_maximum_fusion.1
  65.9 33.7 %all-to-all-done.5 = bf16[32,48,1024]{2,1,0:T(8,128)(2,1)S(1)} async-done(((bf16[32,48,1024]{2,1,0:T(8,128)(2,1)}), bf16[32,48,1024]{2,1,0:T(8,128)(2,1)S(1)}, u32[]{:S(2)}, u32[]{:S(2)}) %all-to-all-start.5) | async-done | bytes 3145760 | tf_op jit(solution)/shard_map/all_to_all | solution.py:36
  99.6 5.0 %all-to-all-start.7 = ((bf16[8,32,1152]{2,1,0:T(8,128)(2,1)}), bf16[8,32,1152]{2,1,0:T(8,128)(2,1)}, u32[]{:S(2)}, u32[]{:S(2)}) async-start(bf16[8,32,1152]{2,1,0:T(8,128)(2,1)} %pad_maximum_fusion.1), calls=%async_computation.7 | async-start | bytes 1179648 | tf_op jit(solution)/shard_map/all_to_all | solution.py:36
  104.6 0.0 all-gather.8.cloned.1.call-start
  104.7 2.9 %shard_map.120.plan = s32[32]{0:T(128)} custom-call(s32[64]{0:T(128)S(1)} %copy-done.16, s32[64]{0:T(128)S(1)} %copy-done.18), custom_call_target="tpu_custom_call" | custom-call | tf_op jit(solution)/shard_map/pallas_call | solution.py:99
  107.6 14.4 %all-to-all-done.7.pieces = bf16[8,32,1152]{2,1,0:T(8,128)(2,1)} async-done(((bf16[8,32,1152]{2,1,0:T(8,128)(2,1)}), bf16[8,32,1152]{2,1,0:T(8,128)(2,1)}, u32[]{:S(2)}, u32[]{:S(2)}) %all-to-all-start.7) | async-done | bytes 589856 | tf_op jit(solution)/shard_map/all_to_all | solution.py:36
  122.0 2.5 shard_map.125
  124.6 0.0 all-gather.8.cloned.1.call-update
  124.6 0.0 all-gather.6.cloned.1.call-done
  124.6 10.7 %all-to-all-start.4 = ((bf16[8,256,1152]{2,1,0:T(8,128)(2,1)}), bf16[8,256,1152]{2,1,0:T(8,128)(2,1)}, u32[]{:S(2)}, u32[]{:S(2)}) async-start(bf16[8,256,1152]{2,1,0:T(8,128)(2,1)} %bitcast.103), calls=%async_computation.4 | async-start | bytes 9437184 | tf_op jit(solution)/shard_map/all_to_all | solution.py:36
  135.3 3.2 %shard_map.123 = (bf16[128,1152]{1,0:T(8,128)(2,1)}, bf16[128,1152]{1,0:T(8,128)(2,1)}, bf16[128,1152]{1,0:T(8,128)(2,1)}, bf16[128,1152]{1,0:T(8,128)(2,1)}) custom-call(s32[32]{0:T(128)} %shard_map.120.plan, bf16[16,128,1152]{2,1,0:T(8,128)(2,1)} %bitcast.104, bf16[16,128,1152]{2,1,0:T(8,128)(2,1)} %bitcast.105, bf16[16,128,1152]{2,1,0:T(8,128)(2,1)} %bitcast.106, ...), custom_call_target="tpu_custom_call" | custom-call | tf_op jit(solution)/shard_map/pallas_call | solution.py:120
  138.5 3.2 %collective-permute-start = (bf16[128,1152]{1,0:T(8,128)(2,1)}, bf16[128,1152]{1,0:T(8,128)(2,1)}, u32[]{:S(2)}, u32[]{:S(2)}) collective-permute-start(bf16[128,1152]{1,0:T(8,128)(2,1)} %get-tuple-element.60), channel_id=1, source_target_pairs={{0,16},{16,32},{32,48},{48,0},{1,17},{17,33},{33,49},{49,1},{2,18}... | collective-permute-start | bytes 884744 | tf_op jit(solution)/shard_map/ppermute | solution.py:256
  141.6 4.3 %collective-permute-start.1 = (bf16[128,1152]{1,0:T(8,128)(2,1)}, bf16[128,1152]{1,0:T(8,128)(2,1)}, u32[]{:S(2)}, u32[]{:S(2)}) collective-permute-start(bf16[128,1152]{1,0:T(8,128)(2,1)} %get-tuple-element.61), channel_id=1, source_target_pairs={{0,32},{16,48},{32,0},{48,16},{1,33},{17,49},{33,1},{49,17},{2,34}... | collective-permute-start | bytes 884744 | tf_op jit(solution)/shard_map/ppermute | solution.py:256
  146.0 3.2 %collective-permute-start.2 = (bf16[128,1152]{1,0:T(8,128)(2,1)}, bf16[128,1152]{1,0:T(8,128)(2,1)}, u32[]{:S(2)}, u32[]{:S(2)}) collective-permute-start(bf16[128,1152]{1,0:T(8,128)(2,1)} %get-tuple-element.62), channel_id=1, source_target_pairs={{0,48},{16,0},{32,16},{48,32},{1,49},{17,1},{33,17},{49,33},{2,50}... | collective-permute-start | bytes 884744 | tf_op jit(solution)/shard_map/ppermute | solution.py:256
  149.2 2.0 copy.21
  151.2 6.5 %collective-permute-done.1 = bf16[128,1152]{1,0:T(8,128)(2,1)} collective-permute-done((bf16[128,1152]{1,0:T(8,128)(2,1)}, bf16[128,1152]{1,0:T(8,128)(2,1)}, u32[]{:S(2)}, u32[]{:S(2)}) %collective-permute-start.1) | collective-permute-done | bytes 294944 | tf_op jit(solution)/shard_map/ppermute | solution.py:256
  157.7 1.2 collective-permute-done.2
  158.9 31.0 %all-to-all-done.4 = bf16[8,256,1152]{2,1,0:T(8,128)(2,1)} async-done(((bf16[8,256,1152]{2,1,0:T(8,128)(2,1)}), bf16[8,256,1152]{2,1,0:T(8,128)(2,1)}, u32[]{:S(2)}, u32[]{:S(2)}) %all-to-all-start.4) | async-done | bytes 4718624 | tf_op jit(solution)/shard_map/all_to_all | solution.py:36
  189.8 10.1 %shard_map.124 = bf16[32,2,24,1024]{3,2,1,0:T(8,128)(2,1)} custom-call(bf16[2,768,1024]{2,1,0:T(8,128)(2,1)} %bitcast.114, bf16[8,2,128,1152]{3,2,1,0:T(8,128)(2,1)} %bitcast.46.weights), custom_call_target="tpu_custom_call" | custom-call | flops 3623878656 | bytes 11010048 | tf_op jit(solution)/shard_map/pallas_call | solution.py:236
  199.9 6.2 %all-to-all-start.6 = ((bf16[32,48,1024]{2,1,0:T(8,128)(2,1)}), bf16[32,48,1024]{2,1,0:T(8,128)(2,1)}, u32[]{:S(2)}, u32[]{:S(2)}) async-start(bf16[32,48,1024]{2,1,0:T(8,128)(2,1)} %bitcast.47), calls=%async_computation.6 | async-start | bytes 6291456 | tf_op jit(solution)/shard_map/all_to_all | solution.py:36
  206.2 0.1 select_reduce_fusion.1
  206.2 0.3 fusion.8
  206.5 0.3 fusion.7
  206.8 0.7 fusion.23
  210.7 10.5 %all-gather.8.cloned.1.call-done = bf16[3072,1152]{1,0:T(8,128)(2,1)} async-done(((bf16[192,1152]{1,0:T(8,128)(2,1)}), bf16[3072,1152]{1,0:T(8,128)(2,1)}) %all-gather.8.cloned.1.call-update) | async-done | bytes 7077904 | tf_op jit(solution)/shard_map/all_gather | solution.py:313
  221.2 2.8 %shard_map.126 = (bf16[2,32,1152]{2,1,0:T(8,128)(2,1)}, bf16[2,32,1152]{2,1,0:T(8,128)(2,1)}, bf16[2,32,1152]{2,1,0:T(8,128)(2,1)}, bf16[2,32,1152]{2,1,0:T(8,128)(2,1)}) custom-call(s32[32]{0:T(128)} %shard_map.120.plan, bf16[8,2,6,32,1152]{4,3,2,1,0:T(8,128)(2,1)} %bitcast.108, bf16[8,2,6,32,1152]{4,3,2,1,0:T(8,128)(2,1)} %bitcast.109, ...), custom_call_target="tpu_custom_call" | custom-call | tf_op jit(solution)/shard_map/pallas_call | solution.py:141
  224.0 3.1 %collective-permute-start.3 = (bf16[2,32,1152]{2,1,0:T(8,128)(2,1)}, bf16[2,32,1152]{2,1,0:T(8,128)(2,1)S(1)}, u32[]{:S(2)}, u32[]{:S(2)}) collective-permute-start(bf16[2,32,1152]{2,1,0:T(8,128)(2,1)} %get-tuple-element.74), channel_id=1, source_target_pairs={{0,16},{16,32},{32,48},{48,0},{1,17},{17,33},{33,49},{49,1},{2,18}... | collective-permute-start | bytes 442376 | tf_op jit(solution)/shard_map/ppermute | solution.py:256
  227.1 4.3 %collective-permute-start.4 = (bf16[2,32,1152]{2,1,0:T(8,128)(2,1)}, bf16[2,32,1152]{2,1,0:T(8,128)(2,1)S(1)}, u32[]{:S(2)}, u32[]{:S(2)}) collective-permute-start(bf16[2,32,1152]{2,1,0:T(8,128)(2,1)} %get-tuple-element.75), channel_id=1, source_target_pairs={{0,32},{16,48},{32,0},{48,16},{1,33},{17,49},{33,1},{49,17},{2,34}... | collective-permute-start | bytes 442376 | tf_op jit(solution)/shard_map/ppermute | solution.py:256
  231.4 3.1 %collective-permute-start.5 = (bf16[2,32,1152]{2,1,0:T(8,128)(2,1)}, bf16[2,32,1152]{2,1,0:T(8,128)(2,1)S(1)}, u32[]{:S(2)}, u32[]{:S(2)}) collective-permute-start(bf16[2,32,1152]{2,1,0:T(8,128)(2,1)} %get-tuple-element.76), channel_id=1, source_target_pairs={{0,48},{16,0},{32,16},{48,32},{1,49},{17,1},{33,17},{49,33},{2,50}... | collective-permute-start | bytes 442376 | tf_op jit(solution)/shard_map/ppermute | solution.py:256
  234.5 1.9 select_bitcast_fusion
  236.3 10.6 %collective-permute-done.3.one = bf16[2,32,1152]{2,1,0:T(8,128)(2,1)S(1)} collective-permute-done((bf16[2,32,1152]{2,1,0:T(8,128)(2,1)}, bf16[2,32,1152]{2,1,0:T(8,128)(2,1)S(1)}, u32[]{:S(2)}, u32[]{:S(2)}) %collective-permute-start.3) | collective-permute-done | bytes 147488 | tf_op jit(solution)/shard_map/ppermute | solution.py:256
  246.9 4.4 %collective-permute-done.4.two = bf16[2,32,1152]{2,1,0:T(8,128)(2,1)S(1)} collective-permute-done((bf16[2,32,1152]{2,1,0:T(8,128)(2,1)}, bf16[2,32,1152]{2,1,0:T(8,128)(2,1)S(1)}, u32[]{:S(2)}, u32[]{:S(2)}) %collective-permute-start.4) | collective-permute-done | bytes 147488 | tf_op jit(solution)/shard_map/ppermute | solution.py:256
  251.3 0.6 copy-done.10
  251.9 0.0 copy-done.11
  252.0 2.0 shard_map.127
  254.0 2.9 %fusion.2 = f32[256,1024]{1,0:T(8,128)S(1)} fusion(bf16[1536,1024]{1,0:T(8,128)(2,1)} %bitcast.48, bf16[1536,128]{1,0:T(8,128)(2,1)S(1)} %fusion.8, bf16[1536,128]{1,0:T(8,128)(2,1)S(1)} %fusion.7), kind=kOutput, calls=%fused_computation.22 | convolution fusion | flops 806879232 | bytes 4980736 | tf_op jit(solution)/shard_map/dot_general | solution.py:338
  256.9 0.8 fusion.14
  257.7 0.8 copy-done.15
  (39 shorter events, 0.1 us)
Async XLA Ops:
  7.2 34.4 %copy-start = (bf16[128,1024]{1,0:T(8,128)(2,1)S(1)}, bf16[128,1024]{1,0:T(8,128)(2,1)}, u32[]{:S(2)}) copy-start(bf16[128,1024]{1,0:T(8,128)(2,1)} %param.17) | copy-start | bytes 786436
  7.2 47.0 %copy-start.3 = (bf16[1,128,1152]{2,1,0:T(8,128)(2,1)S(1)}, bf16[1,128,1152]{2,1,0:T(8,128)(2,1)}, u32[]{:S(2)}) copy-start(bf16[1,128,1152]{2,1,0:T(8,128)(2,1)} %param.14) | copy-start | bytes 884740
  7.2 46.9 %copy-start.7 = (f32[1,128,1152]{2,1,0:T(8,128)S(1)}, f32[1,128,1152]{2,1,0:T(8,128)}, u32[]{:S(2)}) copy-start(f32[1,128,1152]{2,1,0:T(8,128)} %param.11) | copy-start | bytes 1769476
  7.2 46.9 %copy-start.4 = (f32[1,128,1152]{2,1,0:T(8,128)S(1)}, f32[1,128,1152]{2,1,0:T(8,128)}, u32[]{:S(2)}) copy-start(f32[1,128,1152]{2,1,0:T(8,128)} %param.12) | copy-start | bytes 1769476
  7.2 46.9 %copy-start.5 = (f32[1,128,1152]{2,1,0:T(8,128)S(1)}, f32[1,128,1152]{2,1,0:T(8,128)}, u32[]{:S(2)}) copy-start(f32[1,128,1152]{2,1,0:T(8,128)} %param.13) | copy-start | bytes 1769476
  9.2 17.3 %all-to-all-start.2 = ((f32[32,1,128]{2,1,0:T(1,128)}), f32[32,1,128]{2,1,0:T(1,128)S(1)}, u32[]{:S(2)}, u32[]{:S(2)}) async-start(f32[32,1,128]{2,1,0:T(1,128)} %shard_map.121), calls=%async_computation.2 | async-start | bytes 32768 | tf_op jit(solution)/shard_map/all_to_all | solution.py:36
  26.5 0.6 copy-start.12
  28.5 24.3 %all-to-all-start.3 = ((f32[16,1,128]{2,1,0:T(1,128)}), f32[16,1,128]{2,1,0:T(1,128)S(1)}, u32[]{:S(2)}, u32[]{:S(2)}) async-start(f32[16,1,128]{2,1,0:T(1,128)} %shard_map.122), calls=%async_computation.3 | async-start | bytes 16384 | tf_op jit(solution)/shard_map/all_to_all | solution.py:36
  41.5 83.1 %all-gather.6.cloned.1.call-start = ((), (), s32[]{:S(2)}) async-start(), calls=%async_computation.9 | async-start | bytes 5013504 | tf_op jit(solution)/shard_map/all_gather | solution.py:305
  55.8 43.8 %all-to-all-start.5 = ((bf16[32,48,1024]{2,1,0:T(8,128)(2,1)}), bf16[32,48,1024]{2,1,0:T(8,128)(2,1)S(1)}, u32[]{:S(2)}, u32[]{:S(2)}) async-start(bf16[32,48,1024]{2,1,0:T(8,128)(2,1)} %bitcast.113), calls=%async_computation.5 | async-start | bytes 6291456 | tf_op jit(solution)/shard_map/all_to_all | solution.py:36
  62.7 42.0 %copy-start.16 = (s32[64]{0:T(128)S(1)}, s32[64]{0:T(128)}, u32[]{:S(2)}) copy-start(s32[64]{0:T(128)} %old_host.1) | copy-start | bytes 772
  62.7 42.0 %copy-start.18 = (s32[64]{0:T(128)S(1)}, s32[64]{0:T(128)}, u32[]{:S(2)}) copy-start(s32[64]{0:T(128)} %new_host.1) | copy-start | bytes 772
  99.6 22.5 %all-to-all-start.7 = ((bf16[8,32,1152]{2,1,0:T(8,128)(2,1)}), bf16[8,32,1152]{2,1,0:T(8,128)(2,1)}, u32[]{:S(2)}, u32[]{:S(2)}) async-start(bf16[8,32,1152]{2,1,0:T(8,128)(2,1)} %pad_maximum_fusion.1), calls=%async_computation.7 | async-start | bytes 1179648 | tf_op jit(solution)/shard_map/all_to_all | solution.py:36
  104.6 116.6 %all-gather.8.cloned.1.call-start = ((), (), s32[]{:S(2)}) async-start(), calls=%async_computation.10 | async-start | bytes 7520256 | tf_op jit(solution)/shard_map/all_gather | solution.py:313
  124.6 65.2 %all-to-all-start.4 = ((bf16[8,256,1152]{2,1,0:T(8,128)(2,1)}), bf16[8,256,1152]{2,1,0:T(8,128)(2,1)}, u32[]{:S(2)}, u32[]{:S(2)}) async-start(bf16[8,256,1152]{2,1,0:T(8,128)(2,1)} %bitcast.103), calls=%async_computation.4 | async-start | bytes 9437184 | tf_op jit(solution)/shard_map/all_to_all | solution.py:36
  138.5 12.7 %collective-permute-start = (bf16[128,1152]{1,0:T(8,128)(2,1)}, bf16[128,1152]{1,0:T(8,128)(2,1)}, u32[]{:S(2)}, u32[]{:S(2)}) collective-permute-start(bf16[128,1152]{1,0:T(8,128)(2,1)} %get-tuple-element.60), channel_id=1, source_target_pairs={{0,16},{16,32},{32,48},{48,0},{1,17},{17,33},{33,49},{49,1},{2,18}... | collective-permute-start | bytes 884744 | tf_op jit(solution)/shard_map/ppermute | solution.py:256
  141.6 16.0 %collective-permute-start.1 = (bf16[128,1152]{1,0:T(8,128)(2,1)}, bf16[128,1152]{1,0:T(8,128)(2,1)}, u32[]{:S(2)}, u32[]{:S(2)}) collective-permute-start(bf16[128,1152]{1,0:T(8,128)(2,1)} %get-tuple-element.61), channel_id=1, source_target_pairs={{0,32},{16,48},{32,0},{48,16},{1,33},{17,49},{33,1},{49,17},{2,34}... | collective-permute-start | bytes 884744 | tf_op jit(solution)/shard_map/ppermute | solution.py:256
  146.0 12.9 %collective-permute-start.2 = (bf16[128,1152]{1,0:T(8,128)(2,1)}, bf16[128,1152]{1,0:T(8,128)(2,1)}, u32[]{:S(2)}, u32[]{:S(2)}) collective-permute-start(bf16[128,1152]{1,0:T(8,128)(2,1)} %get-tuple-element.62), channel_id=1, source_target_pairs={{0,48},{16,0},{32,16},{48,32},{1,49},{17,1},{33,17},{49,33},{2,50}... | collective-permute-start | bytes 884744 | tf_op jit(solution)/shard_map/ppermute | solution.py:256
  199.9 6.2 %copy-start.14 = (f32[128,8]{0,1:T(8,128)S(1)}, f32[128,8]{0,1:T(8,128)}, u32[]{:S(2)}) copy-start(f32[128,8]{0,1:T(8,128)} %param.19) | copy-start | bytes 12292
  199.9 6.9 %copy-start.13 = (s32[32]{0:T(128)S(1)}, s32[32]{0:T(128)}, u32[]{:S(2)}) copy-start(s32[32]{0:T(128)} %shard_map.120.plan) | copy-start | bytes 388
  199.9 54.1 %all-to-all-start.6 = ((bf16[32,48,1024]{2,1,0:T(8,128)(2,1)}), bf16[32,48,1024]{2,1,0:T(8,128)(2,1)}, u32[]{:S(2)}, u32[]{:S(2)}) async-start(bf16[32,48,1024]{2,1,0:T(8,128)(2,1)} %bitcast.47), calls=%async_computation.6 | async-start | bytes 6291456 | tf_op jit(solution)/shard_map/all_to_all | solution.py:36
  221.2 13.2 %copy-start.6 = (f32[128,1152]{1,0:T(8,128)S(1)}, f32[128,1152]{1,0:T(8,128)}, u32[]{:S(2)}) copy-start(f32[128,1152]{1,0:T(8,128)} %get-tuple-element.89) | copy-start | bytes 1769476
  221.2 13.2 %copy-start.8 = (bf16[128,1152]{1,0:T(8,128)(2,1)S(1)}, bf16[128,1152]{1,0:T(8,128)(2,1)}, u32[]{:S(2)}) copy-start(bf16[128,1152]{1,0:T(8,128)(2,1)} %get-tuple-element.63) | copy-start | bytes 884740
  221.2 30.7 %copy-start.1 = (f32[128,1152]{1,0:T(8,128)S(1)}, f32[128,1152]{1,0:T(8,128)}, u32[]{:S(2)}) copy-start(f32[128,1152]{1,0:T(8,128)} %get-tuple-element.90.own_one) | copy-start | bytes 1769476
  221.2 30.7 %copy-start.2 = (f32[128,1152]{1,0:T(8,128)S(1)}, f32[128,1152]{1,0:T(8,128)}, u32[]{:S(2)}) copy-start(f32[128,1152]{1,0:T(8,128)} %get-tuple-element.91.own_two) | copy-start | bytes 1769476
  224.0 22.9 %collective-permute-start.3 = (bf16[2,32,1152]{2,1,0:T(8,128)(2,1)}, bf16[2,32,1152]{2,1,0:T(8,128)(2,1)S(1)}, u32[]{:S(2)}, u32[]{:S(2)}) collective-permute-start(bf16[2,32,1152]{2,1,0:T(8,128)(2,1)} %get-tuple-element.74), channel_id=1, source_target_pairs={{0,16},{16,32},{32,48},{48,0},{1,17},{17,33},{33,49},{49,1},{2,18}... | collective-permute-start | bytes 442376 | tf_op jit(solution)/shard_map/ppermute | solution.py:256
  227.1 24.1 %collective-permute-start.4 = (bf16[2,32,1152]{2,1,0:T(8,128)(2,1)}, bf16[2,32,1152]{2,1,0:T(8,128)(2,1)S(1)}, u32[]{:S(2)}, u32[]{:S(2)}) collective-permute-start(bf16[2,32,1152]{2,1,0:T(8,128)(2,1)} %get-tuple-element.75), channel_id=1, source_target_pairs={{0,32},{16,48},{32,0},{48,16},{1,33},{17,49},{33,1},{49,17},{2,34}... | collective-permute-start | bytes 442376 | tf_op jit(solution)/shard_map/ppermute | solution.py:256
  231.4 19.9 %collective-permute-start.5 = (bf16[2,32,1152]{2,1,0:T(8,128)(2,1)}, bf16[2,32,1152]{2,1,0:T(8,128)(2,1)S(1)}, u32[]{:S(2)}, u32[]{:S(2)}) collective-permute-start(bf16[2,32,1152]{2,1,0:T(8,128)(2,1)} %get-tuple-element.76), channel_id=1, source_target_pairs={{0,48},{16,0},{32,16},{48,32},{1,49},{17,1},{33,17},{49,33},{2,50}... | collective-permute-start | bytes 442376 | tf_op jit(solution)/shard_map/ppermute | solution.py:256
  246.9 4.4 %copy-start.9 = (bf16[2,32,1152]{2,1,0:T(8,128)(2,1)}, bf16[2,32,1152]{2,1,0:T(8,128)(2,1)S(1)}, u32[]{:S(2)}) copy-start(bf16[2,32,1152]{2,1,0:T(8,128)(2,1)S(1)} %collective-permute-done.3.one) | copy-start | bytes 442372
  251.3 0.7 copy-start.10
  251.3 0.7 copy-start.11
  254.0 3.7 %copy-start.17 = (s32[64]{0:T(128)S(1)}, s32[64]{0:T(128)}, u32[]{:S(2)}) copy-start(s32[64]{0:T(128)} %old_host.1) | copy-start | bytes 772
  254.0 3.7 %copy-start.19 = (s32[64]{0:T(128)S(1)}, s32[64]{0:T(128)}, u32[]{:S(2)}) copy-start(s32[64]{0:T(128)} %new_host.1) | copy-start | bytes 772
  257.7 0.8 copy-start.15
Sparse Core Ops, SparseCore 0:
  55.9 67.2 all-gather.5
  125.9 95.2 all-gather.7

commit v5 on v4

--- a/solution.py
+++ b/solution.py
@@ -36,6 +36,10 @@
     return lax.all_to_all(array, axes, split_axis=0, concat_axis=0, tiled=True)
 
 
+def limit(mebibytes):
+    return pltpu.CompilerParams(vmem_limit_bytes=mebibytes * 2**20)
+
+
 def spread_squares(values, sent):
     value = values[...].astype(f32)
     sent[...] = jnp.full(sent.shape, jnp.sum(value * value), f32)
@@ -47,7 +51,9 @@
 
 def spread(kernel, operand, axes):
     return pl.pallas_call(
-        kernel, out_shape=jax.ShapeDtypeStruct((lax.axis_size(axes), 1, 128), f32)
+        kernel,
+        out_shape=jax.ShapeDtypeStruct((lax.axis_size(axes), 1, 128), f32),
+        compiler_params=limit(2),
     )(operand)
 
 
@@ -102,6 +108,7 @@
         in_specs=[scalars, scalars],
         out_specs=scalars,
         scratch_shapes=[pltpu.SMEM((X * Z,), jnp.int32)] * 3,
+        compiler_params=limit(1),
     )(old_host, new_host)
 
 
@@ -126,6 +133,7 @@
             in_specs=[take(shift) for shift in range(X)],
             out_specs=[pl.BlockSpec((rows, cols), lambda i, plan: (0, 0))] * X,
         ),
+        compiler_params=limit(60),
     )(plan, *[planes] * X)
 
 
@@ -147,6 +155,7 @@
             in_specs=[take(shift) for shift in range(X)],
             out_specs=[pl.BlockSpec((NEAR, rows, cols), lambda i, plan: (0, 0, 0))] * X,
         ),
+        compiler_params=limit(60),
     )(plan, *[pieces] * X)
 
 
@@ -165,6 +174,7 @@
             in_specs=[pl.BlockSpec(pieces.shape, lambda i, plan: (0, 0, 0))],
             out_specs=pl.BlockSpec((SLOTS,) + pieces.shape[1:], lambda i, plan: (0, 0, 0)),
         ),
+        compiler_params=limit(4),
     )(plan, pieces)
 
 
@@ -191,6 +201,7 @@
         out_shape=[jax.ShapeDtypeStruct(own_one.shape, f32)] * 2,
         in_specs=[pl.BlockSpec(memory_space=pltpu.SMEM)] + [whole] * 6,
         out_specs=[whole] * 2,
+        compiler_params=limit(8),
     )(plan, *arrived, own_one, own_two)
 
 
@@ -231,18 +242,16 @@
 def experts(rows, weights, capacity):
     shares, row_count, width = rows.shape
     shards, _, shard_rows, cols = weights.shape
-    parts = 2
-    part = row_count // parts
     return pl.pallas_call(
         expert_layer,
         out_shape=jax.ShapeDtypeStruct((row_count // capacity, shares, capacity, width), bf16),
-        grid=(shares, parts),
+        grid=(shares,),
         in_specs=[
-            pl.BlockSpec((1, part, width), lambda j, i: (j, i, 0)),
-            pl.BlockSpec((shards, 1, shard_rows, cols), lambda j, i: (0, j, 0, 0)),
+            pl.BlockSpec((1, row_count, width), lambda j: (j, 0, 0)),
+            pl.BlockSpec((shards, 1, shard_rows, cols), lambda j: (0, j, 0, 0)),
         ],
-        out_specs=pl.BlockSpec((part // capacity, 1, capacity, width), lambda j, i: (i, j, 0, 0)),
-        compiler_params=pltpu.CompilerParams(vmem_limit_bytes=48 * 2**20),
+        out_specs=pl.BlockSpec((row_count // capacity, 1, capacity, width), lambda j: (0, j, 0, 0)),
+        compiler_params=limit(30),
         cost_estimate=pl.CostEstimate(
             flops=2 * shares * row_count * width * cols,
             bytes_accessed=2 * (weights.size + 2 * rows.size),
@@ -302,14 +311,17 @@
     outgoing, factor = lax.optimization_barrier((outgoing, factor))
 
     new_master, new_one, new_two = adamw(master, moment_one, moment_two, gradients, factor)
-    gathered = lax.all_gather(new_master.astype(bf16), RING, axis=0, tiled=True)
-    received = swap(outgoing, PLANE)
+    new_master, new_one, new_two, rounded = lax.optimization_barrier(
+        (new_master, new_one, new_two, new_master.astype(bf16))
+    )
+    gathered = lax.all_gather(rounded, RING, axis=0, tiled=True)
     piece = rows // (X * NEAR)
     pieces = jnp.concatenate(
         [item.astype(bf16).reshape(-1, piece, cols) for item in (new_one, new_two)], axis=1
     )
-    pieces, received = lax.optimization_barrier((pieces, received))
-    pieces = compacted(plan, swap(pieces, ("x", "near")))
+    pieces, outgoing = lax.optimization_barrier((swap(pieces, ("x", "near")), outgoing))
+    received = swap(outgoing, PLANE)
+    pieces = compacted(plan, pieces)
     pieces = lax.all_gather(pieces.reshape(-1, cols), RING, axis=0, tiled=True)
 
     held = pick_planes(plan, gathered.reshape(Z, rows, cols))

time: 267 us -> 257 us (0.963)
  blocking collectives: 0 us -> 47 us
  waiting for transfers between devices: 126 us -> 90.1 us
  starting transfers between devices: 72.3 us -> 60.2 us
  Pallas kernels: 26.8 us -> 21 us
  other arithmetic: 11.6 us -> 8.29 us
    all_to_all x0 -> x1, blocking collectives: none -> 47 us  [swap(): return lax.all_to_all(array, axes, split_axis=0, concat_axis=0, tiled=True)]
    all_to_all x6 -> x5, waiting for transfers between devices: 92.5 us -> 56.9 us  [swap(): return lax.all_to_all(array, axes, split_axis=0, concat_axis=0, tiled=True)]
    all_to_all x6 -> x5, starting transfers between devices: 51.2 us -> 39.1 us  [swap(): return lax.all_to_all(array, axes, split_axis=0, concat_axis=0, tiled=True)]
    mul x3 -> x0, other arithmetic: 3.25 us -> none  [the longest x1 1.13 us: adamw(): new_two = beta_two * moment_two + (1.0 - beta_two) * scaled * scaled]
  transfers between devices with their start and end apart: 14 -> 13, of which waited for: 10 -> 9; matrix products, arithmetic and copies ran while one was open for 5% -> 4% of each run, Pallas kernels for 9% -> 8%
where the time goes in v5:
time: 257 us; the launch traced here: 256 us
  waiting for transfers between devices  90.1 us (35%)
  starting transfers between devices  60.2 us (23%)
  blocking collectives  47 us (18%)
  Pallas kernels  21 us (8%)
  between operations  18.2 us (7%)
  other arithmetic  8.29 us (3%)
  local copies, waits for them, and re-layouts  5.94 us (2%)
  matrix products  5.68 us (2%)
    all_to_all x5, waiting for transfers between devices, swap(): return lax.all_to_all(array, axes, split_axis=0, concat_axis=0, tiled=True)  56.9 us
    all_to_all x1, blocking collectives, swap(): return lax.all_to_all(array, axes, split_axis=0, concat_axis=0, tiled=True)  47 us
    all_to_all x5, starting transfers between devices, swap(): return lax.all_to_all(array, axes, split_axis=0, concat_axis=0, tiled=True)  39.1 us
    ppermute x6, starting transfers between devices, shifted(): lax.ppermute(block, 'x', [(i, (i + shift) % size) for i in range(size)])  20.9 us
    ppermute x6, waiting for transfers between devices, shifted(): lax.ppermute(block, 'x', [(i, (i + shift) % size) for i in range(size)])  20.6 us
    all_gather x1, waiting for transfers between devices, per_device(): pieces = lax.all_gather(pieces.reshape(-1, cols), RING, axis=0, tiled=True)  12.6 us
    pallas_call x1, Pallas kernels, experts(): pl.pallas_call(expert_layer, out_shape=jax.ShapeDtypeStruct((row_count //...  8.76 us
  transfers between devices with their start and end apart: 13, of which 9 were waited for; matrix products, arithmetic and copies ran while one was open for 4% of the time, Pallas kernels for 8%

profile of v5, /device:TPU:1, one launch (start us, length us, event | category | flops | bytes accessed | tf_op | source)
XLA Modules:
  0.0 256.3 jit_solution(13568060540141370819)
XLA Ops:
  7.2 0.0 copy-start
  7.2 0.0 copy-start.1
  7.2 1.0 copy-done.1
  8.2 0.9 shard_map.121
  9.1 10.4 %all-to-all-start.2 = ((f32[32,1,128]{2,1,0:T(1,128)}), f32[32,1,128]{2,1,0:T(1,128)S(1)}, u32[]{:S(2)}, u32[]{:S(2)}) async-start(f32[32,1,128]{2,1,0:T(1,128)} %shard_map.121), calls=%async_computation.2 | async-start | bytes 32768 | tf_op jit(solution)/shard_map/all_to_all | solution.py:36
  19.5 0.7 fusion.14
  20.1 0.8 select_reduce_fusion.2
  20.9 0.1 fusion.13
  21.0 0.1 convolution_select_fusion
  21.2 0.1 eq.86
  21.3 0.3 bitcast_compare_fusion
  21.6 4.9 %all-to-all-done.2.values = f32[32,1,128]{2,1,0:T(1,128)S(1)} async-done(((f32[32,1,128]{2,1,0:T(1,128)}), f32[32,1,128]{2,1,0:T(1,128)S(1)}, u32[]{:S(2)}, u32[]{:S(2)}) %all-to-all-start.2) | async-done | bytes 16416 | tf_op jit(solution)/shard_map/all_to_all | solution.py:36
  26.4 0.6 shard_map.122
  27.0 13.0 %all-to-all-start.3 = ((f32[16,1,128]{2,1,0:T(1,128)}), f32[16,1,128]{2,1,0:T(1,128)S(1)}, u32[]{:S(2)}, u32[]{:S(2)}) async-start(f32[16,1,128]{2,1,0:T(1,128)} %shard_map.122), calls=%async_computation.3 | async-start | bytes 16384 | tf_op jit(solution)/shard_map/all_to_all | solution.py:36
  40.1 0.0 all-gather.6.cloned.1.call-start
  40.1 0.0 copy-done
  40.1 2.6 %convolution_convert_fusion = bf16[1536,1024]{1,0:T(8,128)(2,1)} fusion(pred[1536,128]{1,0:T(32,128)(4,1)S(1)} %bitcast_compare_fusion, bf16[128,1024]{1,0:T(8,128)(2,1)S(1)} %copy-done), kind=kOutput, calls=%fused_computation.18 | convolution fusion | flops 404226048 | bytes 3604480 | tf_op jit(solution)/shard_map/dot_general | solution.py:305
  42.8 8.5 %all-to-all-done.3 = f32[16,1,128]{2,1,0:T(1,128)S(1)} async-done(((f32[16,1,128]{2,1,0:T(1,128)}), f32[16,1,128]{2,1,0:T(1,128)S(1)}, u32[]{:S(2)}, u32[]{:S(2)}) %all-to-all-start.3) | async-done | bytes 8224 | tf_op jit(solution)/shard_map/all_to_all | solution.py:36
  51.3 0.6 slice_reduce_fusion
  52.7 1.4 fusion.16
  54.1 0.0 all-gather.6.cloned.1.call-update
  54.2 1.0 pad_maximum_fusion.1
  55.2 0.0 copy-done.7
  55.2 3.5 %all-to-all-start.5 = ((bf16[8,32,1152]{2,1,0:T(8,128)(2,1)}), bf16[8,32,1152]{2,1,0:T(8,128)(2,1)S(1)}, u32[]{:S(2)}, u32[]{:S(2)}) async-start(bf16[8,32,1152]{2,1,0:T(8,128)(2,1)} %pad_maximum_fusion.1), calls=%async_computation.5 | async-start | bytes 1179648 | tf_op jit(solution)/shard_map/all_to_all | solution.py:36
  58.8 0.0 all-gather.8.cloned.1.call-start
  58.9 3.0 %shard_map.120.plan = s32[32]{0:T(128)S(1)} custom-call(s32[64]{0:T(128)S(1)} %copy-done.19, s32[64]{0:T(128)S(1)} %copy-done.20), custom_call_target="tpu_custom_call" | custom-call | tf_op jit(solution)/shard_map/pallas_call | solution.py:105
  61.8 12.3 %all-to-all-done.5.pieces = bf16[8,32,1152]{2,1,0:T(8,128)(2,1)S(1)} async-done(((bf16[8,32,1152]{2,1,0:T(8,128)(2,1)}), bf16[8,32,1152]{2,1,0:T(8,128)(2,1)S(1)}, u32[]{:S(2)}, u32[]{:S(2)}) %all-to-all-start.5) | async-done | bytes 589856 | tf_op jit(solution)/shard_map/all_to_all | solution.py:36
  74.2 1.3 shard_map.125
  75.5 0.0 all-gather.8.cloned.1.call-update
  75.5 47.0 %all_to_all.39 = bf16[32,48,1024]{2,1,0:T(8,128)(2,1)} all-to-all(bf16[32,48,1024]{2,1,0:T(8,128)(2,1)} %bitcast.113), channel_id=1, replica_groups=mesh['y'=4,'c'=2,'x'=4,'far'=8,'near'=2] {'y','c','x'}, dimensions={0} | all-to-all | bytes 6291456 | tf_op jit(solution)/shard_map/all_to_all | solution.py:36
  122.5 0.0 copy-done.9
  122.5 6.1 %all-to-all-start.4 = ((bf16[8,256,1152]{2,1,0:T(8,128)(2,1)}), bf16[8,256,1152]{2,1,0:T(8,128)(2,1)}, u32[]{:S(2)}, u32[]{:S(2)}) async-start(bf16[8,256,1152]{2,1,0:T(8,128)(2,1)} %bitcast.104), calls=%async_computation.4 | async-start | bytes 9437184 | tf_op jit(solution)/shard_map/all_to_all | solution.py:36
  128.7 2.9 %shard_map.123 = (bf16[128,1152]{1,0:T(8,128)(2,1)}, bf16[128,1152]{1,0:T(8,128)(2,1)}, bf16[128,1152]{1,0:T(8,128)(2,1)}, bf16[128,1152]{1,0:T(8,128)(2,1)}) custom-call(s32[32]{0:T(128)} %copy-done.4, bf16[16,128,1152]{2,1,0:T(8,128)(2,1)} %bitcast.105, bf16[16,128,1152]{2,1,0:T(8,128)(2,1)} %bitcast.106, bf16[16,128,1152]{2,1,0:T(8,128)(2,1)} %bitcast.107, ...), custom_call_target="tpu_custom_call" | custom-call | tf_op jit(solution)/shard_map/pallas_call | solution.py:127
  131.6 2.8 %collective-permute-start = (bf16[128,1152]{1,0:T(8,128)(2,1)}, bf16[128,1152]{1,0:T(8,128)(2,1)}, u32[]{:S(2)}, u32[]{:S(2)}) collective-permute-start(bf16[128,1152]{1,0:T(8,128)(2,1)} %get-tuple-element.65), channel_id=1, source_target_pairs={{0,16},{16,32},{32,48},{48,0},{1,17},{17,33},{33,49},{49,1},{2,18}... | collective-permute-start | bytes 884744 | tf_op jit(solution)/shard_map/ppermute | solution.py:265
  134.4 4.7 %collective-permute-start.1 = (bf16[128,1152]{1,0:T(8,128)(2,1)}, bf16[128,1152]{1,0:T(8,128)(2,1)}, u32[]{:S(2)}, u32[]{:S(2)}) collective-permute-start(bf16[128,1152]{1,0:T(8,128)(2,1)} %get-tuple-element.66), channel_id=1, source_target_pairs={{0,32},{16,48},{32,0},{48,16},{1,33},{17,49},{33,1},{49,17},{2,34}... | collective-permute-start | bytes 884744 | tf_op jit(solution)/shard_map/ppermute | solution.py:265
  139.1 2.9 %collective-permute-start.2 = (bf16[128,1152]{1,0:T(8,128)(2,1)}, bf16[128,1152]{1,0:T(8,128)(2,1)}, u32[]{:S(2)}, u32[]{:S(2)}) collective-permute-start(bf16[128,1152]{1,0:T(8,128)(2,1)} %get-tuple-element.67), channel_id=1, source_target_pairs={{0,48},{16,0},{32,16},{48,32},{1,49},{17,1},{33,17},{49,33},{2,50}... | collective-permute-start | bytes 884744 | tf_op jit(solution)/shard_map/ppermute | solution.py:265
  142.1 2.3 copy.21
  144.4 0.0 collective-permute-done
  144.4 6.5 %collective-permute-done.1 = bf16[128,1152]{1,0:T(8,128)(2,1)} collective-permute-done((bf16[128,1152]{1,0:T(8,128)(2,1)}, bf16[128,1152]{1,0:T(8,128)(2,1)}, u32[]{:S(2)}, u32[]{:S(2)}) %collective-permute-start.1) | collective-permute-done | bytes 294944 | tf_op jit(solution)/shard_map/ppermute | solution.py:265
  150.8 1.1 collective-permute-done.2
  152.0 31.2 %all-to-all-done.4 = bf16[8,256,1152]{2,1,0:T(8,128)(2,1)} async-done(((bf16[8,256,1152]{2,1,0:T(8,128)(2,1)}), bf16[8,256,1152]{2,1,0:T(8,128)(2,1)}, u32[]{:S(2)}, u32[]{:S(2)}) %all-to-all-start.4) | async-done | bytes 4718624 | tf_op jit(solution)/shard_map/all_to_all | solution.py:36
  183.2 8.8 %shard_map.124 = bf16[32,2,24,1024]{3,2,1,0:T(8,128)(2,1)} custom-call(bf16[2,768,1024]{2,1,0:T(8,128)(2,1)S(1)} %bitcast.102, bf16[8,2,128,1152]{3,2,1,0:T(8,128)(2,1)} %bitcast.45.weights), custom_call_target="tpu_custom_call" | custom-call | flops 3623878656 | bytes 11010048 | tf_op jit(solution)/shard_map/pallas_call | solution.py:245
  192.0 6.0 %all-to-all-start.7 = ((bf16[32,48,1024]{2,1,0:T(8,128)(2,1)}), bf16[32,48,1024]{2,1,0:T(8,128)(2,1)}, u32[]{:S(2)}, u32[]{:S(2)}) async-start(bf16[32,48,1024]{2,1,0:T(8,128)(2,1)} %bitcast.46), calls=%async_computation.7 | async-start | bytes 6291456 | tf_op jit(solution)/shard_map/all_to_all | solution.py:36
  198.0 0.1 select_reduce_fusion.1
  198.1 0.3 fusion.8
  198.4 0.3 fusion.7
  198.7 0.6 fusion.21
  202.4 12.6 %all-gather.8.cloned.1.call-done = bf16[3072,1152]{1,0:T(8,128)(2,1)} async-done(((bf16[192,1152]{1,0:T(8,128)(2,1)}), bf16[3072,1152]{1,0:T(8,128)(2,1)}) %all-gather.8.cloned.1.call-update) | async-done | bytes 7077904 | tf_op jit(solution)/shard_map/all_gather | solution.py:325
  214.9 2.8 %shard_map.126 = (bf16[2,32,1152]{2,1,0:T(8,128)(2,1)}, bf16[2,32,1152]{2,1,0:T(8,128)(2,1)}, bf16[2,32,1152]{2,1,0:T(8,128)(2,1)}, bf16[2,32,1152]{2,1,0:T(8,128)(2,1)}) custom-call(s32[32]{0:T(128)} %copy-done.4, bf16[8,2,6,32,1152]{4,3,2,1,0:T(8,128)(2,1)} %bitcast.109, bf16[8,2,6,32,1152]{4,3,2,1,0:T(8,128)(2,1)} %bitcast.110, ...), custom_call_target="tpu_custom_call" | custom-call | tf_op jit(solution)/shard_map/pallas_call | solution.py:149
  217.7 3.1 %collective-permute-start.3 = (bf16[2,32,1152]{2,1,0:T(8,128)(2,1)}, bf16[2,32,1152]{2,1,0:T(8,128)(2,1)S(1)}, u32[]{:S(2)}, u32[]{:S(2)}) collective-permute-start(bf16[2,32,1152]{2,1,0:T(8,128)(2,1)} %get-tuple-element.82), channel_id=1, source_target_pairs={{0,16},{16,32},{32,48},{48,0},{1,17},{17,33},{33,49},{49,1},{2,18}... | collective-permute-start | bytes 442376 | tf_op jit(solution)/shard_map/ppermute | solution.py:265
  220.8 4.3 %collective-permute-start.4 = (bf16[2,32,1152]{2,1,0:T(8,128)(2,1)}, bf16[2,32,1152]{2,1,0:T(8,128)(2,1)S(1)}, u32[]{:S(2)}, u32[]{:S(2)}) collective-permute-start(bf16[2,32,1152]{2,1,0:T(8,128)(2,1)} %get-tuple-element.83), channel_id=1, source_target_pairs={{0,32},{16,48},{32,0},{48,16},{1,33},{17,49},{33,1},{49,17},{2,34}... | collective-permute-start | bytes 442376 | tf_op jit(solution)/shard_map/ppermute | solution.py:265
  225.1 3.1 %collective-permute-start.5 = (bf16[2,32,1152]{2,1,0:T(8,128)(2,1)}, bf16[2,32,1152]{2,1,0:T(8,128)(2,1)S(1)}, u32[]{:S(2)}, u32[]{:S(2)}) collective-permute-start(bf16[2,32,1152]{2,1,0:T(8,128)(2,1)} %get-tuple-element.84), channel_id=1, source_target_pairs={{0,48},{16,0},{32,16},{48,32},{1,49},{17,1},{33,17},{49,33},{2,50}... | collective-permute-start | bytes 442376 | tf_op jit(solution)/shard_map/ppermute | solution.py:265
  228.2 2.0 select_bitcast_fusion
  230.2 8.6 %collective-permute-done.3.one = bf16[2,32,1152]{2,1,0:T(8,128)(2,1)S(1)} collective-permute-done((bf16[2,32,1152]{2,1,0:T(8,128)(2,1)}, bf16[2,32,1152]{2,1,0:T(8,128)(2,1)S(1)}, u32[]{:S(2)}, u32[]{:S(2)}) %collective-permute-start.3) | collective-permute-done | bytes 147488 | tf_op jit(solution)/shard_map/ppermute | solution.py:265
  238.8 4.4 %collective-permute-done.4.two = bf16[2,32,1152]{2,1,0:T(8,128)(2,1)S(1)} collective-permute-done((bf16[2,32,1152]{2,1,0:T(8,128)(2,1)}, bf16[2,32,1152]{2,1,0:T(8,128)(2,1)S(1)}, u32[]{:S(2)}, u32[]{:S(2)}) %collective-permute-start.4) | collective-permute-done | bytes 147488 | tf_op jit(solution)/shard_map/ppermute | solution.py:265
  243.1 0.0 collective-permute-done.5.three
  243.1 0.0 copy-start.3
  243.2 0.9 copy-done.3
  244.1 0.7 shard_map.127
  244.8 0.0 all-to-all-done.7
  244.8 2.9 %fusion.2 = f32[256,1024]{1,0:T(8,128)S(1)} fusion(bf16[1536,1024]{1,0:T(8,128)(2,1)} %bitcast.47, bf16[1536,128]{1,0:T(8,128)(2,1)S(1)} %fusion.8, bf16[1536,128]{1,0:T(8,128)(2,1)S(1)} %fusion.7), kind=kOutput, calls=%fused_computation.21 | convolution fusion | flops 806879232 | bytes 4980736 | tf_op jit(solution)/shard_map/dot_general | solution.py:350
  247.7 0.8 fusion.12
  248.4 0.8 copy-done.17
  249.3 0.2 copy-done.18
  (38 shorter events, 0.1 us)
Async XLA Ops:
  7.2 33.0 %copy-start = (bf16[128,1024]{1,0:T(8,128)(2,1)S(1)}, bf16[128,1024]{1,0:T(8,128)(2,1)}, u32[]{:S(2)}) copy-start(bf16[128,1024]{1,0:T(8,128)(2,1)} %param.17) | copy-start | bytes 786436
  7.2 1.0 copy-start.1
  8.2 44.5 %copy-start.2 = (bf16[1,128,1152]{2,1,0:T(8,128)(2,1)S(1)}, bf16[1,128,1152]{2,1,0:T(8,128)(2,1)}, u32[]{:S(2)}) copy-start(bf16[1,128,1152]{2,1,0:T(8,128)(2,1)} %param.14) | copy-start | bytes 884740
  8.2 44.5 %copy-start.12 = (f32[1,128,1152]{2,1,0:T(8,128)S(1)}, f32[1,128,1152]{2,1,0:T(8,128)}, u32[]{:S(2)}) copy-start(f32[1,128,1152]{2,1,0:T(8,128)} %param.11) | copy-start | bytes 1769476
  8.2 44.5 %copy-start.13 = (f32[1,128,1152]{2,1,0:T(8,128)S(1)}, f32[1,128,1152]{2,1,0:T(8,128)}, u32[]{:S(2)}) copy-start(f32[1,128,1152]{2,1,0:T(8,128)} %param.12) | copy-start | bytes 1769476
  8.2 44.5 %copy-start.14 = (f32[1,128,1152]{2,1,0:T(8,128)S(1)}, f32[1,128,1152]{2,1,0:T(8,128)}, u32[]{:S(2)}) copy-start(f32[1,128,1152]{2,1,0:T(8,128)} %param.13) | copy-start | bytes 1769476
  9.1 17.3 %all-to-all-start.2 = ((f32[32,1,128]{2,1,0:T(1,128)}), f32[32,1,128]{2,1,0:T(1,128)S(1)}, u32[]{:S(2)}, u32[]{:S(2)}) async-start(f32[32,1,128]{2,1,0:T(1,128)} %shard_map.121), calls=%async_computation.2 | async-start | bytes 32768 | tf_op jit(solution)/shard_map/all_to_all | solution.py:36
  27.0 24.3 %all-to-all-start.3 = ((f32[16,1,128]{2,1,0:T(1,128)}), f32[16,1,128]{2,1,0:T(1,128)S(1)}, u32[]{:S(2)}, u32[]{:S(2)}) async-start(f32[16,1,128]{2,1,0:T(1,128)} %shard_map.122), calls=%async_computation.3 | async-start | bytes 16384 | tf_op jit(solution)/shard_map/all_to_all | solution.py:36
  40.1 82.4 %all-gather.6.cloned.1.call-start = ((), (), s32[]{:S(2)}) async-start(), calls=%async_computation.9 | async-start | bytes 5013504 | tf_op jit(solution)/shard_map/all_gather | solution.py:317
  54.1 1.1 copy-start.7
  54.1 68.4 %copy-start.9 = (f32[128,1152]{1,0:T(8,128)}, f32[128,1152]{1,0:T(8,128)S(1)}, u32[]{:S(2)}) copy-start(f32[128,1152]{1,0:T(8,128)S(1)} %get-tuple-element.74.own_two) | copy-start | bytes 1769476
  54.1 4.7 %copy-start.19 = (s32[64]{0:T(128)S(1)}, s32[64]{0:T(128)}, u32[]{:S(2)}) copy-start(s32[64]{0:T(128)} %old_host.1) | copy-start | bytes 772
  54.1 4.7 %copy-start.20 = (s32[64]{0:T(128)S(1)}, s32[64]{0:T(128)}, u32[]{:S(2)}) copy-start(s32[64]{0:T(128)} %new_host.1) | copy-start | bytes 772
  55.2 18.9 %all-to-all-start.5 = ((bf16[8,32,1152]{2,1,0:T(8,128)(2,1)}), bf16[8,32,1152]{2,1,0:T(8,128)(2,1)S(1)}, u32[]{:S(2)}, u32[]{:S(2)}) async-start(bf16[8,32,1152]{2,1,0:T(8,128)(2,1)} %pad_maximum_fusion.1), calls=%async_computation.5 | async-start | bytes 1179648 | tf_op jit(solution)/shard_map/all_to_all | solution.py:36
  58.8 156.1 %all-gather.8.cloned.1.call-start = ((), (), s32[]{:S(2)}) async-start(), calls=%async_computation.10 | async-start | bytes 7520256 | tf_op jit(solution)/shard_map/all_gather | solution.py:325
  61.8 60.7 %copy-start.4 = (s32[32]{0:T(128)}, s32[32]{0:T(128)S(1)}, u32[]{:S(2)}) copy-start(s32[32]{0:T(128)S(1)} %shard_map.120.plan) | copy-start | bytes 388
  122.5 60.7 %all-to-all-start.4 = ((bf16[8,256,1152]{2,1,0:T(8,128)(2,1)}), bf16[8,256,1152]{2,1,0:T(8,128)(2,1)}, u32[]{:S(2)}, u32[]{:S(2)}) async-start(bf16[8,256,1152]{2,1,0:T(8,128)(2,1)} %bitcast.104), calls=%async_computation.4 | async-start | bytes 9437184 | tf_op jit(solution)/shard_map/all_to_all | solution.py:36
  131.6 12.8 %collective-permute-start = (bf16[128,1152]{1,0:T(8,128)(2,1)}, bf16[128,1152]{1,0:T(8,128)(2,1)}, u32[]{:S(2)}, u32[]{:S(2)}) collective-permute-start(bf16[128,1152]{1,0:T(8,128)(2,1)} %get-tuple-element.65), channel_id=1, source_target_pairs={{0,16},{16,32},{32,48},{48,0},{1,17},{17,33},{33,49},{49,1},{2,18}... | collective-permute-start | bytes 884744 | tf_op jit(solution)/shard_map/ppermute | solution.py:265
  134.4 16.4 %collective-permute-start.1 = (bf16[128,1152]{1,0:T(8,128)(2,1)}, bf16[128,1152]{1,0:T(8,128)(2,1)}, u32[]{:S(2)}, u32[]{:S(2)}) collective-permute-start(bf16[128,1152]{1,0:T(8,128)(2,1)} %get-tuple-element.66), channel_id=1, source_target_pairs={{0,32},{16,48},{32,0},{48,16},{1,33},{17,49},{33,1},{49,17},{2,34}... | collective-permute-start | bytes 884744 | tf_op jit(solution)/shard_map/ppermute | solution.py:265
  139.1 12.8 %collective-permute-start.2 = (bf16[128,1152]{1,0:T(8,128)(2,1)}, bf16[128,1152]{1,0:T(8,128)(2,1)}, u32[]{:S(2)}, u32[]{:S(2)}) collective-permute-start(bf16[128,1152]{1,0:T(8,128)(2,1)} %get-tuple-element.67), channel_id=1, source_target_pairs={{0,48},{16,0},{32,16},{48,32},{1,49},{17,1},{33,17},{49,33},{2,50}... | collective-permute-start | bytes 884744 | tf_op jit(solution)/shard_map/ppermute | solution.py:265
  192.0 6.1 %copy-start.16 = (f32[128,8]{0,1:T(8,128)S(1)}, f32[128,8]{0,1:T(8,128)}, u32[]{:S(2)}) copy-start(f32[128,8]{0,1:T(8,128)} %param.19) | copy-start | bytes 12292
  192.0 6.7 %copy-start.5 = (s32[32]{0:T(128)S(1)}, s32[32]{0:T(128)}, u32[]{:S(2)}) copy-start(s32[32]{0:T(128)} %copy-done.4) | copy-start | bytes 388
  192.0 52.8 %all-to-all-start.7 = ((bf16[32,48,1024]{2,1,0:T(8,128)(2,1)}), bf16[32,48,1024]{2,1,0:T(8,128)(2,1)}, u32[]{:S(2)}, u32[]{:S(2)}) async-start(bf16[32,48,1024]{2,1,0:T(8,128)(2,1)} %bitcast.46), calls=%async_computation.7 | async-start | bytes 6291456 | tf_op jit(solution)/shard_map/all_to_all | solution.py:36
  214.9 13.3 %copy-start.11 = (f32[128,1152]{1,0:T(8,128)S(1)}, f32[128,1152]{1,0:T(8,128)}, u32[]{:S(2)}) copy-start(f32[128,1152]{1,0:T(8,128)} %get-tuple-element.72) | copy-start | bytes 1769476
  214.9 13.3 %copy-start.15 = (bf16[128,1152]{1,0:T(8,128)(2,1)S(1)}, bf16[128,1152]{1,0:T(8,128)(2,1)}, u32[]{:S(2)}) copy-start(bf16[128,1152]{1,0:T(8,128)(2,1)} %get-tuple-element.68) | copy-start | bytes 884740
  214.9 28.2 %copy-start.6 = (s32[32]{0:T(128)S(1)}, s32[32]{0:T(128)}, u32[]{:S(2)}) copy-start(s32[32]{0:T(128)} %copy-done.4) | copy-start | bytes 388
  214.9 28.2 %copy-start.8 = (f32[128,1152]{1,0:T(8,128)S(1)}, f32[128,1152]{1,0:T(8,128)}, u32[]{:S(2)}) copy-start(f32[128,1152]{1,0:T(8,128)} %copy-done.7) | copy-start | bytes 1769476
  214.9 28.2 %copy-start.10 = (f32[128,1152]{1,0:T(8,128)S(1)}, f32[128,1152]{1,0:T(8,128)}, u32[]{:S(2)}) copy-start(f32[128,1152]{1,0:T(8,128)} %copy-done.9) | copy-start | bytes 1769476
  217.7 21.1 %collective-permute-start.3 = (bf16[2,32,1152]{2,1,0:T(8,128)(2,1)}, bf16[2,32,1152]{2,1,0:T(8,128)(2,1)S(1)}, u32[]{:S(2)}, u32[]{:S(2)}) collective-permute-start(bf16[2,32,1152]{2,1,0:T(8,128)(2,1)} %get-tuple-element.82), channel_id=1, source_target_pairs={{0,16},{16,32},{32,48},{48,0},{1,17},{17,33},{33,49},{49,1},{2,18}... | collective-permute-start | bytes 442376 | tf_op jit(solution)/shard_map/ppermute | solution.py:265
  220.8 22.4 %collective-permute-start.4 = (bf16[2,32,1152]{2,1,0:T(8,128)(2,1)}, bf16[2,32,1152]{2,1,0:T(8,128)(2,1)S(1)}, u32[]{:S(2)}, u32[]{:S(2)}) collective-permute-start(bf16[2,32,1152]{2,1,0:T(8,128)(2,1)} %get-tuple-element.83), channel_id=1, source_target_pairs={{0,32},{16,48},{32,0},{48,16},{1,33},{17,49},{33,1},{49,17},{2,34}... | collective-permute-start | bytes 442376 | tf_op jit(solution)/shard_map/ppermute | solution.py:265
  225.1 18.0 %collective-permute-start.5 = (bf16[2,32,1152]{2,1,0:T(8,128)(2,1)}, bf16[2,32,1152]{2,1,0:T(8,128)(2,1)S(1)}, u32[]{:S(2)}, u32[]{:S(2)}) collective-permute-start(bf16[2,32,1152]{2,1,0:T(8,128)(2,1)} %get-tuple-element.84), channel_id=1, source_target_pairs={{0,48},{16,0},{32,16},{48,32},{1,49},{17,1},{33,17},{49,33},{2,50}... | collective-permute-start | bytes 442376 | tf_op jit(solution)/shard_map/ppermute | solution.py:265
  243.1 0.9 copy-start.3
  248.4 0.8 copy-start.17
  248.4 1.0 copy-start.18
Sparse Core Ops, SparseCore 0:
  54.3 62.6 all-gather.5
  119.6 95.2 all-gather.7

commit v6 on v5

--- a/solution.py
+++ b/solution.py
@@ -305,9 +305,7 @@
     outgoing = jnp.dot(pick, tokens, preferred_element_type=f32).astype(bf16)
     outgoing = outgoing.reshape(Y * CORE * X, SHARE * capacity, width)
     mix = jnp.where(taken, gate[:, None, :], 0.0).reshape(-1, tok_count)
-    mix_high = mix.astype(bf16)
-    mix_low = (mix - mix_high.astype(f32)).astype(bf16)
-    mix_both = jnp.concatenate([mix_high, mix_low], axis=1)
+    mix = mix.astype(bf16)
     outgoing, factor = lax.optimization_barrier((outgoing, factor))
 
     new_master, new_one, new_two = adamw(master, moment_one, moment_two, gradients, factor)
@@ -338,17 +336,17 @@
     returned = swap(results, PLANE).reshape(-1, width)
 
     held = pick_pieces(late_plan, pieces.reshape(Z // NEAR, NEAR, SLOTS, 2 * piece, cols))
-    moments = finished(plan, [held[0]] + shifted(held[1:], X), new_one, new_two)
-    returned, moments = lax.optimization_barrier((returned, list(moments)))
+    arrived = [held[0]] + shifted(held[1:], X)
+    returned, arrived[0] = lax.optimization_barrier((returned, arrived[0]))
+    contract = (((0,), (0,)), ((), ()))
+    mixed = lax.dot_general(mix, returned, contract, preferred_element_type=f32).astype(bf16)
+    mixed, arrived = lax.optimization_barrier((mixed, arrived))
+    moments = finished(plan, arrived, new_one, new_two)
     moments = lax.cond(
         plan[OVER] == 1,
         lambda: relocated_whole(old_host, new_host, new_one, new_two),
-        lambda: moments,
-    )
-
-    contract = (((0,), (0,)), ((), ()))
-    mixed = lax.dot_general(mix_both, returned, contract, preferred_element_type=f32)
-    mixed = (mixed[:tok_count] + mixed[tok_count:]).astype(bf16)
+        lambda: list(moments),
+    )
     return (
         jnp.where(moved, moved_master, new_master)[None],
         moments[0][None],

time: 257 us -> 253 us (0.984)
  waiting for transfers between devices: 90.1 us -> 87.2 us
    ppermute x6, waiting for transfers between devices: 20.6 us -> 11.5 us  [shifted(): lax.ppermute(block, 'x', [(i, (i + shift) % size) for i in range(size)])]
    all_to_all x5, waiting for transfers between devices: 56.9 us -> 64.8 us  [swap(): return lax.all_to_all(array, axes, split_axis=0, concat_axis=0, tiled=True)]
  transfers between devices with their start and end apart: 13 -> 13, of which waited for: 9 -> 9; matrix products, arithmetic and copies ran while one was open for 4% -> 6% of each run, Pallas kernels for 8% -> 7%
where the time goes in v6:
time: 253 us; the launch traced here: 252 us
  waiting for transfers between devices  87.2 us (34%)
  starting transfers between devices  60.3 us (24%)
  blocking collectives  47 us (19%)
  Pallas kernels  20.8 us (8%)
  between operations  18.2 us (7%)
  other arithmetic  7.2 us (3%)
  matrix products  5.98 us (2%)
  local copies, waits for them, and re-layouts  5.03 us (2%)
    all_to_all x5, waiting for transfers between devices, swap(): return lax.all_to_all(array, axes, split_axis=0, concat_axis=0, tiled=True)  64.8 us
    all_to_all x1, blocking collectives, swap(): return lax.all_to_all(array, axes, split_axis=0, concat_axis=0, tiled=True)  47 us
    all_to_all x5, starting transfers between devices, swap(): return lax.all_to_all(array, axes, split_axis=0, concat_axis=0, tiled=True)  39.1 us
    ppermute x6, starting transfers between devices, shifted(): lax.ppermute(block, 'x', [(i, (i + shift) % size) for i in range(size)])  21.1 us
    ppermute x6, waiting for transfers between devices, shifted(): lax.ppermute(block, 'x', [(i, (i + shift) % size) for i in range(size)])  11.5 us
    all_gather x1, waiting for transfers between devices, per_device(): pieces = lax.all_gather(pieces.reshape(-1, cols), RING, axis=0, tiled=True)  10.9 us
    pallas_call x1, Pallas kernels, experts(): pl.pallas_call(expert_layer, out_shape=jax.ShapeDtypeStruct((row_count //...  8.76 us
  transfers between devices with their start and end apart: 13, of which 9 were waited for; matrix products, arithmetic and copies ran while one was open for 6% of the time, Pallas kernels for 7%

profile of v6, /device:TPU:1, one launch (start us, length us, event | category | flops | bytes accessed | tf_op | source)
XLA Modules:
  0.0 251.7 jit_solution(5218572066270656302)
XLA Ops:
  7.2 0.0 copy-start
  7.2 0.0 copy-start.1
  7.2 1.0 copy-done.1
  8.2 0.9 shard_map.121
  9.1 10.4 %all-to-all-start.2 = ((f32[32,1,128]{2,1,0:T(1,128)}), f32[32,1,128]{2,1,0:T(1,128)S(1)}, u32[]{:S(2)}, u32[]{:S(2)}) async-start(f32[32,1,128]{2,1,0:T(1,128)} %shard_map.121), calls=%async_computation.2 | async-start | bytes 32768 | tf_op jit(solution)/shard_map/all_to_all | solution.py:36
  19.5 0.7 fusion.7
  20.1 0.8 select_reduce_fusion.2
  20.9 0.1 fusion.6
  21.0 0.1 convolution_select_fusion
  21.2 0.1 eq.86
  21.3 0.3 bitcast_compare_fusion
  21.6 4.9 %all-to-all-done.2.values = f32[32,1,128]{2,1,0:T(1,128)S(1)} async-done(((f32[32,1,128]{2,1,0:T(1,128)}), f32[32,1,128]{2,1,0:T(1,128)S(1)}, u32[]{:S(2)}, u32[]{:S(2)}) %all-to-all-start.2) | async-done | bytes 16416 | tf_op jit(solution)/shard_map/all_to_all | solution.py:36
  26.4 0.6 shard_map.122
  27.0 13.0 %all-to-all-start.3 = ((f32[16,1,128]{2,1,0:T(1,128)}), f32[16,1,128]{2,1,0:T(1,128)S(1)}, u32[]{:S(2)}, u32[]{:S(2)}) async-start(f32[16,1,128]{2,1,0:T(1,128)} %shard_map.122), calls=%async_computation.3 | async-start | bytes 16384 | tf_op jit(solution)/shard_map/all_to_all | solution.py:36
  40.1 0.0 all-gather.6.cloned.1.call-start
  40.1 0.0 copy-done
  40.1 2.6 %convolution_convert_fusion = bf16[1536,1024]{1,0:T(8,128)(2,1)} fusion(pred[1536,128]{1,0:T(32,128)(4,1)S(1)} %bitcast_compare_fusion, bf16[128,1024]{1,0:T(8,128)(2,1)S(1)} %copy-done), kind=kOutput, calls=%fused_computation.18 | convolution fusion | flops 404226048 | bytes 3604480 | tf_op jit(solution)/shard_map/dot_general | solution.py:305
  42.8 8.5 %all-to-all-done.3 = f32[16,1,128]{2,1,0:T(1,128)S(1)} async-done(((f32[16,1,128]{2,1,0:T(1,128)}), f32[16,1,128]{2,1,0:T(1,128)S(1)}, u32[]{:S(2)}, u32[]{:S(2)}) %all-to-all-start.3) | async-done | bytes 8224 | tf_op jit(solution)/shard_map/all_to_all | solution.py:36
  51.3 0.6 slice_reduce_fusion
  52.7 0.0 copy-done.2
  52.7 1.4 fusion.8
  54.1 0.0 all-gather.6.cloned.1.call-update
  54.2 1.0 pad_maximum_fusion.1
  55.2 0.0 copy-done.7
  55.2 3.5 %all-to-all-start.5 = ((bf16[8,32,1152]{2,1,0:T(8,128)(2,1)}), bf16[8,32,1152]{2,1,0:T(8,128)(2,1)S(1)}, u32[]{:S(2)}, u32[]{:S(2)}) async-start(bf16[8,32,1152]{2,1,0:T(8,128)(2,1)} %pad_maximum_fusion.1), calls=%async_computation.5 | async-start | bytes 1179648 | tf_op jit(solution)/shard_map/all_to_all | solution.py:36
  58.8 0.0 all-gather.8.cloned.1.call-start
  58.9 3.0 %shard_map.120.plan = s32[32]{0:T(128)S(1)} custom-call(s32[64]{0:T(128)S(1)} %copy-done.19, s32[64]{0:T(128)S(1)} %copy-done.20), custom_call_target="tpu_custom_call" | custom-call | tf_op jit(solution)/shard_map/pallas_call | solution.py:105
  61.8 12.3 %all-to-all-done.5.pieces = bf16[8,32,1152]{2,1,0:T(8,128)(2,1)S(1)} async-done(((bf16[8,32,1152]{2,1,0:T(8,128)(2,1)}), bf16[8,32,1152]{2,1,0:T(8,128)(2,1)S(1)}, u32[]{:S(2)}, u32[]{:S(2)}) %all-to-all-start.5) | async-done | bytes 589856 | tf_op jit(solution)/shard_map/all_to_all | solution.py:36
  74.2 1.3 shard_map.125
  75.5 0.0 all-gather.8.cloned.1.call-update
  75.5 47.0 %all_to_all.39 = bf16[32,48,1024]{2,1,0:T(8,128)(2,1)} all-to-all(bf16[32,48,1024]{2,1,0:T(8,128)(2,1)} %bitcast.104), channel_id=1, replica_groups=mesh['y'=4,'c'=2,'x'=4,'far'=8,'near'=2] {'y','c','x'}, dimensions={0} | all-to-all | bytes 6291456 | tf_op jit(solution)/shard_map/all_to_all | solution.py:36
  122.5 0.0 copy-done.9
  122.5 6.1 %all-to-all-start.4 = ((bf16[8,256,1152]{2,1,0:T(8,128)(2,1)}), bf16[8,256,1152]{2,1,0:T(8,128)(2,1)}, u32[]{:S(2)}, u32[]{:S(2)}) async-start(bf16[8,256,1152]{2,1,0:T(8,128)(2,1)} %bitcast.95), calls=%async_computation.4 | async-start | bytes 9437184 | tf_op jit(solution)/shard_map/all_to_all | solution.py:36
  128.7 2.9 %shard_map.123 = (bf16[128,1152]{1,0:T(8,128)(2,1)}, bf16[128,1152]{1,0:T(8,128)(2,1)}, bf16[128,1152]{1,0:T(8,128)(2,1)}, bf16[128,1152]{1,0:T(8,128)(2,1)}) custom-call(s32[32]{0:T(128)} %copy-done.4, bf16[16,128,1152]{2,1,0:T(8,128)(2,1)} %bitcast.96, bf16[16,128,1152]{2,1,0:T(8,128)(2,1)} %bitcast.97, bf16[16,128,1152]{2,1,0:T(8,128)(2,1)} %bitcast.98, ...), custom_call_target="tpu_custom_call" | custom-call | tf_op jit(solution)/shard_map/pallas_call | solution.py:127
  131.6 2.8 %collective-permute-start = (bf16[128,1152]{1,0:T(8,128)(2,1)}, bf16[128,1152]{1,0:T(8,128)(2,1)}, u32[]{:S(2)}, u32[]{:S(2)}) collective-permute-start(bf16[128,1152]{1,0:T(8,128)(2,1)} %get-tuple-element.67), channel_id=1, source_target_pairs={{0,16},{16,32},{32,48},{48,0},{1,17},{17,33},{33,49},{49,1},{2,18}... | collective-permute-start | bytes 884744 | tf_op jit(solution)/shard_map/ppermute | solution.py:265
  134.4 4.7 %collective-permute-start.1 = (bf16[128,1152]{1,0:T(8,128)(2,1)}, bf16[128,1152]{1,0:T(8,128)(2,1)}, u32[]{:S(2)}, u32[]{:S(2)}) collective-permute-start(bf16[128,1152]{1,0:T(8,128)(2,1)} %get-tuple-element.68), channel_id=1, source_target_pairs={{0,32},{16,48},{32,0},{48,16},{1,33},{17,49},{33,1},{49,17},{2,34}... | collective-permute-start | bytes 884744 | tf_op jit(solution)/shard_map/ppermute | solution.py:265
  139.1 2.9 %collective-permute-start.2 = (bf16[128,1152]{1,0:T(8,128)(2,1)}, bf16[128,1152]{1,0:T(8,128)(2,1)}, u32[]{:S(2)}, u32[]{:S(2)}) collective-permute-start(bf16[128,1152]{1,0:T(8,128)(2,1)} %get-tuple-element.69), channel_id=1, source_target_pairs={{0,48},{16,0},{32,16},{48,32},{1,49},{17,1},{33,17},{49,33},{2,50}... | collective-permute-start | bytes 884744 | tf_op jit(solution)/shard_map/ppermute | solution.py:265
  142.1 2.3 copy.21
  144.4 0.0 collective-permute-done
  144.4 6.5 %collective-permute-done.1 = bf16[128,1152]{1,0:T(8,128)(2,1)} collective-permute-done((bf16[128,1152]{1,0:T(8,128)(2,1)}, bf16[128,1152]{1,0:T(8,128)(2,1)}, u32[]{:S(2)}, u32[]{:S(2)}) %collective-permute-start.1) | collective-permute-done | bytes 294944 | tf_op jit(solution)/shard_map/ppermute | solution.py:265
  150.8 1.1 collective-permute-done.2
  152.0 31.2 %all-to-all-done.4 = bf16[8,256,1152]{2,1,0:T(8,128)(2,1)} async-done(((bf16[8,256,1152]{2,1,0:T(8,128)(2,1)}), bf16[8,256,1152]{2,1,0:T(8,128)(2,1)}, u32[]{:S(2)}, u32[]{:S(2)}) %all-to-all-start.4) | async-done | bytes 4718624 | tf_op jit(solution)/shard_map/all_to_all | solution.py:36
  183.2 8.8 %shard_map.124 = bf16[32,2,24,1024]{3,2,1,0:T(8,128)(2,1)} custom-call(bf16[2,768,1024]{2,1,0:T(8,128)(2,1)S(1)} %bitcast.93, bf16[8,2,128,1152]{3,2,1,0:T(8,128)(2,1)} %bitcast.47.weights), custom_call_target="tpu_custom_call" | custom-call | flops 3623878656 | bytes 11010048 | tf_op jit(solution)/shard_map/pallas_call | solution.py:245
  192.0 6.1 %all-to-all-start.7 = ((bf16[32,48,1024]{2,1,0:T(8,128)(2,1)}), bf16[32,48,1024]{2,1,0:T(8,128)(2,1)}, u32[]{:S(2)}, u32[]{:S(2)}) async-start(bf16[32,48,1024]{2,1,0:T(8,128)(2,1)} %bitcast.48), calls=%async_computation.7 | async-start | bytes 6291456 | tf_op jit(solution)/shard_map/all_to_all | solution.py:36
  198.0 0.0 copy-done.5
  198.0 0.6 fusion.13
  201.7 0.1 select_reduce_fusion.1
  201.8 0.3 fusion.2
  202.1 1.9 select_bitcast_fusion
  204.0 10.9 %all-gather.8.cloned.1.call-done = bf16[3072,1152]{1,0:T(8,128)(2,1)} async-done(((bf16[192,1152]{1,0:T(8,128)(2,1)}), bf16[3072,1152]{1,0:T(8,128)(2,1)}) %all-gather.8.cloned.1.call-update) | async-done | bytes 7077904 | tf_op jit(solution)/shard_map/all_gather | solution.py:323
  214.9 2.6 %shard_map.126 = (bf16[2,32,1152]{2,1,0:T(8,128)(2,1)}, bf16[2,32,1152]{2,1,0:T(8,128)(2,1)}, bf16[2,32,1152]{2,1,0:T(8,128)(2,1)}, bf16[2,32,1152]{2,1,0:T(8,128)(2,1)}) custom-call(s32[32]{0:T(128)} %copy-done.4, bf16[8,2,6,32,1152]{4,3,2,1,0:T(8,128)(2,1)} %bitcast.100, bf16[8,2,6,32,1152]{4,3,2,1,0:T(8,128)(2,1)} %bitcast.101, ...), custom_call_target="tpu_custom_call" | custom-call | tf_op jit(solution)/shard_map/pallas_call | solution.py:149
  217.5 3.2 %collective-permute-start.3 = (bf16[2,32,1152]{2,1,0:T(8,128)(2,1)}, bf16[2,32,1152]{2,1,0:T(8,128)(2,1)S(1)}, u32[]{:S(2)}, u32[]{:S(2)}) collective-permute-start(bf16[2,32,1152]{2,1,0:T(8,128)(2,1)} %get-tuple-element.86), channel_id=1, source_target_pairs={{0,16},{16,32},{32,48},{48,0},{1,17},{17,33},{33,49},{49,1},{2,18}... | collective-permute-start | bytes 442376 | tf_op jit(solution)/shard_map/ppermute | solution.py:265
  220.8 4.3 %collective-permute-start.4 = (bf16[2,32,1152]{2,1,0:T(8,128)(2,1)}, bf16[2,32,1152]{2,1,0:T(8,128)(2,1)S(1)}, u32[]{:S(2)}, u32[]{:S(2)}) collective-permute-start(bf16[2,32,1152]{2,1,0:T(8,128)(2,1)} %get-tuple-element.87), channel_id=1, source_target_pairs={{0,32},{16,48},{32,0},{48,16},{1,33},{17,49},{33,1},{49,17},{2,34}... | collective-permute-start | bytes 442376 | tf_op jit(solution)/shard_map/ppermute | solution.py:265
  225.1 3.1 %collective-permute-start.5 = (bf16[2,32,1152]{2,1,0:T(8,128)(2,1)}, bf16[2,32,1152]{2,1,0:T(8,128)(2,1)S(1)}, u32[]{:S(2)}, u32[]{:S(2)}) collective-permute-start(bf16[2,32,1152]{2,1,0:T(8,128)(2,1)} %get-tuple-element.88), channel_id=1, source_target_pairs={{0,48},{16,0},{32,16},{48,32},{1,49},{17,1},{33,17},{49,33},{2,50}... | collective-permute-start | bytes 442376 | tf_op jit(solution)/shard_map/ppermute | solution.py:265
  228.2 7.8 %all-to-all-done.7 = bf16[32,48,1024]{2,1,0:T(8,128)(2,1)} async-done(((bf16[32,48,1024]{2,1,0:T(8,128)(2,1)}), bf16[32,48,1024]{2,1,0:T(8,128)(2,1)}, u32[]{:S(2)}, u32[]{:S(2)}) %all-to-all-start.7) | async-done | bytes 3145760 | tf_op jit(solution)/shard_map/all_to_all | solution.py:36
  236.0 3.2 %convolution_convert_fusion.1 = bf16[128,1024]{1,0:T(8,128)(2,1)} fusion(bf16[1536,128]{1,0:T(8,128)(2,1)S(1)} %fusion.2, bf16[1536,1024]{1,0:T(8,128)(2,1)} %bitcast.49), kind=kOutput, calls=%fused_computation.19 | convolution fusion | flops 402784256 | bytes 3801088 | tf_op jit(solution)/shard_map/dot_general | solution.py:342
  239.2 0.0 collective-permute-done.3.one
  239.2 3.9 %collective-permute-done.4.two = bf16[2,32,1152]{2,1,0:T(8,128)(2,1)S(1)} collective-permute-done((bf16[2,32,1152]{2,1,0:T(8,128)(2,1)}, bf16[2,32,1152]{2,1,0:T(8,128)(2,1)S(1)}, u32[]{:S(2)}, u32[]{:S(2)}) %collective-permute-start.4) | collective-permute-done | bytes 147488 | tf_op jit(solution)/shard_map/ppermute | solution.py:265
  243.1 0.0 collective-permute-done.5.three
  243.2 0.6 shard_map.127
  243.8 0.0 copy-start.17
  243.8 0.0 copy-start.18
  243.8 0.8 copy-done.17
  244.6 0.2 copy-done.18
  (36 shorter events, 0.1 us)
Async XLA Ops:
  7.2 33.0 %copy-start = (bf16[128,1024]{1,0:T(8,128)(2,1)S(1)}, bf16[128,1024]{1,0:T(8,128)(2,1)}, u32[]{:S(2)}) copy-start(bf16[128,1024]{1,0:T(8,128)(2,1)} %param.17) | copy-start | bytes 786436
  7.2 1.0 copy-start.1
  8.2 44.5 %copy-start.2 = (bf16[1,128,1152]{2,1,0:T(8,128)(2,1)S(1)}, bf16[1,128,1152]{2,1,0:T(8,128)(2,1)}, u32[]{:S(2)}) copy-start(bf16[1,128,1152]{2,1,0:T(8,128)(2,1)} %param.14) | copy-start | bytes 884740
  8.2 44.5 %copy-start.12 = (f32[1,128,1152]{2,1,0:T(8,128)S(1)}, f32[1,128,1152]{2,1,0:T(8,128)}, u32[]{:S(2)}) copy-start(f32[1,128,1152]{2,1,0:T(8,128)} %param.11) | copy-start | bytes 1769476
  8.2 44.5 %copy-start.13 = (f32[1,128,1152]{2,1,0:T(8,128)S(1)}, f32[1,128,1152]{2,1,0:T(8,128)}, u32[]{:S(2)}) copy-start(f32[1,128,1152]{2,1,0:T(8,128)} %param.12) | copy-start | bytes 1769476
  8.2 44.5 %copy-start.14 = (f32[1,128,1152]{2,1,0:T(8,128)S(1)}, f32[1,128,1152]{2,1,0:T(8,128)}, u32[]{:S(2)}) copy-start(f32[1,128,1152]{2,1,0:T(8,128)} %param.13) | copy-start | bytes 1769476
  9.1 17.3 %all-to-all-start.2 = ((f32[32,1,128]{2,1,0:T(1,128)}), f32[32,1,128]{2,1,0:T(1,128)S(1)}, u32[]{:S(2)}, u32[]{:S(2)}) async-start(f32[32,1,128]{2,1,0:T(1,128)} %shard_map.121), calls=%async_computation.2 | async-start | bytes 32768 | tf_op jit(solution)/shard_map/all_to_all | solution.py:36
  27.0 24.3 %all-to-all-start.3 = ((f32[16,1,128]{2,1,0:T(1,128)}), f32[16,1,128]{2,1,0:T(1,128)S(1)}, u32[]{:S(2)}, u32[]{:S(2)}) async-start(f32[16,1,128]{2,1,0:T(1,128)} %shard_map.122), calls=%async_computation.3 | async-start | bytes 16384 | tf_op jit(solution)/shard_map/all_to_all | solution.py:36
  40.1 82.4 %all-gather.6.cloned.1.call-start = ((), (), s32[]{:S(2)}) async-start(), calls=%async_computation.9 | async-start | bytes 5013504 | tf_op jit(solution)/shard_map/all_gather | solution.py:315
  54.1 1.1 copy-start.7
  54.1 68.4 %copy-start.9 = (f32[128,1152]{1,0:T(8,128)}, f32[128,1152]{1,0:T(8,128)S(1)}, u32[]{:S(2)}) copy-start(f32[128,1152]{1,0:T(8,128)S(1)} %get-tuple-element.76.own_two) | copy-start | bytes 1769476
  54.1 4.7 %copy-start.19 = (s32[64]{0:T(128)S(1)}, s32[64]{0:T(128)}, u32[]{:S(2)}) copy-start(s32[64]{0:T(128)} %old_host.1) | copy-start | bytes 772
  54.1 4.7 %copy-start.20 = (s32[64]{0:T(128)S(1)}, s32[64]{0:T(128)}, u32[]{:S(2)}) copy-start(s32[64]{0:T(128)} %new_host.1) | copy-start | bytes 772
  55.2 18.9 %all-to-all-start.5 = ((bf16[8,32,1152]{2,1,0:T(8,128)(2,1)}), bf16[8,32,1152]{2,1,0:T(8,128)(2,1)S(1)}, u32[]{:S(2)}, u32[]{:S(2)}) async-start(bf16[8,32,1152]{2,1,0:T(8,128)(2,1)} %pad_maximum_fusion.1), calls=%async_computation.5 | async-start | bytes 1179648 | tf_op jit(solution)/shard_map/all_to_all | solution.py:36
  58.8 156.1 %all-gather.8.cloned.1.call-start = ((), (), s32[]{:S(2)}) async-start(), calls=%async_computation.10 | async-start | bytes 7520256 | tf_op jit(solution)/shard_map/all_gather | solution.py:323
  61.8 60.7 %copy-start.4 = (s32[32]{0:T(128)}, s32[32]{0:T(128)S(1)}, u32[]{:S(2)}) copy-start(s32[32]{0:T(128)S(1)} %shard_map.120.plan) | copy-start | bytes 388
  122.5 60.7 %all-to-all-start.4 = ((bf16[8,256,1152]{2,1,0:T(8,128)(2,1)}), bf16[8,256,1152]{2,1,0:T(8,128)(2,1)}, u32[]{:S(2)}, u32[]{:S(2)}) async-start(bf16[8,256,1152]{2,1,0:T(8,128)(2,1)} %bitcast.95), calls=%async_computation.4 | async-start | bytes 9437184 | tf_op jit(solution)/shard_map/all_to_all | solution.py:36
  131.6 12.8 %collective-permute-start = (bf16[128,1152]{1,0:T(8,128)(2,1)}, bf16[128,1152]{1,0:T(8,128)(2,1)}, u32[]{:S(2)}, u32[]{:S(2)}) collective-permute-start(bf16[128,1152]{1,0:T(8,128)(2,1)} %get-tuple-element.67), channel_id=1, source_target_pairs={{0,16},{16,32},{32,48},{48,0},{1,17},{17,33},{33,49},{49,1},{2,18}... | collective-permute-start | bytes 884744 | tf_op jit(solution)/shard_map/ppermute | solution.py:265
  134.4 16.4 %collective-permute-start.1 = (bf16[128,1152]{1,0:T(8,128)(2,1)}, bf16[128,1152]{1,0:T(8,128)(2,1)}, u32[]{:S(2)}, u32[]{:S(2)}) collective-permute-start(bf16[128,1152]{1,0:T(8,128)(2,1)} %get-tuple-element.68), channel_id=1, source_target_pairs={{0,32},{16,48},{32,0},{48,16},{1,33},{17,49},{33,1},{49,17},{2,34}... | collective-permute-start | bytes 884744 | tf_op jit(solution)/shard_map/ppermute | solution.py:265
  139.1 12.8 %collective-permute-start.2 = (bf16[128,1152]{1,0:T(8,128)(2,1)}, bf16[128,1152]{1,0:T(8,128)(2,1)}, u32[]{:S(2)}, u32[]{:S(2)}) collective-permute-start(bf16[128,1152]{1,0:T(8,128)(2,1)} %get-tuple-element.69), channel_id=1, source_target_pairs={{0,48},{16,0},{32,16},{48,32},{1,49},{17,1},{33,17},{49,33},{2,50}... | collective-permute-start | bytes 884744 | tf_op jit(solution)/shard_map/ppermute | solution.py:265
  192.0 6.1 %copy-start.5 = (s32[32]{0:T(128)S(1)}, s32[32]{0:T(128)}, u32[]{:S(2)}) copy-start(s32[32]{0:T(128)} %copy-done.4) | copy-start | bytes 388
  192.0 9.8 %copy-start.16 = (f32[128,8]{0,1:T(8,128)S(1)}, f32[128,8]{0,1:T(8,128)}, u32[]{:S(2)}) copy-start(f32[128,8]{0,1:T(8,128)} %param.19) | copy-start | bytes 12292
  192.0 10.1 %copy-start.11 = (f32[128,1152]{1,0:T(8,128)S(1)}, f32[128,1152]{1,0:T(8,128)}, u32[]{:S(2)}) copy-start(f32[128,1152]{1,0:T(8,128)} %get-tuple-element.74) | copy-start | bytes 1769476
  192.0 10.1 %copy-start.15 = (bf16[128,1152]{1,0:T(8,128)(2,1)S(1)}, bf16[128,1152]{1,0:T(8,128)(2,1)}, u32[]{:S(2)}) copy-start(bf16[128,1152]{1,0:T(8,128)(2,1)} %get-tuple-element.70) | copy-start | bytes 884740
  192.0 44.0 %all-to-all-start.7 = ((bf16[32,48,1024]{2,1,0:T(8,128)(2,1)}), bf16[32,48,1024]{2,1,0:T(8,128)(2,1)}, u32[]{:S(2)}, u32[]{:S(2)}) async-start(bf16[32,48,1024]{2,1,0:T(8,128)(2,1)} %bitcast.48), calls=%async_computation.7 | async-start | bytes 6291456 | tf_op jit(solution)/shard_map/all_to_all | solution.py:36
  217.5 25.6 %copy-start.3 = (bf16[2,32,1152]{2,1,0:T(8,128)(2,1)S(1)}, bf16[2,32,1152]{2,1,0:T(8,128)(2,1)}, u32[]{:S(2)}) copy-start(bf16[2,32,1152]{2,1,0:T(8,128)(2,1)} %get-tuple-element.89.here) | copy-start | bytes 442372
  217.5 25.6 %copy-start.6 = (s32[32]{0:T(128)S(1)}, s32[32]{0:T(128)}, u32[]{:S(2)}) copy-start(s32[32]{0:T(128)} %copy-done.4) | copy-start | bytes 388
  217.5 25.6 %copy-start.8 = (f32[128,1152]{1,0:T(8,128)S(1)}, f32[128,1152]{1,0:T(8,128)}, u32[]{:S(2)}) copy-start(f32[128,1152]{1,0:T(8,128)} %copy-done.7) | copy-start | bytes 1769476
  217.5 25.6 %copy-start.10 = (f32[128,1152]{1,0:T(8,128)S(1)}, f32[128,1152]{1,0:T(8,128)}, u32[]{:S(2)}) copy-start(f32[128,1152]{1,0:T(8,128)} %copy-done.9) | copy-start | bytes 1769476
  217.5 21.7 %collective-permute-start.3 = (bf16[2,32,1152]{2,1,0:T(8,128)(2,1)}, bf16[2,32,1152]{2,1,0:T(8,128)(2,1)S(1)}, u32[]{:S(2)}, u32[]{:S(2)}) collective-permute-start(bf16[2,32,1152]{2,1,0:T(8,128)(2,1)} %get-tuple-element.86), channel_id=1, source_target_pairs={{0,16},{16,32},{32,48},{48,0},{1,17},{17,33},{33,49},{49,1},{2,18}... | collective-permute-start | bytes 442376 | tf_op jit(solution)/shard_map/ppermute | solution.py:265
  220.8 22.4 %collective-permute-start.4 = (bf16[2,32,1152]{2,1,0:T(8,128)(2,1)}, bf16[2,32,1152]{2,1,0:T(8,128)(2,1)S(1)}, u32[]{:S(2)}, u32[]{:S(2)}) collective-permute-start(bf16[2,32,1152]{2,1,0:T(8,128)(2,1)} %get-tuple-element.87), channel_id=1, source_target_pairs={{0,32},{16,48},{32,0},{48,16},{1,33},{17,49},{33,1},{49,17},{2,34}... | collective-permute-start | bytes 442376 | tf_op jit(solution)/shard_map/ppermute | solution.py:265
  225.1 18.0 %collective-permute-start.5 = (bf16[2,32,1152]{2,1,0:T(8,128)(2,1)}, bf16[2,32,1152]{2,1,0:T(8,128)(2,1)S(1)}, u32[]{:S(2)}, u32[]{:S(2)}) collective-permute-start(bf16[2,32,1152]{2,1,0:T(8,128)(2,1)} %get-tuple-element.88), channel_id=1, source_target_pairs={{0,48},{16,0},{32,16},{48,32},{1,49},{17,1},{33,17},{49,33},{2,50}... | collective-permute-start | bytes 442376 | tf_op jit(solution)/shard_map/ppermute | solution.py:265
  243.8 0.8 copy-start.17
  243.8 1.0 copy-start.18
Sparse Core Ops, SparseCore 0:
  54.3 62.6 all-gather.5
  119.6 95.2 all-gather.7

commit v7 on v6

--- a/solution.py
+++ b/solution.py
@@ -112,51 +112,44 @@
     )(old_host, new_host)
 
 
-def copy_picked(plan, *refs):
-    half = len(refs) // 2
-    for taken, kept in zip(refs[:half], refs[half:]):
-        kept[...] = taken[...].reshape(kept.shape)
-
-
-def pick_planes(plan, planes):
-    rows, cols = planes.shape[1:]
-
-    def take(shift):
-        return pl.BlockSpec((1, rows, cols), lambda i, plan: (plan[PLANE_AT + shift], 0, 0))
-
-    return pl.pallas_call(
-        copy_picked,
-        out_shape=[jax.ShapeDtypeStruct((rows, cols), bf16)] * X,
-        grid_spec=pltpu.PrefetchScalarGridSpec(
-            num_scalar_prefetch=1,
-            grid=(1,),
-            in_specs=[take(shift) for shift in range(X)],
-            out_specs=[pl.BlockSpec((rows, cols), lambda i, plan: (0, 0))] * X,
-        ),
+def copy_planes(plan, planes, *refs):
+    done = refs[X]
+    copies = [
+        pltpu.make_async_copy(planes.at[plan[PLANE_AT + shift]], refs[shift], done.at[shift])
+        for shift in range(X)
+    ]
+    for copy in copies:
+        copy.start()
+    for copy in copies:
+        copy.wait()
+
+
+def copy_pieces(plan, pieces, *refs):
+    done = refs[X]
+    copies = [
+        pltpu.make_async_copy(
+            pieces.at[plan[GROUP_AT + shift], :, plan[SLOT_AT + shift]], refs[shift], done.at[shift]
+        )
+        for shift in range(X)
+    ]
+    for copy in copies:
+        copy.start()
+    for copy in copies:
+        copy.wait()
+
+
+def picked(kernel, plan, source, shape):
+    return pl.pallas_call(
+        kernel,
+        out_shape=[jax.ShapeDtypeStruct(shape, bf16)] * X,
+        in_specs=[
+            pl.BlockSpec(memory_space=pltpu.SMEM),
+            pl.BlockSpec(memory_space=pl.ANY),
+        ],
+        out_specs=[pl.BlockSpec(memory_space=pl.ANY)] * X,
+        scratch_shapes=[pltpu.SemaphoreType.DMA((X,))],
         compiler_params=limit(60),
-    )(plan, *[planes] * X)
-
-
-def pick_pieces(plan, pieces):
-    rows, cols = pieces.shape[3:]
-    block = (1, NEAR, 1, rows, cols)
-
-    def take(shift):
-        return pl.BlockSpec(
-            block, lambda i, plan: (plan[GROUP_AT + shift], 0, plan[SLOT_AT + shift], 0, 0)
-        )
-
-    return pl.pallas_call(
-        copy_picked,
-        out_shape=[jax.ShapeDtypeStruct((NEAR, rows, cols), bf16)] * X,
-        grid_spec=pltpu.PrefetchScalarGridSpec(
-            num_scalar_prefetch=1,
-            grid=(1,),
-            in_specs=[take(shift) for shift in range(X)],
-            out_specs=[pl.BlockSpec((NEAR, rows, cols), lambda i, plan: (0, 0, 0))] * X,
-        ),
-        compiler_params=limit(60),
-    )(plan, *[pieces] * X)
+    )(plan, source)
 
 
 def compact(plan, pieces, slots):
@@ -228,36 +221,48 @@
     ]
 
 
-def expert_layer(rows, weights, outs):
-    weight = weights[...].reshape(-1, weights.shape[-1])
-    units = weight.shape[1] // 3
-    projected = jnp.dot(rows[0], weight[:, : 2 * units], preferred_element_type=f32)
-    hidden = (jax.nn.silu(projected[:, :units]) * projected[:, units:]).astype(bf16)
-    produced = lax.dot_general(
-        hidden, weight[:, 2 * units :], (((1,), (1,)), ((), ())), preferred_element_type=f32
-    )
-    outs[...] = produced.reshape(outs.shape).astype(bf16)
+def expert_layer(rows, weights_in, weights_out, outs, hidden):
+    units = weights_out.shape[-1]
+
+    @pl.when(pl.program_id(1) == 0)
+    def _():
+        weight = weights_in[...].reshape(-1, 2 * units)
+        projected = jnp.dot(rows[0], weight, preferred_element_type=f32)
+        hidden[...] = (jax.nn.silu(projected[:, :units]) * projected[:, units:]).astype(bf16)
+
+    @pl.when(pl.program_id(1) == 1)
+    def _():
+        weight = weights_out[...].reshape(-1, units)
+        produced = lax.dot_general(
+            hidden[...], weight, (((1,), (1,)), ((), ())), preferred_element_type=f32
+        )
+        outs[...] = produced.reshape(outs.shape).astype(bf16)
 
 
 def experts(rows, weights, capacity):
     shares, row_count, width = rows.shape
     shards, _, shard_rows, cols = weights.shape
+    units = cols // 3
     return pl.pallas_call(
         expert_layer,
         out_shape=jax.ShapeDtypeStruct((row_count // capacity, shares, capacity, width), bf16),
-        grid=(shares,),
+        grid=(shares, 2),
         in_specs=[
-            pl.BlockSpec((1, row_count, width), lambda j: (j, 0, 0)),
-            pl.BlockSpec((shards, 1, shard_rows, cols), lambda j: (0, j, 0, 0)),
+            pl.BlockSpec((1, row_count, width), lambda j, p: (j, 0, 0)),
+            pl.BlockSpec((shards, 1, shard_rows, 2 * units), lambda j, p: (0, j, 0, 0)),
+            pl.BlockSpec((shards, 1, shard_rows, units), lambda j, p: (0, j, 0, 2)),
         ],
-        out_specs=pl.BlockSpec((row_count // capacity, 1, capacity, width), lambda j: (0, j, 0, 0)),
+        out_specs=pl.BlockSpec(
+            (row_count // capacity, 1, capacity, width), lambda j, p: (0, j, 0, 0)
+        ),
+        scratch_shapes=[pltpu.VMEM((row_count, units), bf16)],
         compiler_params=limit(30),
         cost_estimate=pl.CostEstimate(
             flops=2 * shares * row_count * width * cols,
             bytes_accessed=2 * (weights.size + 2 * rows.size),
-            transcendentals=shares * row_count * cols // 3,
+            transcendentals=shares * row_count * units,
         ),
-    )(rows, weights)
+    )(rows, weights, weights)
 
 
 def shifted(blocks, size):
@@ -305,7 +310,9 @@
     outgoing = jnp.dot(pick, tokens, preferred_element_type=f32).astype(bf16)
     outgoing = outgoing.reshape(Y * CORE * X, SHARE * capacity, width)
     mix = jnp.where(taken, gate[:, None, :], 0.0).reshape(-1, tok_count)
-    mix = mix.astype(bf16)
+    mix_high = mix.astype(bf16)
+    mix_low = (mix - mix_high.astype(f32)).astype(bf16)
+    mix = jnp.concatenate([mix_high, mix_low], axis=1)
     outgoing, factor = lax.optimization_barrier((outgoing, factor))
 
     new_master, new_one, new_two = adamw(master, moment_one, moment_two, gradients, factor)
@@ -322,7 +329,7 @@
     pieces = compacted(plan, pieces)
     pieces = lax.all_gather(pieces.reshape(-1, cols), RING, axis=0, tiled=True)
 
-    held = pick_planes(plan, gathered.reshape(Z, rows, cols))
+    held = picked(copy_planes, plan, gathered.reshape(Z, rows, cols), (rows, cols))
     masters = [held[0]] + shifted(held[1:], X)
 
     weights = swap(gathered.reshape(Y * CORE, SHARE * rows, cols), DP)
@@ -335,11 +342,13 @@
     results, late_plan = lax.optimization_barrier((results, plan))
     returned = swap(results, PLANE).reshape(-1, width)
 
-    held = pick_pieces(late_plan, pieces.reshape(Z // NEAR, NEAR, SLOTS, 2 * piece, cols))
+    pieces = pieces.reshape(Z // NEAR, NEAR, SLOTS, 2 * piece, cols)
+    held = picked(copy_pieces, late_plan, pieces, (NEAR, 2 * piece, cols))
     arrived = [held[0]] + shifted(held[1:], X)
     returned, arrived[0] = lax.optimization_barrier((returned, arrived[0]))
     contract = (((0,), (0,)), ((), ()))
-    mixed = lax.dot_general(mix, returned, contract, preferred_element_type=f32).astype(bf16)
+    mixed = lax.dot_general(mix, returned, contract, preferred_element_type=f32)
+    mixed = (mixed[:tok_count] + mixed[tok_count:]).astype(bf16)
     mixed, arrived = lax.optimization_barrier((mixed, arrived))
     moments = finished(plan, arrived, new_one, new_two)
     moments = lax.cond(

time: 253 us -> 258 us (1.020)
  Pallas kernels: 20.8 us -> 72.1 us
  waiting for transfers between devices: 87.2 us -> 38.4 us
    pallas_call x2, Pallas kernels: 5.55 us -> 57.2 us  [picked(): pl.pallas_call(kernel, out_shape=[jax.ShapeDtypeStruct(shape, bf16)] * X,...]
    all_to_all x5, waiting for transfers between devices: 64.8 us -> 25.8 us  [swap(): return lax.all_to_all(array, axes, split_axis=0, concat_axis=0, tiled=True)]
    all_gather x1, waiting for transfers between devices: 10.9 us -> 4.6 us  [per_device(): pieces = lax.all_gather(pieces.reshape(-1, cols), RING, axis=0, tiled=True)]
    ppermute x6, waiting for transfers between devices: 11.5 us -> 7.94 us  [shifted(): lax.ppermute(block, 'x', [(i, (i + shift) % size) for i in range(size)])]
  transfers between devices with their start and end apart: 13 -> 13, of which waited for: 9 -> 6; matrix products, arithmetic and copies ran while one was open for 6% -> 6% of each run, Pallas kernels for 7% -> 27%
where the time goes in v7:
time: 258 us; the launch traced here: 257 us
  Pallas kernels  72.1 us (28%)
  starting transfers between devices  62.2 us (24%)
  blocking collectives  46.9 us (18%)
  waiting for transfers between devices  38.4 us (15%)
  between operations  18.4 us (7%)
  other arithmetic  8.25 us (3%)
  matrix products  5.76 us (2%)
  local copies, waits for them, and re-layouts  5.06 us (2%)
    pallas_call x2, Pallas kernels, picked(): pl.pallas_call(kernel, out_shape=[jax.ShapeDtypeStruct(shape, bf16)] * X,...  57.2 us
    all_to_all x1, blocking collectives, swap(): return lax.all_to_all(array, axes, split_axis=0, concat_axis=0, tiled=True)  46.9 us
    all_to_all x5, starting transfers between devices, swap(): return lax.all_to_all(array, axes, split_axis=0, concat_axis=0, tiled=True)  41.4 us
    all_to_all x5, waiting for transfers between devices, swap(): return lax.all_to_all(array, axes, split_axis=0, concat_axis=0, tiled=True)  25.8 us
    ppermute x6, starting transfers between devices, shifted(): lax.ppermute(block, 'x', [(i, (i + shift) % size) for i in range(size)])  20.7 us
    pallas_call x1, Pallas kernels, experts(): pl.pallas_call(expert_layer, out_shape=jax.ShapeDtypeStruct((row_count //...  8.45 us
    ppermute x6, waiting for transfers between devices, shifted(): lax.ppermute(block, 'x', [(i, (i + shift) % size) for i in range(size)])  7.94 us
  transfers between devices with their start and end apart: 13, of which 6 were waited for; matrix products, arithmetic and copies ran while one was open for 6% of the time, Pallas kernels for 27%

profile of v7, /device:TPU:1, one launch (start us, length us, event | category | flops | bytes accessed | tf_op | source)
XLA Modules:
  0.0 257.1 jit_solution(4191717694021061956)
XLA Ops:
  7.2 0.0 copy-start
  7.2 0.0 copy-start.1
  7.2 1.0 copy-done.1
  8.2 0.9 shard_map.121
  9.1 10.4 %all-to-all-start.2 = ((f32[32,1,128]{2,1,0:T(1,128)}), f32[32,1,128]{2,1,0:T(1,128)S(1)}, u32[]{:S(2)}, u32[]{:S(2)}) async-start(f32[32,1,128]{2,1,0:T(1,128)} %shard_map.121), calls=%async_computation.2 | async-start | bytes 32768 | tf_op jit(solution)/shard_map/all_to_all | solution.py:36
  19.5 0.7 fusion.14
  20.1 0.8 select_reduce_fusion.2
  20.9 0.1 fusion.13
  21.0 0.1 convolution_select_fusion
  21.2 0.1 eq.86
  21.3 0.3 bitcast_compare_fusion
  21.6 4.9 %all-to-all-done.2.values = f32[32,1,128]{2,1,0:T(1,128)S(1)} async-done(((f32[32,1,128]{2,1,0:T(1,128)}), f32[32,1,128]{2,1,0:T(1,128)S(1)}, u32[]{:S(2)}, u32[]{:S(2)}) %all-to-all-start.2) | async-done | bytes 16416 | tf_op jit(solution)/shard_map/all_to_all | solution.py:36
  26.4 0.6 shard_map.122
  27.0 13.0 %all-to-all-start.3 = ((f32[16,1,128]{2,1,0:T(1,128)}), f32[16,1,128]{2,1,0:T(1,128)S(1)}, u32[]{:S(2)}, u32[]{:S(2)}) async-start(f32[16,1,128]{2,1,0:T(1,128)} %shard_map.122), calls=%async_computation.3 | async-start | bytes 16384 | tf_op jit(solution)/shard_map/all_to_all | solution.py:36
  40.1 0.0 all-gather.6.cloned.1.call-start
  40.1 2.6 %convolution_convert_fusion = bf16[1536,1024]{1,0:T(8,128)(2,1)} fusion(pred[1536,128]{1,0:T(32,128)(4,1)S(1)} %bitcast_compare_fusion, bf16[128,1024]{1,0:T(8,128)(2,1)S(1)} %copy-done), kind=kOutput, calls=%fused_computation.18 | convolution fusion | flops 404226048 | bytes 3604480 | tf_op jit(solution)/shard_map/dot_general | solution.py:310
  42.8 8.5 %all-to-all-done.3 = f32[16,1,128]{2,1,0:T(1,128)S(1)} async-done(((f32[16,1,128]{2,1,0:T(1,128)}), f32[16,1,128]{2,1,0:T(1,128)S(1)}, u32[]{:S(2)}, u32[]{:S(2)}) %all-to-all-start.3) | async-done | bytes 8224 | tf_op jit(solution)/shard_map/all_to_all | solution.py:36
  51.3 0.6 slice_reduce_fusion
  52.7 1.4 fusion.16
  54.1 0.0 all-gather.6.cloned.1.call-update
  54.2 1.0 pad_maximum_fusion.1
  55.3 3.5 %all-to-all-start.5 = ((bf16[8,32,1152]{2,1,0:T(8,128)(2,1)}), bf16[8,32,1152]{2,1,0:T(8,128)(2,1)S(1)}, u32[]{:S(2)}, u32[]{:S(2)}) async-start(bf16[8,32,1152]{2,1,0:T(8,128)(2,1)} %pad_maximum_fusion.1), calls=%async_computation.5 | async-start | bytes 1179648 | tf_op jit(solution)/shard_map/all_to_all | solution.py:36
  58.8 0.0 all-gather.8.cloned.1.call-start
  58.9 3.0 %shard_map.120.plan = s32[32]{0:T(128)S(1)} custom-call(s32[64]{0:T(128)S(1)} %copy-done.19, s32[64]{0:T(128)S(1)} %copy-done.20), custom_call_target="tpu_custom_call" | custom-call | tf_op jit(solution)/shard_map/pallas_call | solution.py:105
  61.9 12.4 %all-to-all-done.5.pieces = bf16[8,32,1152]{2,1,0:T(8,128)(2,1)S(1)} async-done(((bf16[8,32,1152]{2,1,0:T(8,128)(2,1)}), bf16[8,32,1152]{2,1,0:T(8,128)(2,1)S(1)}, u32[]{:S(2)}, u32[]{:S(2)}) %all-to-all-start.5) | async-done | bytes 589856 | tf_op jit(solution)/shard_map/all_to_all | solution.py:36
  74.3 1.3 shard_map.125
  75.6 0.0 all-gather.8.cloned.1.call-update
  75.7 46.9 %all_to_all.39 = bf16[32,48,1024]{2,1,0:T(8,128)(2,1)} all-to-all(bf16[32,48,1024]{2,1,0:T(8,128)(2,1)} %bitcast.106), channel_id=1, replica_groups=mesh['y'=4,'c'=2,'x'=4,'far'=8,'near'=2] {'y','c','x'}, dimensions={0} | all-to-all | bytes 6291456 | tf_op jit(solution)/shard_map/all_to_all | solution.py:36
  122.6 6.2 %all-to-all-start.4 = ((bf16[8,256,1152]{2,1,0:T(8,128)(2,1)}), bf16[8,256,1152]{2,1,0:T(8,128)(2,1)}, u32[]{:S(2)}, u32[]{:S(2)}) async-start(bf16[8,256,1152]{2,1,0:T(8,128)(2,1)} %bitcast.104), calls=%async_computation.4 | async-start | bytes 9437184 | tf_op jit(solution)/shard_map/all_to_all | solution.py:36
  128.8 37.5 %shard_map.123 = (bf16[128,1152]{1,0:T(8,128)(2,1)}, bf16[128,1152]{1,0:T(8,128)(2,1)}, bf16[128,1152]{1,0:T(8,128)(2,1)}, bf16[128,1152]{1,0:T(8,128)(2,1)}) custom-call(s32[32]{0:T(128)} %copy-done.4, bf16[16,128,1152]{2,1,0:T(8,128)(2,1)} %bitcast.105), custom_call_target="tpu_custom_call" | custom-call | tf_op jit(solution)/shard_map/pallas_call | solution.py:142
  166.3 2.8 %collective-permute-start = (bf16[128,1152]{1,0:T(8,128)(2,1)}, bf16[128,1152]{1,0:T(8,128)(2,1)}, u32[]{:S(2)}, u32[]{:S(2)}) collective-permute-start(bf16[128,1152]{1,0:T(8,128)(2,1)} %get-tuple-element.67), channel_id=1, source_target_pairs={{0,16},{16,32},{32,48},{48,0},{1,17},{17,33},{33,49},{49,1},{2,18}... | collective-permute-start | bytes 884744 | tf_op jit(solution)/shard_map/ppermute | solution.py:270
  169.2 4.5 %collective-permute-start.1 = (bf16[128,1152]{1,0:T(8,128)(2,1)}, bf16[128,1152]{1,0:T(8,128)(2,1)}, u32[]{:S(2)}, u32[]{:S(2)}) collective-permute-start(bf16[128,1152]{1,0:T(8,128)(2,1)} %get-tuple-element.68), channel_id=1, source_target_pairs={{0,32},{16,48},{32,0},{48,16},{1,33},{17,49},{33,1},{49,17},{2,34}... | collective-permute-start | bytes 884744 | tf_op jit(solution)/shard_map/ppermute | solution.py:270
  173.6 2.9 %collective-permute-start.2 = (bf16[128,1152]{1,0:T(8,128)(2,1)}, bf16[128,1152]{1,0:T(8,128)(2,1)}, u32[]{:S(2)}, u32[]{:S(2)}) collective-permute-start(bf16[128,1152]{1,0:T(8,128)(2,1)} %get-tuple-element.69), channel_id=1, source_target_pairs={{0,48},{16,0},{32,16},{48,32},{1,49},{17,1},{33,17},{49,33},{2,50}... | collective-permute-start | bytes 884744 | tf_op jit(solution)/shard_map/ppermute | solution.py:270
  176.6 2.2 copy.21
  178.8 0.0 collective-permute-done
  178.8 6.5 %collective-permute-done.1 = bf16[128,1152]{1,0:T(8,128)(2,1)} collective-permute-done((bf16[128,1152]{1,0:T(8,128)(2,1)}, bf16[128,1152]{1,0:T(8,128)(2,1)}, u32[]{:S(2)}, u32[]{:S(2)}) %collective-permute-start.1) | collective-permute-done | bytes 294944 | tf_op jit(solution)/shard_map/ppermute | solution.py:270
  185.3 1.4 collective-permute-done.2
  186.7 0.0 all-to-all-done.4
  186.8 8.4 %shard_map.124 = bf16[32,2,24,1024]{3,2,1,0:T(8,128)(2,1)} custom-call(bf16[2,768,1024]{2,1,0:T(8,128)(2,1)S(1)} %bitcast.102, bf16[8,2,128,1152]{3,2,1,0:T(8,128)(2,1)} %bitcast.47.weights_in.weights_out, bf16[8,2,128,1152]{3,2,1,0:T(8,128)(2,1)} %bitcast.47.weights_in.weights_out), custom_call_target="tpu_custom_call" | custom-call | flops 3623878656 | bytes 11010048 | tf_op jit(solution)/shard_map/pallas_call | solution.py:246
  195.2 0.0 copy-start.15
  195.2 8.2 %all-to-all-start.7 = ((bf16[32,48,1024]{2,1,0:T(8,128)(2,1)}), bf16[32,48,1024]{2,1,0:T(8,128)(2,1)}, u32[]{:S(2)}, u32[]{:S(2)}) async-start(bf16[32,48,1024]{2,1,0:T(8,128)(2,1)} %bitcast.48), calls=%async_computation.7 | async-start | bytes 6291456 | tf_op jit(solution)/shard_map/all_to_all | solution.py:36
  203.4 0.1 select_reduce_fusion.1
  203.5 0.3 fusion.8
  203.8 0.3 fusion.7
  204.1 0.7 fusion.21
  208.0 1.9 select_bitcast_fusion
  209.9 4.6 %all-gather.8.cloned.1.call-done = bf16[3072,1152]{1,0:T(8,128)(2,1)} async-done(((bf16[192,1152]{1,0:T(8,128)(2,1)}), bf16[3072,1152]{1,0:T(8,128)(2,1)}) %all-gather.8.cloned.1.call-update) | async-done | bytes 7077904 | tf_op jit(solution)/shard_map/all_gather | solution.py:330
  214.5 19.7 %shard_map.126 = (bf16[2,32,1152]{2,1,0:T(8,128)(2,1)}, bf16[2,32,1152]{2,1,0:T(8,128)(2,1)}, bf16[2,32,1152]{2,1,0:T(8,128)(2,1)}, bf16[2,32,1152]{2,1,0:T(8,128)(2,1)}) custom-call(s32[32]{0:T(128)} %copy-done.4, bf16[8,2,6,32,1152]{4,3,2,1,0:T(8,128)(2,1)} %bitcast.108), custom_call_target="tpu_custom_call" | custom-call | tf_op jit(solution)/shard_map/pallas_call | solution.py:142
  234.2 3.1 %collective-permute-start.3 = (bf16[2,32,1152]{2,1,0:T(8,128)(2,1)}, bf16[2,32,1152]{2,1,0:T(8,128)(2,1)S(1)}, u32[]{:S(2)}, u32[]{:S(2)}) collective-permute-start(bf16[2,32,1152]{2,1,0:T(8,128)(2,1)} %get-tuple-element.86), channel_id=1, source_target_pairs={{0,16},{16,32},{32,48},{48,0},{1,17},{17,33},{33,49},{49,1},{2,18}... | collective-permute-start | bytes 442376 | tf_op jit(solution)/shard_map/ppermute | solution.py:270
  237.3 4.3 %collective-permute-start.4 = (bf16[2,32,1152]{2,1,0:T(8,128)(2,1)}, bf16[2,32,1152]{2,1,0:T(8,128)(2,1)S(1)}, u32[]{:S(2)}, u32[]{:S(2)}) collective-permute-start(bf16[2,32,1152]{2,1,0:T(8,128)(2,1)} %get-tuple-element.87), channel_id=1, source_target_pairs={{0,32},{16,48},{32,0},{48,16},{1,33},{17,49},{33,1},{49,17},{2,34}... | collective-permute-start | bytes 442376 | tf_op jit(solution)/shard_map/ppermute | solution.py:270
  241.6 3.1 %collective-permute-start.5 = (bf16[2,32,1152]{2,1,0:T(8,128)(2,1)}, bf16[2,32,1152]{2,1,0:T(8,128)(2,1)S(1)}, u32[]{:S(2)}, u32[]{:S(2)}) collective-permute-start(bf16[2,32,1152]{2,1,0:T(8,128)(2,1)} %get-tuple-element.88), channel_id=1, source_target_pairs={{0,48},{16,0},{32,16},{48,32},{1,49},{17,1},{33,17},{49,33},{2,50}... | collective-permute-start | bytes 442376 | tf_op jit(solution)/shard_map/ppermute | solution.py:270
  244.7 0.0 all-to-all-done.7
  244.7 0.0 copy-start.3
  244.8 0.0 copy-start.21
  244.8 3.0 %fusion.2 = f32[256,1024]{1,0:T(8,128)S(1)} fusion(bf16[1536,1024]{1,0:T(8,128)(2,1)} %bitcast.49, bf16[1536,128]{1,0:T(8,128)(2,1)S(1)} %fusion.8, bf16[1536,128]{1,0:T(8,128)(2,1)S(1)} %fusion.7), kind=kOutput, calls=%fused_computation.21 | convolution fusion | flops 806879232 | bytes 4980736 | tf_op jit(solution)/shard_map/dot_general | solution.py:350
  247.8 0.8 fusion.12
  248.5 0.0 collective-permute-done.3.one
  248.5 0.0 collective-permute-done.4.two
  248.5 0.0 collective-permute-done.5.three
  248.6 0.6 shard_map.127
  249.3 0.0 copy-start.17
  249.3 0.0 copy-start.18
  249.3 0.8 copy-done.17
  250.1 0.2 copy-done.18
  (40 shorter events, 0.2 us)
Async XLA Ops:
  7.2 33.0 %copy-start = (bf16[128,1024]{1,0:T(8,128)(2,1)S(1)}, bf16[128,1024]{1,0:T(8,128)(2,1)}, u32[]{:S(2)}) copy-start(bf16[128,1024]{1,0:T(8,128)(2,1)} %param.17) | copy-start | bytes 786436
  7.2 1.0 copy-start.1
  8.2 44.5 %copy-start.2 = (bf16[1,128,1152]{2,1,0:T(8,128)(2,1)S(1)}, bf16[1,128,1152]{2,1,0:T(8,128)(2,1)}, u32[]{:S(2)}) copy-start(bf16[1,128,1152]{2,1,0:T(8,128)(2,1)} %param.14) | copy-start | bytes 884740
  8.2 44.5 %copy-start.12 = (f32[1,128,1152]{2,1,0:T(8,128)S(1)}, f32[1,128,1152]{2,1,0:T(8,128)}, u32[]{:S(2)}) copy-start(f32[1,128,1152]{2,1,0:T(8,128)} %param.11) | copy-start | bytes 1769476
  8.2 44.5 %copy-start.13 = (f32[1,128,1152]{2,1,0:T(8,128)S(1)}, f32[1,128,1152]{2,1,0:T(8,128)}, u32[]{:S(2)}) copy-start(f32[1,128,1152]{2,1,0:T(8,128)} %param.12) | copy-start | bytes 1769476
  8.2 44.5 %copy-start.14 = (f32[1,128,1152]{2,1,0:T(8,128)S(1)}, f32[1,128,1152]{2,1,0:T(8,128)}, u32[]{:S(2)}) copy-start(f32[1,128,1152]{2,1,0:T(8,128)} %param.13) | copy-start | bytes 1769476
  9.1 17.3 %all-to-all-start.2 = ((f32[32,1,128]{2,1,0:T(1,128)}), f32[32,1,128]{2,1,0:T(1,128)S(1)}, u32[]{:S(2)}, u32[]{:S(2)}) async-start(f32[32,1,128]{2,1,0:T(1,128)} %shard_map.121), calls=%async_computation.2 | async-start | bytes 32768 | tf_op jit(solution)/shard_map/all_to_all | solution.py:36
  27.0 24.3 %all-to-all-start.3 = ((f32[16,1,128]{2,1,0:T(1,128)}), f32[16,1,128]{2,1,0:T(1,128)S(1)}, u32[]{:S(2)}, u32[]{:S(2)}) async-start(f32[16,1,128]{2,1,0:T(1,128)} %shard_map.122), calls=%async_computation.3 | async-start | bytes 16384 | tf_op jit(solution)/shard_map/all_to_all | solution.py:36
  40.1 82.5 %all-gather.6.cloned.1.call-start = ((), (), s32[]{:S(2)}) async-start(), calls=%async_computation.9 | async-start | bytes 5013504 | tf_op jit(solution)/shard_map/all_gather | solution.py:322
  54.1 1.1 copy-start.7
  54.1 68.4 %copy-start.9 = (f32[128,1152]{1,0:T(8,128)}, f32[128,1152]{1,0:T(8,128)S(1)}, u32[]{:S(2)}) copy-start(f32[128,1152]{1,0:T(8,128)S(1)} %get-tuple-element.76.own_two) | copy-start | bytes 1769476
  54.1 4.7 %copy-start.19 = (s32[64]{0:T(128)S(1)}, s32[64]{0:T(128)}, u32[]{:S(2)}) copy-start(s32[64]{0:T(128)} %old_host.1) | copy-start | bytes 772
  54.1 4.7 %copy-start.20 = (s32[64]{0:T(128)S(1)}, s32[64]{0:T(128)}, u32[]{:S(2)}) copy-start(s32[64]{0:T(128)} %new_host.1) | copy-start | bytes 772
  55.3 19.0 %all-to-all-start.5 = ((bf16[8,32,1152]{2,1,0:T(8,128)(2,1)}), bf16[8,32,1152]{2,1,0:T(8,128)(2,1)S(1)}, u32[]{:S(2)}, u32[]{:S(2)}) async-start(bf16[8,32,1152]{2,1,0:T(8,128)(2,1)} %pad_maximum_fusion.1), calls=%async_computation.5 | async-start | bytes 1179648 | tf_op jit(solution)/shard_map/all_to_all | solution.py:36
  58.8 155.7 %all-gather.8.cloned.1.call-start = ((), (), s32[]{:S(2)}) async-start(), calls=%async_computation.10 | async-start | bytes 7520256 | tf_op jit(solution)/shard_map/all_gather | solution.py:330
  61.8 60.7 %copy-start.4 = (s32[32]{0:T(128)}, s32[32]{0:T(128)S(1)}, u32[]{:S(2)}) copy-start(s32[32]{0:T(128)S(1)} %shard_map.120.plan) | copy-start | bytes 388
  122.6 64.2 %all-to-all-start.4 = ((bf16[8,256,1152]{2,1,0:T(8,128)(2,1)}), bf16[8,256,1152]{2,1,0:T(8,128)(2,1)}, u32[]{:S(2)}, u32[]{:S(2)}) async-start(bf16[8,256,1152]{2,1,0:T(8,128)(2,1)} %bitcast.104), calls=%async_computation.4 | async-start | bytes 9437184 | tf_op jit(solution)/shard_map/all_to_all | solution.py:36
  166.3 12.5 %collective-permute-start = (bf16[128,1152]{1,0:T(8,128)(2,1)}, bf16[128,1152]{1,0:T(8,128)(2,1)}, u32[]{:S(2)}, u32[]{:S(2)}) collective-permute-start(bf16[128,1152]{1,0:T(8,128)(2,1)} %get-tuple-element.67), channel_id=1, source_target_pairs={{0,16},{16,32},{32,48},{48,0},{1,17},{17,33},{33,49},{49,1},{2,18}... | collective-permute-start | bytes 884744 | tf_op jit(solution)/shard_map/ppermute | solution.py:270
  169.2 16.2 %collective-permute-start.1 = (bf16[128,1152]{1,0:T(8,128)(2,1)}, bf16[128,1152]{1,0:T(8,128)(2,1)}, u32[]{:S(2)}, u32[]{:S(2)}) collective-permute-start(bf16[128,1152]{1,0:T(8,128)(2,1)} %get-tuple-element.68), channel_id=1, source_target_pairs={{0,32},{16,48},{32,0},{48,16},{1,33},{17,49},{33,1},{49,17},{2,34}... | collective-permute-start | bytes 884744 | tf_op jit(solution)/shard_map/ppermute | solution.py:270
  173.6 13.1 %collective-permute-start.2 = (bf16[128,1152]{1,0:T(8,128)(2,1)}, bf16[128,1152]{1,0:T(8,128)(2,1)}, u32[]{:S(2)}, u32[]{:S(2)}) collective-permute-start(bf16[128,1152]{1,0:T(8,128)(2,1)} %get-tuple-element.69), channel_id=1, source_target_pairs={{0,48},{16,0},{32,16},{48,32},{1,49},{17,1},{33,17},{49,33},{2,50}... | collective-permute-start | bytes 884744 | tf_op jit(solution)/shard_map/ppermute | solution.py:270
  195.2 8.2 %copy-start.16 = (f32[128,8]{0,1:T(8,128)S(1)}, f32[128,8]{0,1:T(8,128)}, u32[]{:S(2)}) copy-start(f32[128,8]{0,1:T(8,128)} %param.19) | copy-start | bytes 12292
  195.2 8.9 %copy-start.5 = (s32[32]{0:T(128)S(1)}, s32[32]{0:T(128)}, u32[]{:S(2)}) copy-start(s32[32]{0:T(128)} %copy-done.4) | copy-start | bytes 388
  195.2 12.8 %copy-start.11 = (f32[128,1152]{1,0:T(8,128)S(1)}, f32[128,1152]{1,0:T(8,128)}, u32[]{:S(2)}) copy-start(f32[128,1152]{1,0:T(8,128)} %get-tuple-element.74) | copy-start | bytes 1769476
  195.2 12.8 %copy-start.15 = (bf16[128,1152]{1,0:T(8,128)(2,1)S(1)}, bf16[128,1152]{1,0:T(8,128)(2,1)}, u32[]{:S(2)}) copy-start(bf16[128,1152]{1,0:T(8,128)(2,1)} %get-tuple-element.70) | copy-start | bytes 884740
  195.2 49.5 %all-to-all-start.7 = ((bf16[32,48,1024]{2,1,0:T(8,128)(2,1)}), bf16[32,48,1024]{2,1,0:T(8,128)(2,1)}, u32[]{:S(2)}, u32[]{:S(2)}) async-start(bf16[32,48,1024]{2,1,0:T(8,128)(2,1)} %bitcast.48), calls=%async_computation.7 | async-start | bytes 6291456 | tf_op jit(solution)/shard_map/all_to_all | solution.py:36
  234.2 14.3 %collective-permute-start.3 = (bf16[2,32,1152]{2,1,0:T(8,128)(2,1)}, bf16[2,32,1152]{2,1,0:T(8,128)(2,1)S(1)}, u32[]{:S(2)}, u32[]{:S(2)}) collective-permute-start(bf16[2,32,1152]{2,1,0:T(8,128)(2,1)} %get-tuple-element.86), channel_id=1, source_target_pairs={{0,16},{16,32},{32,48},{48,0},{1,17},{17,33},{33,49},{49,1},{2,18}... | collective-permute-start | bytes 442376 | tf_op jit(solution)/shard_map/ppermute | solution.py:270
  237.3 11.2 %collective-permute-start.4 = (bf16[2,32,1152]{2,1,0:T(8,128)(2,1)}, bf16[2,32,1152]{2,1,0:T(8,128)(2,1)S(1)}, u32[]{:S(2)}, u32[]{:S(2)}) collective-permute-start(bf16[2,32,1152]{2,1,0:T(8,128)(2,1)} %get-tuple-element.87), channel_id=1, source_target_pairs={{0,32},{16,48},{32,0},{48,16},{1,33},{17,49},{33,1},{49,17},{2,34}... | collective-permute-start | bytes 442376 | tf_op jit(solution)/shard_map/ppermute | solution.py:270
  241.6 6.9 %collective-permute-start.5 = (bf16[2,32,1152]{2,1,0:T(8,128)(2,1)}, bf16[2,32,1152]{2,1,0:T(8,128)(2,1)S(1)}, u32[]{:S(2)}, u32[]{:S(2)}) collective-permute-start(bf16[2,32,1152]{2,1,0:T(8,128)(2,1)} %get-tuple-element.88), channel_id=1, source_target_pairs={{0,48},{16,0},{32,16},{48,32},{1,49},{17,1},{33,17},{49,33},{2,50}... | collective-permute-start | bytes 442376 | tf_op jit(solution)/shard_map/ppermute | solution.py:270
  244.7 3.8 %copy-start.3 = (bf16[2,32,1152]{2,1,0:T(8,128)(2,1)S(1)}, bf16[2,32,1152]{2,1,0:T(8,128)(2,1)}, u32[]{:S(2)}) copy-start(bf16[2,32,1152]{2,1,0:T(8,128)(2,1)} %get-tuple-element.89.here) | copy-start | bytes 442372
  244.7 3.8 %copy-start.6 = (s32[32]{0:T(128)S(1)}, s32[32]{0:T(128)}, u32[]{:S(2)}) copy-start(s32[32]{0:T(128)} %copy-done.4) | copy-start | bytes 388
  244.7 3.8 %copy-start.8 = (f32[128,1152]{1,0:T(8,128)S(1)}, f32[128,1152]{1,0:T(8,128)}, u32[]{:S(2)}) copy-start(f32[128,1152]{1,0:T(8,128)} %copy-done.7) | copy-start | bytes 1769476
  244.8 3.8 %copy-start.10 = (f32[128,1152]{1,0:T(8,128)S(1)}, f32[128,1152]{1,0:T(8,128)}, u32[]{:S(2)}) copy-start(f32[128,1152]{1,0:T(8,128)} %copy-done.9) | copy-start | bytes 1769476
  244.8 4.5 %copy-start.21 = (s32[64]{0:T(128)S(1)}, s32[64]{0:T(128)}, u32[]{:S(2)}) copy-start(s32[64]{0:T(128)} %new_host.1) | copy-start | bytes 772
  249.3 0.8 copy-start.17
  249.3 1.0 copy-start.18
Sparse Core Ops, SparseCore 0:
  54.3 62.0 all-gather.5
  119.1 95.4 all-gather.7

commit v8 on v7

--- a/solution.py
+++ b/solution.py
@@ -15,6 +15,7 @@
 Y, CORE, X, Z = 4, 2, 4, 16
 NEAR = 2
 SLOTS = 6
+SHIFTS = (0, 2, 1, 3)
 DP = ("y", "c")
 PLANE = ("y", "c", "x")
 RING = ("far", "near")
@@ -115,8 +116,8 @@
 def copy_planes(plan, planes, *refs):
     done = refs[X]
     copies = [
-        pltpu.make_async_copy(planes.at[plan[PLANE_AT + shift]], refs[shift], done.at[shift])
-        for shift in range(X)
+        pltpu.make_async_copy(planes.at[plan[PLANE_AT + shift]], refs[i], done.at[i])
+        for i, shift in enumerate(SHIFTS)
     ]
     for copy in copies:
         copy.start()
@@ -128,9 +129,9 @@
     done = refs[X]
     copies = [
         pltpu.make_async_copy(
-            pieces.at[plan[GROUP_AT + shift], :, plan[SLOT_AT + shift]], refs[shift], done.at[shift]
+            pieces.at[plan[GROUP_AT + shift], :, plan[SLOT_AT + shift]], refs[i], done.at[i]
         )
-        for shift in range(X)
+        for i, shift in enumerate(SHIFTS)
     ]
     for copy in copies:
         copy.start()
@@ -146,7 +147,7 @@
             pl.BlockSpec(memory_space=pltpu.SMEM),
             pl.BlockSpec(memory_space=pl.ANY),
         ],
-        out_specs=[pl.BlockSpec(memory_space=pl.ANY)] * X,
+        out_specs=[pl.BlockSpec(memory_space=pltpu.VMEM)] * X,
         scratch_shapes=[pltpu.SemaphoreType.DMA((X,))],
         compiler_params=limit(60),
     )(plan, source)
@@ -177,7 +178,7 @@
 
     @pl.when(plan[MOVED] == 1)
     def _():
-        for shift, quarter in enumerate((here, one, two, three)):
+        for shift, quarter in zip(SHIFTS, (here, one, two, three)):
             at = lax.rem(plan[MY_X] + X - shift, X) * NEAR
             for near in range(NEAR):
                 piece = quarter[near].astype(f32)
@@ -265,11 +266,11 @@
     )(rows, weights, weights)
 
 
-def shifted(blocks, size):
-    return [
-        lax.ppermute(block, "x", [(i, (i + shift) % size) for i in range(size)])
-        for shift, block in enumerate(blocks, 1)
-    ]
+def shifted(blocks):
+    arrived = blocks[:1]
+    for block, shift in zip(blocks[1:], SHIFTS[1:]):
+        arrived.append(lax.ppermute(block, "x", [(i, (i + shift) % X) for i in range(X)]))
+    return arrived
 
 
 def per_device(
@@ -330,12 +331,12 @@
     pieces = lax.all_gather(pieces.reshape(-1, cols), RING, axis=0, tiled=True)
 
     held = picked(copy_planes, plan, gathered.reshape(Z, rows, cols), (rows, cols))
-    masters = [held[0]] + shifted(held[1:], X)
+    masters = shifted(list(held))
 
     weights = swap(gathered.reshape(Y * CORE, SHARE * rows, cols), DP)
     weights, masters = lax.optimization_barrier((weights, masters))
     moved = plan[MOVED] == 1
-    moved_master = lax.select_n(plan[BACK], *masters).astype(f32)
+    moved_master = lax.select_n(plan[BACK], *[masters[SHIFTS.index(shift)] for shift in range(X)]).astype(f32)
     weights = weights.reshape(Y * CORE, SHARE, rows, cols)
     inputs = received.reshape(-1, SHARE, capacity, width).transpose(1, 0, 2, 3)
     results = experts(inputs.reshape(SHARE, -1, width), weights, capacity).reshape(received.shape)
@@ -344,7 +345,7 @@
 
     pieces = pieces.reshape(Z // NEAR, NEAR, SLOTS, 2 * piece, cols)
     held = picked(copy_pieces, late_plan, pieces, (NEAR, 2 * piece, cols))
-    arrived = [held[0]] + shifted(held[1:], X)
+    arrived = shifted(list(held))
     returned, arrived[0] = lax.optimization_barrier((returned, arrived[0]))
     contract = (((0,), (0,)), ((), ()))
     mixed = lax.dot_general(mix, returned, contract, preferred_element_type=f32)

time: 258 us -> 251 us (0.973)
  Pallas kernels: 72.1 us -> 20.6 us
  waiting for transfers between devices: 38.4 us -> 84.1 us
    pallas_call x2, Pallas kernels: 57.2 us -> 5.69 us  [picked(): pl.pallas_call(kernel, out_shape=[jax.ShapeDtypeStruct(shape, bf16)] * X,...]
    all_to_all x5, waiting for transfers between devices: 25.8 us -> 65.6 us  [swap(): return lax.all_to_all(array, axes, split_axis=0, concat_axis=0, tiled=True)]
    all_gather x1, waiting for transfers between devices: 4.6 us -> 10.4 us  [per_device(): pieces = lax.all_gather(pieces.reshape(-1, cols), RING, axis=0, tiled=True)]
  transfers between devices with their start and end apart: 13 -> 13, of which waited for: 6 -> 9; matrix products, arithmetic and copies ran while one was open for 6% -> 6% of each run, Pallas kernels for 27% -> 7%
where the time goes in v8:
time: 251 us; the launch traced here: 250 us
  waiting for transfers between devices  84.1 us (34%)
  starting transfers between devices  61 us (24%)
  blocking collectives  46.9 us (19%)
  Pallas kernels  20.6 us (8%)
  between operations  18.4 us (7%)
  other arithmetic  8.26 us (3%)
  matrix products  5.77 us (2%)
  local copies, waits for them, and re-layouts  5.04 us (2%)
    all_to_all x5, waiting for transfers between devices, swap(): return lax.all_to_all(array, axes, split_axis=0, concat_axis=0, tiled=True)  65.6 us
    all_to_all x1, blocking collectives, swap(): return lax.all_to_all(array, axes, split_axis=0, concat_axis=0, tiled=True)  46.9 us
    all_to_all x5, starting transfers between devices, swap(): return lax.all_to_all(array, axes, split_axis=0, concat_axis=0, tiled=True)  38.9 us
    ppermute x6, starting transfers between devices, shifted(): lax.ppermute(block, 'x', [(i, (i + shift) % X) for i in range(X)])  22 us
    all_gather x1, waiting for transfers between devices, per_device(): pieces = lax.all_gather(pieces.reshape(-1, cols), RING, axis=0, tiled=True)  10.4 us
    pallas_call x1, Pallas kernels, experts(): pl.pallas_call(expert_layer, out_shape=jax.ShapeDtypeStruct((row_count //...  8.44 us
    ppermute x6, waiting for transfers between devices, shifted(): lax.ppermute(block, 'x', [(i, (i + shift) % X) for i in range(X)])  8.04 us
    pallas_call x2, Pallas kernels, picked(): pl.pallas_call(kernel, out_shape=[jax.ShapeDtypeStruct(shape, bf16)] * X,...  5.69 us
  transfers between devices with their start and end apart: 13, of which 9 were waited for; matrix products, arithmetic and copies ran while one was open for 6% of the time, Pallas kernels for 7%

profile of v8, /device:TPU:1, one launch (start us, length us, event | category | flops | bytes accessed | tf_op | source)
XLA Modules:
  0.0 250.0 jit_solution(5383731124405162251)
XLA Ops:
  7.2 0.0 copy-start
  7.2 1.0 copy-done.1
  8.2 0.9 shard_map.121
  9.1 10.4 %all-to-all-start.2 = ((f32[32,1,128]{2,1,0:T(1,128)}), f32[32,1,128]{2,1,0:T(1,128)S(1)}, u32[]{:S(2)}, u32[]{:S(2)}) async-start(f32[32,1,128]{2,1,0:T(1,128)} %shard_map.121), calls=%async_computation.2 | async-start | bytes 32768 | tf_op jit(solution)/shard_map/all_to_all | solution.py:37
  19.5 0.7 fusion.14
  20.1 0.8 select_reduce_fusion.2
  20.9 0.1 fusion.13
  21.0 0.1 convolution_select_fusion
  21.2 0.1 eq.86
  21.3 0.3 bitcast_compare_fusion
  21.6 4.9 %all-to-all-done.2.values = f32[32,1,128]{2,1,0:T(1,128)S(1)} async-done(((f32[32,1,128]{2,1,0:T(1,128)}), f32[32,1,128]{2,1,0:T(1,128)S(1)}, u32[]{:S(2)}, u32[]{:S(2)}) %all-to-all-start.2) | async-done | bytes 16416 | tf_op jit(solution)/shard_map/all_to_all | solution.py:37
  26.4 0.6 shard_map.122
  27.0 13.0 %all-to-all-start.3 = ((f32[16,1,128]{2,1,0:T(1,128)}), f32[16,1,128]{2,1,0:T(1,128)S(1)}, u32[]{:S(2)}, u32[]{:S(2)}) async-start(f32[16,1,128]{2,1,0:T(1,128)} %shard_map.122), calls=%async_computation.3 | async-start | bytes 16384 | tf_op jit(solution)/shard_map/all_to_all | solution.py:37
  40.1 0.0 all-gather.6.cloned.1.call-start
  40.1 2.6 %convolution_convert_fusion = bf16[1536,1024]{1,0:T(8,128)(2,1)} fusion(pred[1536,128]{1,0:T(32,128)(4,1)S(1)} %bitcast_compare_fusion, bf16[128,1024]{1,0:T(8,128)(2,1)S(1)} %copy-done), kind=kOutput, calls=%fused_computation.18 | convolution fusion | flops 404226048 | bytes 3604480 | tf_op jit(solution)/shard_map/dot_general | solution.py:311
  42.8 8.5 %all-to-all-done.3 = f32[16,1,128]{2,1,0:T(1,128)S(1)} async-done(((f32[16,1,128]{2,1,0:T(1,128)}), f32[16,1,128]{2,1,0:T(1,128)S(1)}, u32[]{:S(2)}, u32[]{:S(2)}) %all-to-all-start.3) | async-done | bytes 8224 | tf_op jit(solution)/shard_map/all_to_all | solution.py:37
  51.3 0.6 slice_reduce_fusion
  52.7 1.4 fusion.16
  54.1 0.0 all-gather.6.cloned.1.call-update
  54.2 1.0 pad_maximum_fusion.1
  55.3 3.5 %all-to-all-start.5 = ((bf16[8,32,1152]{2,1,0:T(8,128)(2,1)}), bf16[8,32,1152]{2,1,0:T(8,128)(2,1)S(1)}, u32[]{:S(2)}, u32[]{:S(2)}) async-start(bf16[8,32,1152]{2,1,0:T(8,128)(2,1)} %pad_maximum_fusion.1), calls=%async_computation.5 | async-start | bytes 1179648 | tf_op jit(solution)/shard_map/all_to_all | solution.py:37
  58.8 0.0 all-gather.8.cloned.1.call-start
  58.9 3.0 %shard_map.120.plan = s32[32]{0:T(128)S(1)} custom-call(s32[64]{0:T(128)S(1)} %copy-done.19, s32[64]{0:T(128)S(1)} %copy-done.20), custom_call_target="tpu_custom_call" | custom-call | tf_op jit(solution)/shard_map/pallas_call | solution.py:106
  61.8 0.0 copy-start.4
  61.9 12.4 %all-to-all-done.5.pieces = bf16[8,32,1152]{2,1,0:T(8,128)(2,1)S(1)} async-done(((bf16[8,32,1152]{2,1,0:T(8,128)(2,1)}), bf16[8,32,1152]{2,1,0:T(8,128)(2,1)S(1)}, u32[]{:S(2)}, u32[]{:S(2)}) %all-to-all-start.5) | async-done | bytes 589856 | tf_op jit(solution)/shard_map/all_to_all | solution.py:37
  74.3 1.3 shard_map.125
  75.6 0.0 all-gather.8.cloned.1.call-update
  75.7 46.9 %all_to_all.39 = bf16[32,48,1024]{2,1,0:T(8,128)(2,1)} all-to-all(bf16[32,48,1024]{2,1,0:T(8,128)(2,1)} %bitcast.106), channel_id=1, replica_groups=mesh['y'=4,'c'=2,'x'=4,'far'=8,'near'=2] {'y','c','x'}, dimensions={0} | all-to-all | bytes 6291456 | tf_op jit(solution)/shard_map/all_to_all | solution.py:37
  122.6 0.0 copy-done.4
  122.6 6.2 %all-to-all-start.4 = ((bf16[8,256,1152]{2,1,0:T(8,128)(2,1)}), bf16[8,256,1152]{2,1,0:T(8,128)(2,1)}, u32[]{:S(2)}, u32[]{:S(2)}) async-start(bf16[8,256,1152]{2,1,0:T(8,128)(2,1)} %bitcast.104), calls=%async_computation.4 | async-start | bytes 9437184 | tf_op jit(solution)/shard_map/all_to_all | solution.py:37
  128.8 3.1 %shard_map.123 = (bf16[128,1152]{1,0:T(8,128)(2,1)}, bf16[128,1152]{1,0:T(8,128)(2,1)}, bf16[128,1152]{1,0:T(8,128)(2,1)}, bf16[128,1152]{1,0:T(8,128)(2,1)}) custom-call(s32[32]{0:T(128)} %copy-done.4, bf16[16,128,1152]{2,1,0:T(8,128)(2,1)} %bitcast.105), custom_call_target="tpu_custom_call" | custom-call | tf_op jit(solution)/shard_map/pallas_call | solution.py:143
  131.8 4.3 %collective-permute-start = (bf16[128,1152]{1,0:T(8,128)(2,1)}, bf16[128,1152]{1,0:T(8,128)(2,1)}, u32[]{:S(2)}, u32[]{:S(2)}) collective-permute-start(bf16[128,1152]{1,0:T(8,128)(2,1)} %get-tuple-element.67), channel_id=1, source_target_pairs={{0,32},{16,48},{32,0},{48,16},{1,33},{17,49},{33,1},{49,17},{2,34}... | collective-permute-start | bytes 884744 | tf_op jit(solution)/shard_map/ppermute | solution.py:272
  136.2 2.4 collective-permute-start.1
  138.6 4.1 %collective-permute-start.2 = (bf16[128,1152]{1,0:T(8,128)(2,1)}, bf16[128,1152]{1,0:T(8,128)(2,1)}, u32[]{:S(2)}, u32[]{:S(2)}) collective-permute-start(bf16[128,1152]{1,0:T(8,128)(2,1)} %get-tuple-element.69), channel_id=1, source_target_pairs={{0,48},{16,0},{32,16},{48,32},{1,49},{17,1},{33,17},{49,33},{2,50}... | collective-permute-start | bytes 884744 | tf_op jit(solution)/shard_map/ppermute | solution.py:272
  142.7 2.2 copy.21
  144.9 0.0 collective-permute-done
  144.9 5.9 %collective-permute-done.1 = bf16[128,1152]{1,0:T(8,128)(2,1)} collective-permute-done((bf16[128,1152]{1,0:T(8,128)(2,1)}, bf16[128,1152]{1,0:T(8,128)(2,1)}, u32[]{:S(2)}, u32[]{:S(2)}) %collective-permute-start.1) | collective-permute-done | bytes 294944 | tf_op jit(solution)/shard_map/ppermute | solution.py:272
  150.8 0.0 collective-permute-done.2
  150.8 32.5 %all-to-all-done.4 = bf16[8,256,1152]{2,1,0:T(8,128)(2,1)} async-done(((bf16[8,256,1152]{2,1,0:T(8,128)(2,1)}), bf16[8,256,1152]{2,1,0:T(8,128)(2,1)}, u32[]{:S(2)}, u32[]{:S(2)}) %all-to-all-start.4) | async-done | bytes 4718624 | tf_op jit(solution)/shard_map/all_to_all | solution.py:37
  183.3 8.4 %shard_map.124 = bf16[32,2,24,1024]{3,2,1,0:T(8,128)(2,1)} custom-call(bf16[2,768,1024]{2,1,0:T(8,128)(2,1)S(1)} %bitcast.102, bf16[8,2,128,1152]{3,2,1,0:T(8,128)(2,1)} %bitcast.47.weights_in.weights_out, bf16[8,2,128,1152]{3,2,1,0:T(8,128)(2,1)} %bitcast.47.weights_in.weights_out), custom_call_target="tpu_custom_call" | custom-call | flops 3623878656 | bytes 11010048 | tf_op jit(solution)/shard_map/pallas_call | solution.py:247
  191.8 0.0 copy-start.15
  191.8 5.8 %all-to-all-start.7 = ((bf16[32,48,1024]{2,1,0:T(8,128)(2,1)}), bf16[32,48,1024]{2,1,0:T(8,128)(2,1)}, u32[]{:S(2)}, u32[]{:S(2)}) async-start(bf16[32,48,1024]{2,1,0:T(8,128)(2,1)} %bitcast.48), calls=%async_computation.7 | async-start | bytes 6291456 | tf_op jit(solution)/shard_map/all_to_all | solution.py:37
  197.6 0.1 select_reduce_fusion.1
  197.7 0.3 fusion.8
  197.9 0.3 fusion.7
  198.2 0.7 fusion.21
  202.1 1.9 select_bitcast_fusion
  204.1 10.4 %all-gather.8.cloned.1.call-done = bf16[3072,1152]{1,0:T(8,128)(2,1)} async-done(((bf16[192,1152]{1,0:T(8,128)(2,1)}), bf16[3072,1152]{1,0:T(8,128)(2,1)}) %all-gather.8.cloned.1.call-update) | async-done | bytes 7077904 | tf_op jit(solution)/shard_map/all_gather | solution.py:331
  214.5 2.6 %shard_map.126 = (bf16[2,32,1152]{2,1,0:T(8,128)(2,1)}, bf16[2,32,1152]{2,1,0:T(8,128)(2,1)}, bf16[2,32,1152]{2,1,0:T(8,128)(2,1)}, bf16[2,32,1152]{2,1,0:T(8,128)(2,1)}) custom-call(s32[32]{0:T(128)} %copy-done.4, bf16[8,2,6,32,1152]{4,3,2,1,0:T(8,128)(2,1)} %bitcast.108), custom_call_target="tpu_custom_call" | custom-call | tf_op jit(solution)/shard_map/pallas_call | solution.py:143
  217.1 4.7 %collective-permute-start.3 = (bf16[2,32,1152]{2,1,0:T(8,128)(2,1)}, bf16[2,32,1152]{2,1,0:T(8,128)(2,1)S(1)}, u32[]{:S(2)}, u32[]{:S(2)}) collective-permute-start(bf16[2,32,1152]{2,1,0:T(8,128)(2,1)} %get-tuple-element.86), channel_id=1, source_target_pairs={{0,32},{16,48},{32,0},{48,16},{1,33},{17,49},{33,1},{49,17},{2,34}... | collective-permute-start | bytes 442376 | tf_op jit(solution)/shard_map/ppermute | solution.py:272
  221.8 2.2 collective-permute-start.4
  224.0 4.3 %collective-permute-start.5 = (bf16[2,32,1152]{2,1,0:T(8,128)(2,1)}, bf16[2,32,1152]{2,1,0:T(8,128)(2,1)S(1)}, u32[]{:S(2)}, u32[]{:S(2)}) collective-permute-start(bf16[2,32,1152]{2,1,0:T(8,128)(2,1)} %get-tuple-element.88), channel_id=1, source_target_pairs={{0,48},{16,0},{32,16},{48,32},{1,49},{17,1},{33,17},{49,33},{2,50}... | collective-permute-start | bytes 442376 | tf_op jit(solution)/shard_map/ppermute | solution.py:272
  228.3 7.3 %all-to-all-done.7 = bf16[32,48,1024]{2,1,0:T(8,128)(2,1)} async-done(((bf16[32,48,1024]{2,1,0:T(8,128)(2,1)}), bf16[32,48,1024]{2,1,0:T(8,128)(2,1)}, u32[]{:S(2)}, u32[]{:S(2)}) %all-to-all-start.7) | async-done | bytes 3145760 | tf_op jit(solution)/shard_map/all_to_all | solution.py:37
  235.6 0.0 copy-start.21
  235.6 3.0 %fusion.2 = f32[256,1024]{1,0:T(8,128)S(1)} fusion(bf16[1536,1024]{1,0:T(8,128)(2,1)} %bitcast.49, bf16[1536,128]{1,0:T(8,128)(2,1)S(1)} %fusion.8, bf16[1536,128]{1,0:T(8,128)(2,1)S(1)} %fusion.7), kind=kOutput, calls=%fused_computation.21 | convolution fusion | flops 806879232 | bytes 4980736 | tf_op jit(solution)/shard_map/dot_general | solution.py:351
  238.6 0.8 fusion.12
  239.3 0.2 collective-permute-done.3.one
  239.6 1.9 collective-permute-done.4.two
  241.5 0.0 collective-permute-done.5.three
  241.5 0.6 shard_map.127
  242.2 0.0 copy-start.17
  242.2 0.0 copy-start.18
  242.2 0.8 copy-done.17
  243.0 0.2 copy-done.18
  (40 shorter events, 0.2 us)
Async XLA Ops:
  7.2 33.0 %copy-start = (bf16[128,1024]{1,0:T(8,128)(2,1)S(1)}, bf16[128,1024]{1,0:T(8,128)(2,1)}, u32[]{:S(2)}) copy-start(bf16[128,1024]{1,0:T(8,128)(2,1)} %param.17) | copy-start | bytes 786436
  7.2 1.0 copy-start.1
  8.2 44.5 %copy-start.2 = (bf16[1,128,1152]{2,1,0:T(8,128)(2,1)S(1)}, bf16[1,128,1152]{2,1,0:T(8,128)(2,1)}, u32[]{:S(2)}) copy-start(bf16[1,128,1152]{2,1,0:T(8,128)(2,1)} %param.14) | copy-start | bytes 884740
  8.2 44.5 %copy-start.12 = (f32[1,128,1152]{2,1,0:T(8,128)S(1)}, f32[1,128,1152]{2,1,0:T(8,128)}, u32[]{:S(2)}) copy-start(f32[1,128,1152]{2,1,0:T(8,128)} %param.11) | copy-start | bytes 1769476
  8.2 44.5 %copy-start.13 = (f32[1,128,1152]{2,1,0:T(8,128)S(1)}, f32[1,128,1152]{2,1,0:T(8,128)}, u32[]{:S(2)}) copy-start(f32[1,128,1152]{2,1,0:T(8,128)} %param.12) | copy-start | bytes 1769476
  8.2 44.5 %copy-start.14 = (f32[1,128,1152]{2,1,0:T(8,128)S(1)}, f32[1,128,1152]{2,1,0:T(8,128)}, u32[]{:S(2)}) copy-start(f32[1,128,1152]{2,1,0:T(8,128)} %param.13) | copy-start | bytes 1769476
  9.1 17.3 %all-to-all-start.2 = ((f32[32,1,128]{2,1,0:T(1,128)}), f32[32,1,128]{2,1,0:T(1,128)S(1)}, u32[]{:S(2)}, u32[]{:S(2)}) async-start(f32[32,1,128]{2,1,0:T(1,128)} %shard_map.121), calls=%async_computation.2 | async-start | bytes 32768 | tf_op jit(solution)/shard_map/all_to_all | solution.py:37
  27.0 24.3 %all-to-all-start.3 = ((f32[16,1,128]{2,1,0:T(1,128)}), f32[16,1,128]{2,1,0:T(1,128)S(1)}, u32[]{:S(2)}, u32[]{:S(2)}) async-start(f32[16,1,128]{2,1,0:T(1,128)} %shard_map.122), calls=%async_computation.3 | async-start | bytes 16384 | tf_op jit(solution)/shard_map/all_to_all | solution.py:37
  40.1 82.5 %all-gather.6.cloned.1.call-start = ((), (), s32[]{:S(2)}) async-start(), calls=%async_computation.9 | async-start | bytes 5013504 | tf_op jit(solution)/shard_map/all_gather | solution.py:323
  54.1 1.1 copy-start.7
  54.1 68.4 %copy-start.9 = (f32[128,1152]{1,0:T(8,128)}, f32[128,1152]{1,0:T(8,128)S(1)}, u32[]{:S(2)}) copy-start(f32[128,1152]{1,0:T(8,128)S(1)} %get-tuple-element.76.own_two) | copy-start | bytes 1769476
  54.1 4.7 %copy-start.19 = (s32[64]{0:T(128)S(1)}, s32[64]{0:T(128)}, u32[]{:S(2)}) copy-start(s32[64]{0:T(128)} %old_host.1) | copy-start | bytes 772
  54.1 4.7 %copy-start.20 = (s32[64]{0:T(128)S(1)}, s32[64]{0:T(128)}, u32[]{:S(2)}) copy-start(s32[64]{0:T(128)} %new_host.1) | copy-start | bytes 772
  55.3 19.0 %all-to-all-start.5 = ((bf16[8,32,1152]{2,1,0:T(8,128)(2,1)}), bf16[8,32,1152]{2,1,0:T(8,128)(2,1)S(1)}, u32[]{:S(2)}, u32[]{:S(2)}) async-start(bf16[8,32,1152]{2,1,0:T(8,128)(2,1)} %pad_maximum_fusion.1), calls=%async_computation.5 | async-start | bytes 1179648 | tf_op jit(solution)/shard_map/all_to_all | solution.py:37
  58.8 155.7 %all-gather.8.cloned.1.call-start = ((), (), s32[]{:S(2)}) async-start(), calls=%async_computation.10 | async-start | bytes 7520256 | tf_op jit(solution)/shard_map/all_gather | solution.py:331
  61.8 60.7 %copy-start.4 = (s32[32]{0:T(128)}, s32[32]{0:T(128)S(1)}, u32[]{:S(2)}) copy-start(s32[32]{0:T(128)S(1)} %shard_map.120.plan) | copy-start | bytes 388
  122.6 60.7 %all-to-all-start.4 = ((bf16[8,256,1152]{2,1,0:T(8,128)(2,1)}), bf16[8,256,1152]{2,1,0:T(8,128)(2,1)}, u32[]{:S(2)}, u32[]{:S(2)}) async-start(bf16[8,256,1152]{2,1,0:T(8,128)(2,1)} %bitcast.104), calls=%async_computation.4 | async-start | bytes 9437184 | tf_op jit(solution)/shard_map/all_to_all | solution.py:37
  131.8 13.1 %collective-permute-start = (bf16[128,1152]{1,0:T(8,128)(2,1)}, bf16[128,1152]{1,0:T(8,128)(2,1)}, u32[]{:S(2)}, u32[]{:S(2)}) collective-permute-start(bf16[128,1152]{1,0:T(8,128)(2,1)} %get-tuple-element.67), channel_id=1, source_target_pairs={{0,32},{16,48},{32,0},{48,16},{1,33},{17,49},{33,1},{49,17},{2,34}... | collective-permute-start | bytes 884744 | tf_op jit(solution)/shard_map/ppermute | solution.py:272
  136.2 14.6 %collective-permute-start.1 = (bf16[128,1152]{1,0:T(8,128)(2,1)}, bf16[128,1152]{1,0:T(8,128)(2,1)}, u32[]{:S(2)}, u32[]{:S(2)}) collective-permute-start(bf16[128,1152]{1,0:T(8,128)(2,1)} %get-tuple-element.68), channel_id=1, source_target_pairs={{0,16},{16,32},{32,48},{48,0},{1,17},{17,33},{33,49},{49,1},{2,18}... | collective-permute-start | bytes 884744 | tf_op jit(solution)/shard_map/ppermute | solution.py:272
  138.6 12.3 %collective-permute-start.2 = (bf16[128,1152]{1,0:T(8,128)(2,1)}, bf16[128,1152]{1,0:T(8,128)(2,1)}, u32[]{:S(2)}, u32[]{:S(2)}) collective-permute-start(bf16[128,1152]{1,0:T(8,128)(2,1)} %get-tuple-element.69), channel_id=1, source_target_pairs={{0,48},{16,0},{32,16},{48,32},{1,49},{17,1},{33,17},{49,33},{2,50}... | collective-permute-start | bytes 884744 | tf_op jit(solution)/shard_map/ppermute | solution.py:272
  191.8 5.8 %copy-start.16 = (f32[128,8]{0,1:T(8,128)S(1)}, f32[128,8]{0,1:T(8,128)}, u32[]{:S(2)}) copy-start(f32[128,8]{0,1:T(8,128)} %param.19) | copy-start | bytes 12292
  191.8 6.5 %copy-start.5 = (s32[32]{0:T(128)S(1)}, s32[32]{0:T(128)}, u32[]{:S(2)}) copy-start(s32[32]{0:T(128)} %copy-done.4) | copy-start | bytes 388
  191.8 10.3 %copy-start.11 = (f32[128,1152]{1,0:T(8,128)S(1)}, f32[128,1152]{1,0:T(8,128)}, u32[]{:S(2)}) copy-start(f32[128,1152]{1,0:T(8,128)} %get-tuple-element.74) | copy-start | bytes 1769476
  191.8 10.4 %copy-start.15 = (bf16[128,1152]{1,0:T(8,128)(2,1)S(1)}, bf16[128,1152]{1,0:T(8,128)(2,1)}, u32[]{:S(2)}) copy-start(bf16[128,1152]{1,0:T(8,128)(2,1)} %get-tuple-element.70) | copy-start | bytes 884740
  191.8 43.8 %all-to-all-start.7 = ((bf16[32,48,1024]{2,1,0:T(8,128)(2,1)}), bf16[32,48,1024]{2,1,0:T(8,128)(2,1)}, u32[]{:S(2)}, u32[]{:S(2)}) async-start(bf16[32,48,1024]{2,1,0:T(8,128)(2,1)} %bitcast.48), calls=%async_computation.7 | async-start | bytes 6291456 | tf_op jit(solution)/shard_map/all_to_all | solution.py:37
  217.1 22.5 %collective-permute-start.3 = (bf16[2,32,1152]{2,1,0:T(8,128)(2,1)}, bf16[2,32,1152]{2,1,0:T(8,128)(2,1)S(1)}, u32[]{:S(2)}, u32[]{:S(2)}) collective-permute-start(bf16[2,32,1152]{2,1,0:T(8,128)(2,1)} %get-tuple-element.86), channel_id=1, source_target_pairs={{0,32},{16,48},{32,0},{48,16},{1,33},{17,49},{33,1},{49,17},{2,34}... | collective-permute-start | bytes 442376 | tf_op jit(solution)/shard_map/ppermute | solution.py:272
  221.8 19.7 %collective-permute-start.4 = (bf16[2,32,1152]{2,1,0:T(8,128)(2,1)}, bf16[2,32,1152]{2,1,0:T(8,128)(2,1)S(1)}, u32[]{:S(2)}, u32[]{:S(2)}) collective-permute-start(bf16[2,32,1152]{2,1,0:T(8,128)(2,1)} %get-tuple-element.87), channel_id=1, source_target_pairs={{0,16},{16,32},{32,48},{48,0},{1,17},{17,33},{33,49},{49,1},{2,18}... | collective-permute-start | bytes 442376 | tf_op jit(solution)/shard_map/ppermute | solution.py:272
  224.0 17.5 %collective-permute-start.5 = (bf16[2,32,1152]{2,1,0:T(8,128)(2,1)}, bf16[2,32,1152]{2,1,0:T(8,128)(2,1)S(1)}, u32[]{:S(2)}, u32[]{:S(2)}) collective-permute-start(bf16[2,32,1152]{2,1,0:T(8,128)(2,1)} %get-tuple-element.88), channel_id=1, source_target_pairs={{0,48},{16,0},{32,16},{48,32},{1,49},{17,1},{33,17},{49,33},{2,50}... | collective-permute-start | bytes 442376 | tf_op jit(solution)/shard_map/ppermute | solution.py:272
  235.6 5.9 %copy-start.3 = (bf16[2,32,1152]{2,1,0:T(8,128)(2,1)S(1)}, bf16[2,32,1152]{2,1,0:T(8,128)(2,1)}, u32[]{:S(2)}) copy-start(bf16[2,32,1152]{2,1,0:T(8,128)(2,1)} %get-tuple-element.89.here) | copy-start | bytes 442372
  235.6 5.9 %copy-start.6 = (s32[32]{0:T(128)S(1)}, s32[32]{0:T(128)}, u32[]{:S(2)}) copy-start(s32[32]{0:T(128)} %copy-done.4) | copy-start | bytes 388
  235.6 5.9 %copy-start.8 = (f32[128,1152]{1,0:T(8,128)S(1)}, f32[128,1152]{1,0:T(8,128)}, u32[]{:S(2)}) copy-start(f32[128,1152]{1,0:T(8,128)} %copy-done.7) | copy-start | bytes 1769476
  235.6 5.9 %copy-start.10 = (f32[128,1152]{1,0:T(8,128)S(1)}, f32[128,1152]{1,0:T(8,128)}, u32[]{:S(2)}) copy-start(f32[128,1152]{1,0:T(8,128)} %copy-done.9) | copy-start | bytes 1769476
  235.6 6.6 %copy-start.21 = (s32[64]{0:T(128)S(1)}, s32[64]{0:T(128)}, u32[]{:S(2)}) copy-start(s32[64]{0:T(128)} %new_host.1) | copy-start | bytes 772
  242.2 0.8 copy-start.17
  242.2 1.0 copy-start.18
Sparse Core Ops, SparseCore 0:
  54.3 62.0 all-gather.5
  119.1 95.3 all-gather.7

commit v9 on v8

--- a/solution.py
+++ b/solution.py
@@ -231,13 +231,17 @@
         projected = jnp.dot(rows[0], weight, preferred_element_type=f32)
         hidden[...] = (jax.nn.silu(projected[:, :units]) * projected[:, units:]).astype(bf16)
 
-    @pl.when(pl.program_id(1) == 1)
-    def _():
-        weight = weights_out[...].reshape(-1, units)
-        produced = lax.dot_general(
-            hidden[...], weight, (((1,), (1,)), ((), ())), preferred_element_type=f32
-        )
-        outs[...] = produced.reshape(outs.shape).astype(bf16)
+    half = hidden.shape[0] // 2
+    for i in range(2):
+
+        @pl.when(pl.program_id(1) == i + 1)
+        def _(i=i):
+            weight = weights_out[...].reshape(-1, units)
+            rows_in = hidden[i * half : (i + 1) * half]
+            produced = lax.dot_general(
+                rows_in, weight, (((1,), (1,)), ((), ())), preferred_element_type=f32
+            )
+            outs[...] = produced.reshape(outs.shape).astype(bf16)
 
 
 def experts(rows, weights, capacity):
@@ -247,14 +251,14 @@
     return pl.pallas_call(
         expert_layer,
         out_shape=jax.ShapeDtypeStruct((row_count // capacity, shares, capacity, width), bf16),
-        grid=(shares, 2),
+        grid=(shares, 3),
         in_specs=[
             pl.BlockSpec((1, row_count, width), lambda j, p: (j, 0, 0)),
             pl.BlockSpec((shards, 1, shard_rows, 2 * units), lambda j, p: (0, j, 0, 0)),
             pl.BlockSpec((shards, 1, shard_rows, units), lambda j, p: (0, j, 0, 2)),
         ],
         out_specs=pl.BlockSpec(
-            (row_count // capacity, 1, capacity, width), lambda j, p: (0, j, 0, 0)
+            (row_count // capacity // 2, 1, capacity, width), lambda j, p: (p // 2, j, 0, 0)
         ),
         scratch_shapes=[pltpu.VMEM((row_count, units), bf16)],
         compiler_params=limit(30),

time: 251 us -> 252 us (level)
  transfers between devices with their start and end apart: 13 -> 13, of which waited for: 9 -> 9; matrix products, arithmetic and copies ran while one was open for 6% -> 6% of each run, Pallas kernels for 7% -> 8%
where the time goes in v9:
time: 252 us; the launch traced here: 251 us
  waiting for transfers between devices  84.2 us (33%)
  starting transfers between devices  60.9 us (24%)
  blocking collectives  46.9 us (19%)
  Pallas kernels  21.7 us (9%)
  between operations  18.4 us (7%)
  other arithmetic  8.26 us (3%)
  matrix products  5.77 us (2%)
  local copies, waits for them, and re-layouts  5.04 us (2%)
    all_to_all x5, waiting for transfers between devices, swap(): return lax.all_to_all(array, axes, split_axis=0, concat_axis=0, tiled=True)  66.9 us
    all_to_all x1, blocking collectives, swap(): return lax.all_to_all(array, axes, split_axis=0, concat_axis=0, tiled=True)  46.9 us
    all_to_all x5, starting transfers between devices, swap(): return lax.all_to_all(array, axes, split_axis=0, concat_axis=0, tiled=True)  38.9 us
    ppermute x6, starting transfers between devices, shifted(): lax.ppermute(block, 'x', [(i, (i + shift) % X) for i in range(X)])  21.9 us
    pallas_call x1, Pallas kernels, experts(): pl.pallas_call(expert_layer, out_shape=jax.ShapeDtypeStruct((row_count //...  9.63 us
    all_gather x1, waiting for transfers between devices, per_device(): pieces = lax.all_gather(pieces.reshape(-1, cols), RING, axis=0, tiled=True)  9.28 us
    ppermute x6, waiting for transfers between devices, shifted(): lax.ppermute(block, 'x', [(i, (i + shift) % X) for i in range(X)])  8.04 us
    pallas_call x2, Pallas kernels, picked(): pl.pallas_call(kernel, out_shape=[jax.ShapeDtypeStruct(shape, bf16)] * X,...  5.58 us
  transfers between devices with their start and end apart: 13, of which 9 were waited for; matrix products, arithmetic and copies ran while one was open for 6% of the time, Pallas kernels for 8%

profile of v9, /device:TPU:1, one launch (start us, length us, event | category | flops | bytes accessed | tf_op | source)
XLA Modules:
  0.0 251.2 jit_solution(3899035650560700973)
XLA Ops:
  7.2 0.0 copy-start
  7.2 0.0 copy-start.1
  7.2 1.0 copy-done.1
  8.2 0.9 shard_map.121
  9.1 10.4 %all-to-all-start.2 = ((f32[32,1,128]{2,1,0:T(1,128)}), f32[32,1,128]{2,1,0:T(1,128)S(1)}, u32[]{:S(2)}, u32[]{:S(2)}) async-start(f32[32,1,128]{2,1,0:T(1,128)} %shard_map.121), calls=%async_computation.2 | async-start | bytes 32768 | tf_op jit(solution)/shard_map/all_to_all | solution.py:37
  19.5 0.7 fusion.14
  20.1 0.8 select_reduce_fusion.2
  20.9 0.1 fusion.13
  21.0 0.1 convolution_select_fusion
  21.2 0.1 eq.86
  21.3 0.3 bitcast_compare_fusion
  21.6 4.9 %all-to-all-done.2.values = f32[32,1,128]{2,1,0:T(1,128)S(1)} async-done(((f32[32,1,128]{2,1,0:T(1,128)}), f32[32,1,128]{2,1,0:T(1,128)S(1)}, u32[]{:S(2)}, u32[]{:S(2)}) %all-to-all-start.2) | async-done | bytes 16416 | tf_op jit(solution)/shard_map/all_to_all | solution.py:37
  26.4 0.6 shard_map.122
  27.0 13.0 %all-to-all-start.3 = ((f32[16,1,128]{2,1,0:T(1,128)}), f32[16,1,128]{2,1,0:T(1,128)S(1)}, u32[]{:S(2)}, u32[]{:S(2)}) async-start(f32[16,1,128]{2,1,0:T(1,128)} %shard_map.122), calls=%async_computation.3 | async-start | bytes 16384 | tf_op jit(solution)/shard_map/all_to_all | solution.py:37
  40.1 0.0 all-gather.6.cloned.1.call-start
  40.1 2.6 %convolution_convert_fusion = bf16[1536,1024]{1,0:T(8,128)(2,1)} fusion(pred[1536,128]{1,0:T(32,128)(4,1)S(1)} %bitcast_compare_fusion, bf16[128,1024]{1,0:T(8,128)(2,1)S(1)} %copy-done), kind=kOutput, calls=%fused_computation.18 | convolution fusion | flops 404226048 | bytes 3604480 | tf_op jit(solution)/shard_map/dot_general | solution.py:315
  42.8 8.5 %all-to-all-done.3 = f32[16,1,128]{2,1,0:T(1,128)S(1)} async-done(((f32[16,1,128]{2,1,0:T(1,128)}), f32[16,1,128]{2,1,0:T(1,128)S(1)}, u32[]{:S(2)}, u32[]{:S(2)}) %all-to-all-start.3) | async-done | bytes 8224 | tf_op jit(solution)/shard_map/all_to_all | solution.py:37
  51.3 0.6 slice_reduce_fusion
  52.7 1.4 fusion.16
  54.1 0.0 all-gather.6.cloned.1.call-update
  54.2 1.0 pad_maximum_fusion.1
  55.3 3.5 %all-to-all-start.5 = ((bf16[8,32,1152]{2,1,0:T(8,128)(2,1)}), bf16[8,32,1152]{2,1,0:T(8,128)(2,1)S(1)}, u32[]{:S(2)}, u32[]{:S(2)}) async-start(bf16[8,32,1152]{2,1,0:T(8,128)(2,1)} %pad_maximum_fusion.1), calls=%async_computation.5 | async-start | bytes 1179648 | tf_op jit(solution)/shard_map/all_to_all | solution.py:37
  58.8 0.0 all-gather.8.cloned.1.call-start
  58.9 3.0 %shard_map.120.plan = s32[32]{0:T(128)S(1)} custom-call(s32[64]{0:T(128)S(1)} %copy-done.19, s32[64]{0:T(128)S(1)} %copy-done.20), custom_call_target="tpu_custom_call" | custom-call | tf_op jit(solution)/shard_map/pallas_call | solution.py:106
  61.9 12.4 %all-to-all-done.5.pieces = bf16[8,32,1152]{2,1,0:T(8,128)(2,1)S(1)} async-done(((bf16[8,32,1152]{2,1,0:T(8,128)(2,1)}), bf16[8,32,1152]{2,1,0:T(8,128)(2,1)S(1)}, u32[]{:S(2)}, u32[]{:S(2)}) %all-to-all-start.5) | async-done | bytes 589856 | tf_op jit(solution)/shard_map/all_to_all | solution.py:37
  74.3 1.3 shard_map.125
  75.6 0.0 all-gather.8.cloned.1.call-update
  75.7 46.9 %all_to_all.39 = bf16[32,48,1024]{2,1,0:T(8,128)(2,1)} all-to-all(bf16[32,48,1024]{2,1,0:T(8,128)(2,1)} %bitcast.106), channel_id=1, replica_groups=mesh['y'=4,'c'=2,'x'=4,'far'=8,'near'=2] {'y','c','x'}, dimensions={0} | all-to-all | bytes 6291456 | tf_op jit(solution)/shard_map/all_to_all | solution.py:37
  122.6 6.2 %all-to-all-start.4 = ((bf16[8,256,1152]{2,1,0:T(8,128)(2,1)}), bf16[8,256,1152]{2,1,0:T(8,128)(2,1)}, u32[]{:S(2)}, u32[]{:S(2)}) async-start(bf16[8,256,1152]{2,1,0:T(8,128)(2,1)} %bitcast.104), calls=%async_computation.4 | async-start | bytes 9437184 | tf_op jit(solution)/shard_map/all_to_all | solution.py:37
  128.8 2.9 %shard_map.123 = (bf16[128,1152]{1,0:T(8,128)(2,1)}, bf16[128,1152]{1,0:T(8,128)(2,1)}, bf16[128,1152]{1,0:T(8,128)(2,1)}, bf16[128,1152]{1,0:T(8,128)(2,1)}) custom-call(s32[32]{0:T(128)} %copy-done.4, bf16[16,128,1152]{2,1,0:T(8,128)(2,1)} %bitcast.105), custom_call_target="tpu_custom_call" | custom-call | tf_op jit(solution)/shard_map/pallas_call | solution.py:143
  131.7 4.3 %collective-permute-start = (bf16[128,1152]{1,0:T(8,128)(2,1)}, bf16[128,1152]{1,0:T(8,128)(2,1)}, u32[]{:S(2)}, u32[]{:S(2)}) collective-permute-start(bf16[128,1152]{1,0:T(8,128)(2,1)} %get-tuple-element.67), channel_id=1, source_target_pairs={{0,32},{16,48},{32,0},{48,16},{1,33},{17,49},{33,1},{49,17},{2,34}... | collective-permute-start | bytes 884744 | tf_op jit(solution)/shard_map/ppermute | solution.py:276
  136.1 2.4 collective-permute-start.1
  138.4 4.1 %collective-permute-start.2 = (bf16[128,1152]{1,0:T(8,128)(2,1)}, bf16[128,1152]{1,0:T(8,128)(2,1)}, u32[]{:S(2)}, u32[]{:S(2)}) collective-permute-start(bf16[128,1152]{1,0:T(8,128)(2,1)} %get-tuple-element.69), channel_id=1, source_target_pairs={{0,48},{16,0},{32,16},{48,32},{1,49},{17,1},{33,17},{49,33},{2,50}... | collective-permute-start | bytes 884744 | tf_op jit(solution)/shard_map/ppermute | solution.py:276
  142.6 2.2 copy.21
  144.8 0.0 collective-permute-done
  144.8 5.9 %collective-permute-done.1 = bf16[128,1152]{1,0:T(8,128)(2,1)} collective-permute-done((bf16[128,1152]{1,0:T(8,128)(2,1)}, bf16[128,1152]{1,0:T(8,128)(2,1)}, u32[]{:S(2)}, u32[]{:S(2)}) %collective-permute-start.1) | collective-permute-done | bytes 294944 | tf_op jit(solution)/shard_map/ppermute | solution.py:276
  150.7 0.0 collective-permute-done.2
  150.7 32.6 %all-to-all-done.4 = bf16[8,256,1152]{2,1,0:T(8,128)(2,1)} async-done(((bf16[8,256,1152]{2,1,0:T(8,128)(2,1)}), bf16[8,256,1152]{2,1,0:T(8,128)(2,1)}, u32[]{:S(2)}, u32[]{:S(2)}) %all-to-all-start.4) | async-done | bytes 4718624 | tf_op jit(solution)/shard_map/all_to_all | solution.py:37
  183.3 9.6 %shard_map.124 = bf16[32,2,24,1024]{3,2,1,0:T(8,128)(2,1)} custom-call(bf16[2,768,1024]{2,1,0:T(8,128)(2,1)S(1)} %bitcast.102, bf16[8,2,128,1152]{3,2,1,0:T(8,128)(2,1)} %bitcast.47.weights_in.weights_out, bf16[8,2,128,1152]{3,2,1,0:T(8,128)(2,1)} %bitcast.47.weights_in.weights_out), custom_call_target="tpu_custom_call" | custom-call | flops 3623878656 | bytes 11010048 | tf_op jit(solution)/shard_map/pallas_call | solution.py:251
  193.0 0.0 copy-start.15
  193.0 5.8 %all-to-all-start.7 = ((bf16[32,48,1024]{2,1,0:T(8,128)(2,1)}), bf16[32,48,1024]{2,1,0:T(8,128)(2,1)}, u32[]{:S(2)}, u32[]{:S(2)}) async-start(bf16[32,48,1024]{2,1,0:T(8,128)(2,1)} %bitcast.48), calls=%async_computation.7 | async-start | bytes 6291456 | tf_op jit(solution)/shard_map/all_to_all | solution.py:37
  198.7 0.0 copy-done.16
  198.8 0.1 select_reduce_fusion.1
  198.8 0.3 fusion.8
  199.1 0.3 fusion.7
  199.4 0.7 fusion.21
  203.3 1.9 select_bitcast_fusion
  205.2 9.3 %all-gather.8.cloned.1.call-done = bf16[3072,1152]{1,0:T(8,128)(2,1)} async-done(((bf16[192,1152]{1,0:T(8,128)(2,1)}), bf16[3072,1152]{1,0:T(8,128)(2,1)}) %all-gather.8.cloned.1.call-update) | async-done | bytes 7077904 | tf_op jit(solution)/shard_map/all_gather | solution.py:335
  214.5 2.6 %shard_map.126 = (bf16[2,32,1152]{2,1,0:T(8,128)(2,1)}, bf16[2,32,1152]{2,1,0:T(8,128)(2,1)}, bf16[2,32,1152]{2,1,0:T(8,128)(2,1)}, bf16[2,32,1152]{2,1,0:T(8,128)(2,1)}) custom-call(s32[32]{0:T(128)} %copy-done.4, bf16[8,2,6,32,1152]{4,3,2,1,0:T(8,128)(2,1)} %bitcast.108), custom_call_target="tpu_custom_call" | custom-call | tf_op jit(solution)/shard_map/pallas_call | solution.py:143
  217.2 4.6 %collective-permute-start.3 = (bf16[2,32,1152]{2,1,0:T(8,128)(2,1)}, bf16[2,32,1152]{2,1,0:T(8,128)(2,1)S(1)}, u32[]{:S(2)}, u32[]{:S(2)}) collective-permute-start(bf16[2,32,1152]{2,1,0:T(8,128)(2,1)} %get-tuple-element.86), channel_id=1, source_target_pairs={{0,32},{16,48},{32,0},{48,16},{1,33},{17,49},{33,1},{49,17},{2,34}... | collective-permute-start | bytes 442376 | tf_op jit(solution)/shard_map/ppermute | solution.py:276
  221.8 2.2 collective-permute-start.4
  223.9 4.3 %collective-permute-start.5 = (bf16[2,32,1152]{2,1,0:T(8,128)(2,1)}, bf16[2,32,1152]{2,1,0:T(8,128)(2,1)S(1)}, u32[]{:S(2)}, u32[]{:S(2)}) collective-permute-start(bf16[2,32,1152]{2,1,0:T(8,128)(2,1)} %get-tuple-element.88), channel_id=1, source_target_pairs={{0,48},{16,0},{32,16},{48,32},{1,49},{17,1},{33,17},{49,33},{2,50}... | collective-permute-start | bytes 442376 | tf_op jit(solution)/shard_map/ppermute | solution.py:276
  228.3 8.5 %all-to-all-done.7 = bf16[32,48,1024]{2,1,0:T(8,128)(2,1)} async-done(((bf16[32,48,1024]{2,1,0:T(8,128)(2,1)}), bf16[32,48,1024]{2,1,0:T(8,128)(2,1)}, u32[]{:S(2)}, u32[]{:S(2)}) %all-to-all-start.7) | async-done | bytes 3145760 | tf_op jit(solution)/shard_map/all_to_all | solution.py:37
  236.7 0.0 copy-start.21
  236.8 3.0 %fusion.2 = f32[256,1024]{1,0:T(8,128)S(1)} fusion(bf16[1536,1024]{1,0:T(8,128)(2,1)} %bitcast.49, bf16[1536,128]{1,0:T(8,128)(2,1)S(1)} %fusion.8, bf16[1536,128]{1,0:T(8,128)(2,1)S(1)} %fusion.7), kind=kOutput, calls=%fused_computation.21 | convolution fusion | flops 806879232 | bytes 4980736 | tf_op jit(solution)/shard_map/dot_general | solution.py:355
  239.8 0.8 fusion.12
  240.5 0.2 collective-permute-done.3.one
  240.7 1.9 collective-permute-done.4.two
  242.7 0.0 collective-permute-done.5.three
  242.7 0.6 shard_map.127
  243.4 0.0 copy-start.17
  243.4 0.0 copy-start.18
  243.4 0.8 copy-done.17
  244.2 0.2 copy-done.18
  (40 shorter events, 0.2 us)
Async XLA Ops:
  7.2 33.0 %copy-start = (bf16[128,1024]{1,0:T(8,128)(2,1)S(1)}, bf16[128,1024]{1,0:T(8,128)(2,1)}, u32[]{:S(2)}) copy-start(bf16[128,1024]{1,0:T(8,128)(2,1)} %param.17) | copy-start | bytes 786436
  7.2 1.0 copy-start.1
  8.2 44.5 %copy-start.2 = (bf16[1,128,1152]{2,1,0:T(8,128)(2,1)S(1)}, bf16[1,128,1152]{2,1,0:T(8,128)(2,1)}, u32[]{:S(2)}) copy-start(bf16[1,128,1152]{2,1,0:T(8,128)(2,1)} %param.14) | copy-start | bytes 884740
  8.2 44.5 %copy-start.12 = (f32[1,128,1152]{2,1,0:T(8,128)S(1)}, f32[1,128,1152]{2,1,0:T(8,128)}, u32[]{:S(2)}) copy-start(f32[1,128,1152]{2,1,0:T(8,128)} %param.11) | copy-start | bytes 1769476
  8.2 44.5 %copy-start.13 = (f32[1,128,1152]{2,1,0:T(8,128)S(1)}, f32[1,128,1152]{2,1,0:T(8,128)}, u32[]{:S(2)}) copy-start(f32[1,128,1152]{2,1,0:T(8,128)} %param.12) | copy-start | bytes 1769476
  8.2 44.5 %copy-start.14 = (f32[1,128,1152]{2,1,0:T(8,128)S(1)}, f32[1,128,1152]{2,1,0:T(8,128)}, u32[]{:S(2)}) copy-start(f32[1,128,1152]{2,1,0:T(8,128)} %param.13) | copy-start | bytes 1769476
  9.1 17.3 %all-to-all-start.2 = ((f32[32,1,128]{2,1,0:T(1,128)}), f32[32,1,128]{2,1,0:T(1,128)S(1)}, u32[]{:S(2)}, u32[]{:S(2)}) async-start(f32[32,1,128]{2,1,0:T(1,128)} %shard_map.121), calls=%async_computation.2 | async-start | bytes 32768 | tf_op jit(solution)/shard_map/all_to_all | solution.py:37
  27.0 24.3 %all-to-all-start.3 = ((f32[16,1,128]{2,1,0:T(1,128)}), f32[16,1,128]{2,1,0:T(1,128)S(1)}, u32[]{:S(2)}, u32[]{:S(2)}) async-start(f32[16,1,128]{2,1,0:T(1,128)} %shard_map.122), calls=%async_computation.3 | async-start | bytes 16384 | tf_op jit(solution)/shard_map/all_to_all | solution.py:37
  40.1 82.5 %all-gather.6.cloned.1.call-start = ((), (), s32[]{:S(2)}) async-start(), calls=%async_computation.9 | async-start | bytes 5013504 | tf_op jit(solution)/shard_map/all_gather | solution.py:327
  54.1 1.1 copy-start.7
  54.1 68.4 %copy-start.9 = (f32[128,1152]{1,0:T(8,128)}, f32[128,1152]{1,0:T(8,128)S(1)}, u32[]{:S(2)}) copy-start(f32[128,1152]{1,0:T(8,128)S(1)} %get-tuple-element.76.own_two) | copy-start | bytes 1769476
  54.1 4.7 %copy-start.19 = (s32[64]{0:T(128)S(1)}, s32[64]{0:T(128)}, u32[]{:S(2)}) copy-start(s32[64]{0:T(128)} %old_host.1) | copy-start | bytes 772
  54.1 4.7 %copy-start.20 = (s32[64]{0:T(128)S(1)}, s32[64]{0:T(128)}, u32[]{:S(2)}) copy-start(s32[64]{0:T(128)} %new_host.1) | copy-start | bytes 772
  55.3 19.0 %all-to-all-start.5 = ((bf16[8,32,1152]{2,1,0:T(8,128)(2,1)}), bf16[8,32,1152]{2,1,0:T(8,128)(2,1)S(1)}, u32[]{:S(2)}, u32[]{:S(2)}) async-start(bf16[8,32,1152]{2,1,0:T(8,128)(2,1)} %pad_maximum_fusion.1), calls=%async_computation.5 | async-start | bytes 1179648 | tf_op jit(solution)/shard_map/all_to_all | solution.py:37
  58.8 155.7 %all-gather.8.cloned.1.call-start = ((), (), s32[]{:S(2)}) async-start(), calls=%async_computation.10 | async-start | bytes 7520256 | tf_op jit(solution)/shard_map/all_gather | solution.py:335
  61.8 60.7 %copy-start.4 = (s32[32]{0:T(128)}, s32[32]{0:T(128)S(1)}, u32[]{:S(2)}) copy-start(s32[32]{0:T(128)S(1)} %shard_map.120.plan) | copy-start | bytes 388
  122.6 60.7 %all-to-all-start.4 = ((bf16[8,256,1152]{2,1,0:T(8,128)(2,1)}), bf16[8,256,1152]{2,1,0:T(8,128)(2,1)}, u32[]{:S(2)}, u32[]{:S(2)}) async-start(bf16[8,256,1152]{2,1,0:T(8,128)(2,1)} %bitcast.104), calls=%async_computation.4 | async-start | bytes 9437184 | tf_op jit(solution)/shard_map/all_to_all | solution.py:37
  131.7 13.1 %collective-permute-start = (bf16[128,1152]{1,0:T(8,128)(2,1)}, bf16[128,1152]{1,0:T(8,128)(2,1)}, u32[]{:S(2)}, u32[]{:S(2)}) collective-permute-start(bf16[128,1152]{1,0:T(8,128)(2,1)} %get-tuple-element.67), channel_id=1, source_target_pairs={{0,32},{16,48},{32,0},{48,16},{1,33},{17,49},{33,1},{49,17},{2,34}... | collective-permute-start | bytes 884744 | tf_op jit(solution)/shard_map/ppermute | solution.py:276
  136.1 14.6 %collective-permute-start.1 = (bf16[128,1152]{1,0:T(8,128)(2,1)}, bf16[128,1152]{1,0:T(8,128)(2,1)}, u32[]{:S(2)}, u32[]{:S(2)}) collective-permute-start(bf16[128,1152]{1,0:T(8,128)(2,1)} %get-tuple-element.68), channel_id=1, source_target_pairs={{0,16},{16,32},{32,48},{48,0},{1,17},{17,33},{33,49},{49,1},{2,18}... | collective-permute-start | bytes 884744 | tf_op jit(solution)/shard_map/ppermute | solution.py:276
  138.4 12.3 %collective-permute-start.2 = (bf16[128,1152]{1,0:T(8,128)(2,1)}, bf16[128,1152]{1,0:T(8,128)(2,1)}, u32[]{:S(2)}, u32[]{:S(2)}) collective-permute-start(bf16[128,1152]{1,0:T(8,128)(2,1)} %get-tuple-element.69), channel_id=1, source_target_pairs={{0,48},{16,0},{32,16},{48,32},{1,49},{17,1},{33,17},{49,33},{2,50}... | collective-permute-start | bytes 884744 | tf_op jit(solution)/shard_map/ppermute | solution.py:276
  192.9 5.8 %copy-start.16 = (f32[128,8]{0,1:T(8,128)S(1)}, f32[128,8]{0,1:T(8,128)}, u32[]{:S(2)}) copy-start(f32[128,8]{0,1:T(8,128)} %param.19) | copy-start | bytes 12292
  192.9 6.5 %copy-start.5 = (s32[32]{0:T(128)S(1)}, s32[32]{0:T(128)}, u32[]{:S(2)}) copy-start(s32[32]{0:T(128)} %copy-done.4) | copy-start | bytes 388
  192.9 10.3 %copy-start.11 = (f32[128,1152]{1,0:T(8,128)S(1)}, f32[128,1152]{1,0:T(8,128)}, u32[]{:S(2)}) copy-start(f32[128,1152]{1,0:T(8,128)} %get-tuple-element.74) | copy-start | bytes 1769476
  193.0 10.4 %copy-start.15 = (bf16[128,1152]{1,0:T(8,128)(2,1)S(1)}, bf16[128,1152]{1,0:T(8,128)(2,1)}, u32[]{:S(2)}) copy-start(bf16[128,1152]{1,0:T(8,128)(2,1)} %get-tuple-element.70) | copy-start | bytes 884740
  193.0 43.8 %all-to-all-start.7 = ((bf16[32,48,1024]{2,1,0:T(8,128)(2,1)}), bf16[32,48,1024]{2,1,0:T(8,128)(2,1)}, u32[]{:S(2)}, u32[]{:S(2)}) async-start(bf16[32,48,1024]{2,1,0:T(8,128)(2,1)} %bitcast.48), calls=%async_computation.7 | async-start | bytes 6291456 | tf_op jit(solution)/shard_map/all_to_all | solution.py:37
  217.2 23.6 %collective-permute-start.3 = (bf16[2,32,1152]{2,1,0:T(8,128)(2,1)}, bf16[2,32,1152]{2,1,0:T(8,128)(2,1)S(1)}, u32[]{:S(2)}, u32[]{:S(2)}) collective-permute-start(bf16[2,32,1152]{2,1,0:T(8,128)(2,1)} %get-tuple-element.86), channel_id=1, source_target_pairs={{0,32},{16,48},{32,0},{48,16},{1,33},{17,49},{33,1},{49,17},{2,34}... | collective-permute-start | bytes 442376 | tf_op jit(solution)/shard_map/ppermute | solution.py:276
  221.8 20.9 %collective-permute-start.4 = (bf16[2,32,1152]{2,1,0:T(8,128)(2,1)}, bf16[2,32,1152]{2,1,0:T(8,128)(2,1)S(1)}, u32[]{:S(2)}, u32[]{:S(2)}) collective-permute-start(bf16[2,32,1152]{2,1,0:T(8,128)(2,1)} %get-tuple-element.87), channel_id=1, source_target_pairs={{0,16},{16,32},{32,48},{48,0},{1,17},{17,33},{33,49},{49,1},{2,18}... | collective-permute-start | bytes 442376 | tf_op jit(solution)/shard_map/ppermute | solution.py:276
  223.9 18.7 %collective-permute-start.5 = (bf16[2,32,1152]{2,1,0:T(8,128)(2,1)}, bf16[2,32,1152]{2,1,0:T(8,128)(2,1)S(1)}, u32[]{:S(2)}, u32[]{:S(2)}) collective-permute-start(bf16[2,32,1152]{2,1,0:T(8,128)(2,1)} %get-tuple-element.88), channel_id=1, source_target_pairs={{0,48},{16,0},{32,16},{48,32},{1,49},{17,1},{33,17},{49,33},{2,50}... | collective-permute-start | bytes 442376 | tf_op jit(solution)/shard_map/ppermute | solution.py:276
  236.7 5.9 %copy-start.3 = (bf16[2,32,1152]{2,1,0:T(8,128)(2,1)S(1)}, bf16[2,32,1152]{2,1,0:T(8,128)(2,1)}, u32[]{:S(2)}) copy-start(bf16[2,32,1152]{2,1,0:T(8,128)(2,1)} %get-tuple-element.89.here) | copy-start | bytes 442372
  236.7 5.9 %copy-start.6 = (s32[32]{0:T(128)S(1)}, s32[32]{0:T(128)}, u32[]{:S(2)}) copy-start(s32[32]{0:T(128)} %copy-done.4) | copy-start | bytes 388
  236.7 5.9 %copy-start.8 = (f32[128,1152]{1,0:T(8,128)S(1)}, f32[128,1152]{1,0:T(8,128)}, u32[]{:S(2)}) copy-start(f32[128,1152]{1,0:T(8,128)} %copy-done.7) | copy-start | bytes 1769476
  236.7 5.9 %copy-start.10 = (f32[128,1152]{1,0:T(8,128)S(1)}, f32[128,1152]{1,0:T(8,128)}, u32[]{:S(2)}) copy-start(f32[128,1152]{1,0:T(8,128)} %copy-done.9) | copy-start | bytes 1769476
  236.7 6.6 %copy-start.21 = (s32[64]{0:T(128)S(1)}, s32[64]{0:T(128)}, u32[]{:S(2)}) copy-start(s32[64]{0:T(128)} %new_host.1) | copy-start | bytes 772
  243.4 0.8 copy-start.17
  243.4 1.0 copy-start.18
Sparse Core Ops, SparseCore 0:
  54.3 62.0 all-gather.5
  119.1 95.4 all-gather.7
